TPU v7x, 32 devices: a whole 2x2x4 slice. The times are simulated.
32 devices in a mesh: wide: 4 (over z), mid: 4 (over y, core), low: 2 (over x).
Axes of the slice: x: 2, y: 2, z: 4, core: 2. Of those that a mesh axis runs over, the one named last changes fastest.
Arguments:
- state: float32 [2, 4, 4, 2, 16384], P(None, 'wide', 'mid', 'low'), may hold values from -6 to 6
- gates: float32 [10, 2, 128, 128], replicated, may hold values from -0.375 to 0.375
- phase_low: float32 [128], replicated, may hold values from -3.140625 to 3.140625
- phase_mid: float32 [128], replicated, may hold values from -3.140625 to 3.140625
- phase_top: float32 [4, 4, 2, 1], P('wide', 'mid', 'low'), may hold values from -3.140625 to 3.140625
- swap_qubits: int32 [2], replicated, may hold values from 0 to 2, as said below
- regroup_order: int32 [4], replicated, may hold values from 0 to 3, each once
Outputs:
- final_state: float32 [2, 4, 4, 2, 16384], P(None, 'wide', 'mid', 'low')
Inputs may be any that keep to these rules, and one draw needn't show every extreme that they name: `swap_qubits`: the two entries differ, and one of them is 2. `regroup_order`: each of 0 to 3 once.
All inputs are finite; a program needn't handle non-finite values.
Results may differ from a plain program's by a relative error of at most 0.0003.
Values sent between devices are 32-bit elements; how exact they have to be, the bound alone decides.
No kernel may reach another device: no remote copies, remote signals or barrier semaphores. Data moves between devices by JAX's collectives and lax.ppermute only.
A program may use at most 64 MiB of HBM per device.

v0:
```python
from functools import partial

import jax
import jax.numpy as jnp
from jax import lax
from jax.sharding import PartitionSpec as P

HIGH = lax.Precision.HIGHEST


def partner(value, axis, stride):
    mask = 2**stride
    pairs = [(source, source ^ mask) for source in range(lax.axis_size(axis))]
    return lax.ppermute(value, axis, pairs)


def gate_inner(vector, real_gate, imag_gate):

    def product(values, matrix):
        return jnp.einsum("...b,ab->...a", values, matrix, precision=HIGH)

    real_part, imag_part = (vector[0], vector[1])
    return jnp.stack(
        [
            product(real_part, real_gate) - product(imag_part, imag_gate),
            product(real_part, imag_gate) + product(imag_part, real_gate),
        ]
    )


def gate_outer(vector, real_gate, imag_gate):

    def product(values, matrix):
        return jnp.einsum("ab,rbc->rac", matrix, values, precision=HIGH)

    real_part, imag_part = (vector[0], vector[1])
    return jnp.stack(
        [
            product(real_part, real_gate) - product(imag_part, imag_gate),
            product(real_part, imag_gate) + product(imag_part, real_gate),
        ]
    )


def apply_gate(vector, gates, number, gate_len):
    if number % 2 == 0:
        result = gate_inner(vector.reshape(2, -1, gate_len), gates[number, 0], gates[number, 1])
    else:
        result = gate_outer(
            vector.reshape(2, -1, gate_len, gate_len), gates[number, 0], gates[number, 1]
        )
    return result.reshape(2, -1)


def half_rows(vector, offset, base, own_bit, local_len):
    counter = jnp.arange(4, dtype=jnp.int32)
    lower = counter & jnp.left_shift(1, offset) - 1
    higher = jnp.right_shift(counter, offset)
    row_index = jnp.left_shift(higher, offset + 1) | jnp.left_shift(1 - own_bit, offset) | lower
    blocks = vector.reshape(2, local_len >> base + 3, 8, 1 << base)
    return (blocks, row_index, jnp.take(blocks, row_index, axis=2))


def move_bits(vector, lower, upper, local_len):
    if lower == upper:
        return vector
    shaped = vector.reshape(2, local_len >> upper + 1, 2, 1 << upper - lower - 1, 2, 1 << lower)
    return jnp.swapaxes(shaped, 2, 4).reshape(2, local_len)


def on_device(state, gates, phase_low, phase_mid, phase_top, swap_qubits, regroup_order):
    local_len = state.shape[-1]
    gate_len = gates.shape[-1]
    gate_count = gates.shape[0]
    local_bits = local_len.bit_length() - 1
    upper_len = local_len // (gate_len * gate_len)
    wide_count = lax.axis_size("wide")
    wide_bits = wide_count.bit_length() - 1
    vector = apply_gate(state.reshape(2, -1), gates, 0, gate_len)
    vector = vector.reshape(2, upper_len, gate_len, gate_len)
    angle = (
        phase_top.reshape(upper_len)[:, None, None]
        + phase_mid[None, :, None]
        + phase_low[None, None, :]
    )
    cosine = jnp.cos(angle)
    sine_part = jnp.sin(angle)
    vector = jnp.stack(
        [vector[0] * cosine - vector[1] * sine_part, vector[0] * sine_part + vector[1] * cosine]
    ).reshape(2, -1)
    for number in range(1, 4):
        vector = apply_gate(vector, gates, number, gate_len)
    mid_bit = lax.axis_index("mid") & 1
    blocks, row_index, sent_half = half_rows(
        vector, swap_qubits[0], local_bits - 3, mid_bit, local_len
    )
    received = partner(sent_half, "mid", 0)
    vector = blocks.at[:, :, row_index].set(received).reshape(2, local_len)
    row_ids = jnp.arange(16, dtype=jnp.int32)[:, None]
    row_bits = jnp.right_shift(row_ids, jnp.arange(4, dtype=jnp.int32)[None, :]) & 1
    order_index = jnp.sum(jnp.left_shift(row_bits, regroup_order[None, :]), axis=1)
    vector = jnp.take(vector.reshape(2, 16, local_len // 16), order_index, axis=1).reshape(
        2, local_len
    )
    low_base = local_bits - wide_bits - 3
    target = low_base + 2
    branches = [
        partial(move_bits, lower=low_base + place, upper=target, local_len=local_len)
        for place in range(3)
    ]
    vector = lax.switch(swap_qubits[1], branches, vector)
    shaped = vector.reshape(2, wide_count, 2, local_len // (2 * wide_count))
    moved = lax.all_to_all(
        lax.all_to_all(shaped, "wide", split_axis=1, concat_axis=1, tiled=True),
        "low",
        split_axis=2,
        concat_axis=2,
        tiled=True,
    )
    vector = lax.switch(swap_qubits[1], branches, moved.reshape(2, local_len))
    for number in range(4, gate_count):
        vector = apply_gate(vector, gates, number, gate_len)
    return vector.reshape(state.shape)


def solution(mesh):
    return jax.shard_map(
        on_device,
        mesh=mesh,
        in_specs=(
            P(None, "wide", "mid", "low", None),
            P(),
            P(),
            P(),
            P("wide", "mid", "low", None),
            P(),
            P(),
        ),
        out_specs=P(None, "wide", "mid", "low", None),
        check_vma=False,
    )
```

profile of v0, /device:TPU:0, one launch (start us, length us, event | category | flops | bytes accessed | tf_op | source)
XLA Modules:
  0.0 49.1 jit_solution(6737051799380090311)
XLA Ops:
  0.0 1.4 %fusion.126 = (s32[1]{0:T(128)}, s32[1]{0:T(128)}) fusion(s32[2]{0:T(128)} %param.18), kind=kLoop, calls=%fused_computation.168 | loop fusion | bytes 16 | tf_op jit(solution)/shard_map/slice | solution.py:95
  3.4 0.7 %fusion.116 = s32[4]{0:T(128)S(1)} fusion(s32[]{:T(128)S(6)} %sub.80, s32[]{:T(128)S(6)} %shift_left.37, s32[]{:T(128)S(6)} %add.140, s32[]{:T(128)} %bitcast.34), kind=kLoop, calls=%fused_computation.161 | loop fusion | flops 32 | bytes 32 | tf_op jit(solution)/shard_map/select_n | solution.py:98
  4.0 0.7 %compare_and_fusion = pred[4]{0:T(512)(128)(4,1)S(1)} fusion(s32[]{:T(128)S(6)} %sub.80, s32[]{:T(128)S(6)} %shift_left.37, s32[]{:T(128)S(6)} %add.140, s32[]{:T(128)} %bitcast.34), kind=kLoop, calls=%fused_computation.159 | loop fusion | flops 44 | bytes 20 | tf_op jit(solution)/shard_map/jit(_take)/and | solution.py:61
  4.7 0.9 %fusion.125 = (f32[1,1,1,1,16384]{4,3,2,1,0:T(1,128)S(1)}, f32[1,1,1,1,16384]{4,3,2,1,0:T(1,128)S(1)}) fusion(f32[2,1,1,1,16384]{4,3,2,1,0:T(1,128)} %param.13), kind=kLoop, calls=%fused_computation.167 | loop fusion | bytes 262144 | tf_op jit(solution)/shard_map/slice | solution.py:22
  5.6 1.1 %fusion.70 = f32[128,128]{1,0:T(8,128)S(1)} fusion(f32[128,128]{1,0:T(8,128)S(1)} %bitcast.247, f32[10,2,128,128]{3,2,1,0:T(8,128)} %param.14), kind=kOutput, calls=%fused_computation.106 | convolution fusion | flops 25165824 | bytes 196608 | tf_op jit(solution)/shard_map/...b,ab->...a/dot_general | solution.py:20
  6.7 1.1 %fusion.74 = f32[128,128]{1,0:T(8,128)S(1)} fusion(f32[128,128]{1,0:T(8,128)S(1)} %bitcast.248, f32[10,2,128,128]{3,2,1,0:T(8,128)} %param.14), kind=kOutput, calls=%fused_computation.110 | convolution fusion | flops 25165824 | bytes 196608 | tf_op jit(solution)/shard_map/...b,ab->...a/dot_general | solution.py:20
  8.4 1.1 %convolution_add_fusion.9 = f32[128,128]{1,0:T(8,128)S(1)} fusion(f32[128,128]{1,0:T(8,128)S(1)} %fusion.70, f32[128,128]{1,0:T(8,128)S(1)} %bitcast.249, f32[10,2,128,128]{3,2,1,0:T(8,128)} %param.14), kind=kOutput, calls=%fused_computation.39 | convolution fusion | flops 25182208 | bytes 262144 | tf_op jit(solution)/shard_map/...b,ab->...a/dot_general | solution.py:20
  9.6 1.1 %convolution_subtract_fusion.9 = f32[128,128]{1,0:T(8,128)S(1)} fusion(f32[128,128]{1,0:T(8,128)S(1)} %fusion.74, f32[128,128]{1,0:T(8,128)S(1)} %bitcast.250, f32[10,2,128,128]{3,2,1,0:T(8,128)} %param.14), kind=kOutput, calls=%fused_computation.40 | convolution fusion | flops 25182208 | bytes 262144 | tf_op jit(solution)/shard_map/...b,ab->...a/dot_general | solution.py:20
  10.7 0.7 %broadcast_add_fusion = f32[128]{0:T(128)S(1)} fusion(f32[128]{0:T(128)} %param.16, f32[]{:T(128)} %bitcast.240), kind=kLoop, calls=%fused_computation.163 | loop fusion | flops 128 | bytes 1028 | tf_op jit(solution)/shard_map/add | solution.py:82
  11.3 1.4 %fusion.64 = f32[128,128]{1,0:T(8,128)S(1)} fusion(f32[10,2,128,128]{3,2,1,0:T(8,128)} %param.14, f32[128,128]{1,0:T(8,128)S(1)} %convolution_add_fusion.9, f32[128,128]{1,0:T(8,128)S(1)} %convolution_subtract_fusion.9, f32[128]{0:T(128)} %param.15, f32[128]{0:T(128)S(1)} %broadcast_add_fusion), kind=kOutput, calls=%fused_computation.100 | convolution fusion | flops 25231360 | bytes 263168 | tf_op jit(solution)/shard_map/ab,rbc->rac/dot_general | solution.py:34
  12.8 0.6 %fusion.68 = f32[128,128]{1,0:T(8,128)S(1)} fusion(f32[10,2,128,128]{3,2,1,0:T(8,128)S(1)} %copy-done, f32[128,128]{1,0:T(8,128)S(1)} %convolution_add_fusion.9, f32[128,128]{1,0:T(8,128)S(1)} %convolution_subtract_fusion.9, f32[128]{0:T(128)S(1)} %copy-done.1, f32[128]{0:T(128)S(1)} %broadcast_add_fusion), kind=kOutput, calls=%fused_computation.104 | convolution fusion | flops 25231360 | bytes 263168 | tf_op jit(solution)/shard_map/ab,rbc->rac/dot_general | solution.py:34
  13.4 0.6 %fusion.9 = f32[128,128]{0,1:T(8,128)S(1)} fusion(f32[128,128]{1,0:T(8,128)S(1)} %fusion.68, f32[10,2,128,128]{3,2,1,0:T(8,128)S(1)} %copy-done, f32[128,128]{1,0:T(8,128)S(1)} %convolution_subtract_fusion.9, f32[128,128]{1,0:T(8,128)S(1)} %convolution_add_fusion.9, f32[128]{0:T(128)S(1)} %copy-done.1, f32[128]{0:T(128)S(1)} %broadcast_add_fusion), kind=kOutput, calls=%fused_computation.38 | convolution fusion | flops 25247744 | bytes 328704 | tf_op jit(solution)/shard_map/ab,rbc->rac/dot_general | solution.py:34
  14.0 0.3 fusion.58
  14.2 0.3 fusion.62
  14.6 0.6 %fusion.8 = f32[128,128]{0,1:T(8,128)S(1)} fusion(f32[128,128]{1,0:T(8,128)S(1)} %fusion.64, f32[10,2,128,128]{3,2,1,0:T(8,128)S(1)} %copy-done, f32[128,128]{1,0:T(8,128)S(1)} %convolution_subtract_fusion.9, f32[128,128]{1,0:T(8,128)S(1)} %convolution_add_fusion.9, f32[128]{0:T(128)S(1)} %copy-done.1, f32[128]{0:T(128)S(1)} %broadcast_add_fusion), kind=kOutput, calls=%fused_computation.36 | convolution fusion | flops 25247744 | bytes 328704 | tf_op jit(solution)/shard_map/ab,rbc->rac/dot_general | solution.py:34
  15.1 0.3 convolution_subtract_fusion.7
  15.4 0.3 fusion.52
  15.7 0.3 fusion.56
  16.0 0.3 convolution_add_fusion.7
  16.3 0.3 fusion.7
  16.6 0.3 fusion.6
  17.0 0.1 copy.70
  17.1 0.1 maximum_bitcast_fusion
  17.2 0.6 %gather_fusion = f32[4,2,2048]{2,1,0:T(2,128)S(1)} fusion(f32[2,8,2048]{2,0,1:T(2,128)S(1)} %maximum_bitcast_fusion, s32[1024]{0:T(1024)S(1)} %pad_clamp_fusion.1), kind=kCustom, calls=%fused_computation | custom fusion | bytes 131088 | tf_op jit(solution)/shard_map/jit(_take)/gather | solution.py:61
  17.9 0.1 bitcast_select_fusion
  18.0 0.5 %collective-permute-start = (f32[2,1,4,2048]{3,0,2,1:T(2,128)S(1)}, f32[2,1,4,2048]{3,0,2,1:T(2,128)S(1)}, u32[]{:S(2)}, u32[]{:S(2)}) collective-permute-start(f32[2,1,4,2048]{3,0,2,1:T(2,128)S(1)} %bitcast_select_fusion), channel_id=1, source_target_pairs={{0,2},{2,0},{4,6},{6,4},{1,3},{3,1},{5,7},{7,5},{8,10},{10,8},{12,... | collective-permute-start | bytes 196616 | tf_op jit(solution)/shard_map/ppermute | solution.py:14
  19.2 0.2 collective-permute-done
  19.4 0.6 %scatter_fusion = f32[2,8,2048]{2,0,1:T(2,128)S(1)} fusion(f32[2,8,2048]{2,0,1:T(2,128)S(1)} %maximum_bitcast_fusion, s32[4]{0:T(128)S(1)} %fusion.116, f32[4,2,2048]{2,1,0:T(2,128)S(1)} %bitcast.259), kind=kCustom, calls=%fused_computation.2 | custom fusion | bytes 196624 | tf_op jit(solution)/shard_map/scatter | solution.py:98
  20.0 0.7 %gather_fusion.1 = f32[16,2,1024]{2,1,0:T(2,128)S(1)} fusion(f32[2,16,1024]{2,0,1:T(2,128)S(1)} %bitcast.246, s32[1024]{0:T(1024)S(1)} %pad_clamp_fusion), kind=kCustom, calls=%fused_computation.1 | custom fusion | bytes 262208 | tf_op jit(solution)/shard_map/jit(_take)/gather | solution.py:102
  20.7 0.5 conditional.2
  20.8 0.1 reshape_reshape.5
  21.0 0.2 reshape.257
  21.2 0.2 reshape.260
  21.4 12.2 %all_to_all.19 = f32[2,4,2,2048]{3,2,0,1:T(2,128)S(1)} all-to-all(f32[2,4,2,2048]{3,2,0,1:T(2,128)S(1)} %copy.79), channel_id=1, replica_groups=mesh['wide'=4,'mid'=4,'low'=2] {'wide'}, dimensions={1} | all-to-all | bytes 262144 | tf_op jit(solution)/shard_map/all_to_all | solution.py:114
  33.7 7.0 %all_to_all.20 = f32[2,4,2,2048]{3,1,0,2:T(4,128)S(1)} all-to-all(f32[2,4,2,2048]{3,1,0,2:T(4,128)S(1)} %copy.80), channel_id=1, replica_groups=mesh['wide'=4,'mid'=4,'low'=2] {'low'}, dimensions={2} | all-to-all | bytes 262144 | tf_op jit(solution)/shard_map/all_to_all | solution.py:113
  40.7 0.4 conditional.3
  40.7 0.1 reshape.290
  40.9 0.1 copy.101
  41.1 0.3 fusion.46
  41.4 0.3 fusion.50
  41.7 0.3 convolution_subtract_fusion.5
  41.9 0.3 fusion.40
  42.2 0.3 fusion.44
  42.5 0.3 convolution_add_fusion.5
  42.8 0.3 fusion.5
  43.1 0.3 fusion.34
  43.4 0.3 fusion.38
  43.7 0.3 fusion.4
  44.0 0.3 convolution_subtract_fusion.3
  44.3 0.3 fusion.28
  44.6 0.3 fusion.32
  44.9 0.3 convolution_add_fusion.3
  45.1 0.3 fusion.3
  45.4 0.3 fusion.22
  45.7 0.3 fusion.26
  46.0 0.3 fusion.2
  46.3 0.3 convolution_subtract_fusion.1
  46.6 0.3 fusion.16
  46.9 0.3 fusion.20
  47.2 0.3 convolution_add_fusion.1
  47.5 0.3 fusion.1
  47.8 0.3 fusion
  48.2 0.1 copy.84
  48.3 0.8 %pad_maximum_fusion = f32[2,1,1,1,16384]{4,3,2,1,0:T(1,128)} fusion(f32[1,1,1,1,16384]{4,3,2,1,0:T(1,128)S(1)} %bitcast.256, f32[1,1,1,1,16384]{4,3,2,1,0:T(1,128)S(1)} %bitcast.258), kind=kLoop, calls=%fused_computation.42 | loop fusion | flops 32768 | bytes 262144 | tf_op jit(solution)/shard_map/stack | solution.py:37
  (20 shorter events, 0.7 us)
Async XLA Ops:
  0.0 12.8 %copy-start = (f32[10,2,128,128]{3,2,1,0:T(8,128)S(1)}, f32[10,2,128,128]{3,2,1,0:T(8,128)}, u32[]{:S(2)}) copy-start(f32[10,2,128,128]{3,2,1,0:T(8,128)} %param.14) | copy-start | bytes 3932164
  0.0 12.8 %copy-start.1 = (f32[128]{0:T(128)S(1)}, f32[128]{0:T(128)}, u32[]{:S(2)}) copy-start(f32[128]{0:T(128)} %param.15) | copy-start | bytes 1540
  14.5 3.9 %copy-start.2 = (s32[4]{0:T(128)S(1)}, s32[4]{0:T(128)}, u32[]{:S(2)}) copy-start(s32[4]{0:T(128)} %param.19) | copy-start | bytes 52
  18.0 1.4 %collective-permute-start = (f32[2,1,4,2048]{3,0,2,1:T(2,128)S(1)}, f32[2,1,4,2048]{3,0,2,1:T(2,128)S(1)}, u32[]{:S(2)}, u32[]{:S(2)}) collective-permute-start(f32[2,1,4,2048]{3,0,2,1:T(2,128)S(1)} %bitcast_select_fusion), channel_id=1, source_target_pairs={{0,2},{2,0},{4,6},{6,4},{1,3},{3,1},{5,7},{7,5},{8,10},{10,8},{12,... | collective-permute-start | bytes 196616 | tf_op jit(solution)/shard_map/ppermute | solution.py:14
where the time goes:
time: 49.6 us; the launch traced here: 49.1 us
  blocking collectives  19.3 us (39%)
  matrix products  16.7 us (34%)
  local copies, waits for them, and re-layouts  5.55 us (11%)
  between operations  3.65 us (7%)
  other arithmetic  3.17 us (6%)
  starting transfers between devices  0.52 us (1%)
    all_to_all x1, blocking collectives, on_device(): lax.all_to_all(shaped, 'wide', split_axis=1, concat_axis=1, tiled=True)  12.2 us
    dot_general x20, matrix products, product(): return jnp.einsum('...b,ab->...a', values, matrix, precision=HIGH)  8.93 us
    dot_general x20, matrix products, product(): return jnp.einsum('ab,rbc->rac', matrix, values, precision=HIGH)  7.73 us
    all_to_all x1, blocking collectives, on_device(): lax.all_to_all(lax.all_to_all(shaped, 'wide', split_axis=1, concat_axis=1...  7.03 us
    slice x1, local copies, waits for them, and re-layouts, on_device(): swap_qubits[0]  1.41 us
  transfers between devices with their start and end apart: 1, of which 1 were waited for; matrix products, arithmetic and copies ran while one was open for 0% of the time, Pallas kernels for 0%

commit v1 on v0

--- a/solution.py
+++ b/solution.py
@@ -3,9 +3,313 @@
 import jax
 import jax.numpy as jnp
 from jax import lax
+from jax.experimental import pallas as pl
+from jax.experimental.pallas import tpu as pltpu
 from jax.sharding import PartitionSpec as P
 
 HIGH = lax.Precision.HIGHEST
+AXES = ("wide", "mid", "low")
+VSPEC = pl.BlockSpec(memory_space=pltpu.VMEM)
+SSPEC = pl.BlockSpec(memory_space=pltpu.SMEM)
+
+
+def split(value):
+    high = value.astype(jnp.bfloat16)
+    return high, (value - high.astype(jnp.float32)).astype(jnp.bfloat16)
+
+
+def embed(value):
+    half = value.shape[1] // 2
+    return jnp.concatenate([value, jnp.concatenate([-value[:, half:], value[:, :half]], 1)], 0)
+
+
+def dot(left, right, transposed=False):
+    dims = (((1,), (1 if transposed else 0,)), ((), ()))
+    return lax.dot_general(left, right, dims, preferred_element_type=jnp.float32)
+
+
+def product(left, right, transposed=False):
+    rows = left[0].shape[0]
+    both = dot(jnp.concatenate(left, 0), right[0], transposed)
+    return both[:rows] + both[rows:] + dot(left[0], right[1], transposed)
+
+
+def complex_product(left, right):
+    return product(left, tuple(embed(part) for part in right))
+
+
+def turn(value, angle):
+    half = value.shape[1] // 2
+    cosine, sine = jnp.cos(angle), jnp.sin(angle)
+    real, imag = value[:, :half], value[:, half:]
+    return jnp.concatenate([real * cosine - imag * sine, real * sine + imag * cosine], 1)
+
+
+def side(ref):
+    return jnp.concatenate([ref[0], ref[1]], 1)
+
+
+class Plan:
+    def __init__(self, rows, wide_count):
+        self.rows = rows
+        self.row_bits = rows.bit_length() - 1
+        self.wide_bits = wide_count.bit_length() - 1
+        self.low_base = self.row_bits - self.wide_bits - 3
+        self.chunk = rows // (2 * wide_count)
+        self.offsets = [wide_count - 1] + list(range(1, wide_count - 1))
+        self.slots = len(self.offsets)
+
+    def first(self, slot):
+        return slot % 2
+
+
+def pick(index, table):
+    value = jnp.zeros_like(index)
+    for place, entry in enumerate(table):
+        value = jnp.where(index == place, entry, value)
+    return value
+
+
+def free_row(plan, inner, swap):
+    base = plan.low_base
+    lower = base + jnp.where(swap == 0, 1, 0)
+    upper = base + jnp.where(swap == 2, 1, 2)
+    return (
+        (inner & ((1 << base) - 1))
+        | jnp.left_shift(jnp.right_shift(inner, base) & 1, lower)
+        | jnp.left_shift(jnp.right_shift(inner, base + 1) & 1, upper)
+    )
+
+
+def sent_rows(plan, index, swaps, order):
+    wide, core, low = lax.axis_index("wide"), lax.axis_index("mid") & 1, lax.axis_index("low")
+    block, inner = index // plan.chunk, index % plan.chunk
+    wide_offsets, low_offsets, cores = [0], [0], [core]
+    for slot, offset in enumerate(plan.offsets):
+        wide_offsets += [offset, offset]
+        low_offsets += [core ^ plan.first(slot)] * 2
+        cores += [core, 1 - core]
+    wide_offsets.append(0)
+    low_offsets.append(1)
+    cores.append(core)
+    to_wide = wide ^ pick(block, wide_offsets)
+    to_low = (low & 1) ^ pick(block, low_offsets)
+    to_core = pick(block, cores)
+    row = free_row(plan, inner, swaps[1])
+    row |= jnp.left_shift(to_low, plan.low_base + swaps[1])
+    row |= jnp.left_shift(to_wide, plan.row_bits - plan.wide_bits)
+    base = plan.row_bits - 4
+    old = row & ((1 << base) - 1)
+    for place in range(4):
+        old |= jnp.left_shift(jnp.right_shift(row, base + place) & 1, base + order[place])
+    position = plan.row_bits - 3 + swaps[0]
+    from_core = jnp.right_shift(old, position) & 1
+    old = (old & ~jnp.left_shift(1, position)) | jnp.left_shift(to_core, position)
+    return old, from_core
+
+
+def received_rows(plan, index, swaps):
+    wide, core, low = lax.axis_index("wide"), lax.axis_index("mid") & 1, lax.axis_index("low")
+    block, inner = index // plan.chunk, index % plan.chunk
+    wide_offsets = [0] + plan.offsets + [0] + plan.offsets
+    low_offsets = [0] + [core ^ plan.first(slot) for slot in range(plan.slots)] + [1]
+    low_offsets += [1 - (core ^ plan.first(slot)) for slot in range(plan.slots)]
+    from_wide = wide ^ pick(block, wide_offsets)
+    from_low = (low & 1) ^ pick(block, low_offsets)
+    row = free_row(plan, inner, swaps[1])
+    row |= jnp.left_shift(from_low, plan.low_base + swaps[1])
+    return row | jnp.left_shift(from_wide, plan.row_bits - plan.wide_bits)
+
+
+def fetch(pairs, sems):
+    copies = [pltpu.make_async_copy(a, b, sems.at[place]) for place, (a, b) in enumerate(pairs)]
+    for copy in copies:
+        copy.start()
+    return copies
+
+
+def front_kernel(plan, gates, phase_mid, phase_top, state, swaps, order, own, high, low, *scratch):
+    *buffers, sems = scratch
+    sources = (swaps, order, gates.at[3], gates.at[1], phase_mid, state, phase_top)
+    copies = fetch(list(zip(sources, buffers)), sems)
+    swaps, order, gate_three, gate_one, phase_mid, state, phase_top = buffers
+    copies[0].wait()
+    copies[1].wait()
+    rows = plan.rows
+    index = lax.broadcasted_iota(jnp.int32, (rows, rows), 0)
+    source, from_core = sent_rows(plan, index, swaps, order)
+    chosen = (lax.broadcasted_iota(jnp.int32, (rows, rows), 1) == source).astype(jnp.bfloat16)
+    copies[2].wait()
+    outer = split(side(gate_three))
+    outer = tuple(dot(chosen, part).astype(jnp.bfloat16) for part in outer)
+    copies[3].wait()
+    copies[4].wait()
+    inner = turn(side(gate_one), phase_mid[...])
+    merged = complex_product(outer, split(inner))
+    mine = jnp.concatenate([from_core == (lax.axis_index("mid") & 1)] * 2, 1)
+    zeros = jnp.zeros_like(merged)
+    copies[5].wait()
+    copies[6].wait()
+    value = split(side(state))
+    own[...] = turn(complex_product(split(jnp.where(mine, merged, zeros)), value), phase_top[...])
+    high[...], low[...] = split(jnp.where(mine, zeros, merged))
+
+
+def send_kernel(plan, own, high, low, state, phase_top, *sent):
+    value = split(side(state))
+    total = own[...] + turn(complex_product((high[...], low[...]), value), phase_top[...])
+    start = 0
+    for ref in sent:
+        ref[...] = total[start : start + ref.shape[0]]
+        start += ref.shape[0]
+
+
+def back_kernel(plan, count, gates, phase_low, swaps, kept, right_high, right_low, left_high, left_low):
+    del kept
+    rows = plan.rows
+
+    def gate(number):
+        return split(side(gates.at[number]))
+
+    def chain(numbers, value):
+        for number in numbers:
+            value = complex_product(gate(number), split(value))
+        return value
+
+    right = turn(side(gates.at[2]), phase_low[...])
+    right = complex_product(split(right), gate(0))
+    right = chain(range(4, count, 2), right)
+    half = rows
+    real, imag = right[:, :half], right[:, half:]
+    right = jnp.concatenate(
+        [jnp.concatenate([real, -imag], 1), jnp.concatenate([imag, real], 1)], 0
+    )
+    right_high[...], right_low[...] = split(right)
+    index = lax.broadcasted_iota(jnp.int32, (rows, rows), 1)
+    target = received_rows(plan, index, swaps)
+    placed = (lax.broadcasted_iota(jnp.int32, (rows, rows), 0) == target).astype(jnp.bfloat16)
+    first = tuple(
+        jnp.concatenate([dot(part[:, :half], placed), dot(part[:, half:], placed)], 1)
+        for part in gate(5)
+    )
+    left = complex_product(gate(7), tuple(part.astype(jnp.bfloat16) for part in first))
+    left = chain(range(9, count, 2), left)
+    left_high[...], left_low[...] = split(left)
+
+
+def sort_kernel(plan, *refs):
+    chunk = plan.chunk
+    received, give = refs[: plan.slots], refs[-1]
+    for slot, ref in enumerate(received):
+        give[slot * chunk : (slot + 1) * chunk] = ref[chunk:]
+
+
+def kept_kernel(plan, *refs):
+    *parts, right_high, right_low, high, low = refs
+    value = jnp.concatenate([ref[: plan.chunk] for ref in parts], 0)
+    value = product(split(value), (right_high[...], right_low[...]), True)
+    high[...], low[...] = split(value)
+
+
+def last_kernel(plan, high, low, given, right_high, right_low, left_high, left_low, out):
+    value = split(product(split(given[...]), (right_high[...], right_low[...]), True))
+    value = tuple(jnp.concatenate([a[...], b], 0) for a, b in zip((high, low), value))
+    result = complex_product((left_high[...], left_low[...]), value)
+    half = plan.rows
+    out[0] = result[:, :half]
+    out[1] = result[:, half:]
+
+
+def call(kernel, shapes, args, specs, flops=0, scratch=()):
+    args = [
+        pltpu.with_memory_space_constraint(arg, pltpu.VMEM) if spec is VSPEC else arg
+        for arg, spec in zip(args, specs)
+    ]
+    return pl.pallas_call(
+        kernel,
+        out_shape=[pltpu.VMEM(shape, dtype) for shape, dtype in shapes],
+        in_specs=[pl.BlockSpec() if spec is None else spec for spec in specs],
+        out_specs=[VSPEC] * len(shapes),
+        scratch_shapes=scratch,
+        cost_estimate=pl.CostEstimate(flops=flops, bytes_accessed=1 << 17, transcendentals=0),
+    )(*args)
+
+
+def exchange(value, offset, cores=(0, 0), flip=0):
+    wides, mids, lows = (lax.axis_size(axis) for axis in AXES)
+    pairs = []
+    for wide in range(wides):
+        for mid in range(mids):
+            for low in range(lows):
+                source = (wide * mids + mid) * lows + low
+                to = ((wide ^ offset) * mids + (mid ^ flip)) * lows + (low ^ cores[mid & 1])
+                pairs.append((source, to))
+    return lax.ppermute(value, AXES, pairs)
+
+
+def merged_device(state, gates, phase_low, phase_mid, phase_top, swap_qubits, regroup_order):
+    rows = gates.shape[-1]
+    plan = Plan(rows, lax.axis_size("wide"))
+    chunk = plan.chunk
+    f32, bf16 = jnp.float32, jnp.bfloat16
+    square = state.reshape(2, rows, rows)
+    top = phase_top.reshape(1, 1)
+    other = exchange(square, 0, flip=1)
+    other_top = exchange(top, 0, flip=1)
+
+    pair = pltpu.VMEM((2, rows, rows), f32)
+    sources = (gates, phase_mid.reshape(1, rows), top, square, swap_qubits, regroup_order)
+    buffers = [pltpu.SMEM(arg.shape, arg.dtype) for arg in sources[4:]]
+    buffers += [pair, pair, pltpu.VMEM((1, rows), f32), pair, pltpu.VMEM((1, 1), f32)]
+    own, high, low = call(
+        partial(front_kernel, plan),
+        [((rows, 2 * rows), f32), ((rows, 2 * rows), bf16), ((rows, 2 * rows), bf16)],
+        sources,
+        (pl.BlockSpec(memory_space=pl.ANY),) * len(sources),
+        scratch=buffers + [pltpu.SemaphoreType.DMA((len(buffers),))],
+    )
+    shapes = [(chunk, 2 * rows)] + [(2 * chunk, 2 * rows)] * plan.slots + [(chunk, 2 * rows)]
+    local, *sent = call(
+        partial(send_kernel, plan),
+        [(shape, f32) for shape in shapes],
+        (own, high, low, other, other_top),
+        (VSPEC,) * 5,
+    )
+    received = [
+        exchange(value, offset, (plan.first(slot), 1 - plan.first(slot)))
+        for slot, (value, offset) in enumerate(zip(sent, plan.offsets))
+    ]
+    received.append(exchange(sent[-1], 0, (1, 1)))
+    wide_square = ((2 * rows, 2 * rows), bf16)
+    tall = ((rows, 2 * rows), bf16)
+    right_high, right_low, left_high, left_low = call(
+        partial(back_kernel, plan, gates.shape[0]),
+        [wide_square, wide_square, tall, tall],
+        (gates, phase_low.reshape(1, rows), swap_qubits, local),
+        (None, None, SSPEC, VSPEC),
+        flops=6 * 24 * rows**3,
+    )
+    (give,) = call(
+        partial(sort_kernel, plan),
+        [((plan.slots * chunk, 2 * rows), f32)],
+        received[:-1],
+        (VSPEC,) * plan.slots,
+    )
+    given = exchange(give, 0, flip=1)
+    kept_rows = (plan.slots + 2) * chunk
+    high, low = call(
+        partial(kept_kernel, plan),
+        [((kept_rows, 2 * rows), bf16)] * 2,
+        (local, *received, right_high, right_low),
+        (VSPEC,) * (plan.slots + 4),
+    )
+    args = (high, low, given, right_high, right_low, left_high, left_low)
+    out = pl.pallas_call(
+        partial(last_kernel, plan),
+        out_shape=jax.ShapeDtypeStruct((2, rows, rows), f32),
+        in_specs=[VSPEC] * len(args),
+    )(*[pltpu.with_memory_space_constraint(arg, pltpu.VMEM) for arg in args])
+    return out.reshape(state.shape)
 
 
 def partner(value, axis, stride):
@@ -68,7 +372,7 @@
     return jnp.swapaxes(shaped, 2, 4).reshape(2, local_len)
 
 
-def on_device(state, gates, phase_low, phase_mid, phase_top, swap_qubits, regroup_order):
+def general_device(state, gates, phase_low, phase_mid, phase_top, swap_qubits, regroup_order):
     local_len = state.shape[-1]
     gate_len = gates.shape[-1]
     gate_count = gates.shape[0]
@@ -121,6 +425,13 @@
     for number in range(4, gate_count):
         vector = apply_gate(vector, gates, number, gate_len)
     return vector.reshape(state.shape)
+
+
+def on_device(state, gates, *rest):
+    rows = gates.shape[-1]
+    plan_base = rows.bit_length() - 1 - (lax.axis_size("wide").bit_length() - 1) - 3
+    merged = state.shape[-1] == rows * rows and plan_base >= 1 and gates.shape[0] >= 8
+    return (merged_device if merged else general_device)(state, gates, *rest)
 
 
 def solution(mesh):

time: 49.6 us -> 19.8 us (0.40)
  blocking collectives: 19.3 us -> 0 us
  matrix products: 16.7 us -> 0 us
  starting transfers between devices: 0.52 us -> 8.5 us
  Pallas kernels: 0 us -> 6.78 us
  local copies, waits for them, and re-layouts: 5.55 us -> 0 us
  waiting for transfers between devices: 0.15 us -> 3.59 us
  other arithmetic: 3.17 us -> 0 us
  between operations: 3.65 us -> 0.72 us
    all_to_all x2 -> x0, blocking collectives: 19.3 us -> none  [the longest x1 12.2 us: on_device(): lax.all_to_all(shaped, 'wide', split_axis=1, concat_axis=1, tiled=True)]
    dot_general x40 -> x0, matrix products: 16.7 us -> none  [the longest x20 8.93 us: product(): return jnp.einsum('...b,ab->...a', values, matrix, precision=HIGH)]
    ppermute x1 -> x7, starting transfers between devices: 0.52 us -> 8.5 us  [exchange(): return lax.ppermute(value, AXES, pairs)]
    pallas_call x0 -> x6, Pallas kernels: none -> 6.78 us  [the longest x5 5.63 us: call(): pl.pallas_call(kernel, out_shape=[pltpu.VMEM(shape, dtype) for shape, dty...]
    ppermute x1 -> x7, waiting for transfers between devices: 0.15 us -> 3.59 us  [exchange(): return lax.ppermute(value, AXES, pairs)]
    slice x3 -> x0, local copies, waits for them, and re-layouts: 2.3 us -> none  [the longest x1 1.41 us: on_device(): swap_qubits[0]]
    gather x2 -> x0, local copies, waits for them, and re-layouts: 1.31 us -> none  [the longest x1 0.69 us: on_device(): jnp.take(vector.reshape(2, 16, local_len // 16), order_index, axis=1)]
    another operation x2 -> x0, other arithmetic: 0.91 us -> none  [gate_outer(): jnp.stack([product(real_part, real_gate) - product(imag_part, imag_gate),...]
  transfers between devices with their start and end apart: 1 -> 7, of which waited for: 1 -> 3; matrix products, arithmetic and copies ran while one was open for 0% -> 0% of each run, Pallas kernels for 0% -> 24%
where the time goes in v1:
time: 19.8 us; the launch traced here: 19.6 us
  starting transfers between devices  8.5 us (43%)
  Pallas kernels  6.78 us (34%)
  waiting for transfers between devices  3.59 us (18%)
  between operations  0.72 us (4%)
    ppermute x7, starting transfers between devices, exchange(): return lax.ppermute(value, AXES, pairs)  8.5 us
    pallas_call x5, Pallas kernels, call(): pl.pallas_call(kernel, out_shape=[pltpu.VMEM(shape, dtype) for shape, dty...  5.63 us
    ppermute x7, waiting for transfers between devices, exchange(): return lax.ppermute(value, AXES, pairs)  3.59 us
    pallas_call x1, Pallas kernels, merged_device(): pl.pallas_call(partial(last_kernel, plan), out_shape=jax.ShapeDtypeStruct...  1.15 us
  transfers between devices with their start and end apart: 7, of which 3 were waited for; matrix products, arithmetic and copies ran while one was open for 0% of the time, Pallas kernels for 24%

profile of v1, /device:TPU:0, one launch (start us, length us, event | category | flops | bytes accessed | tf_op | source)
XLA Modules:
  0.0 19.6 jit_solution(12684187741454841209)
XLA Ops:
  0.0 0.5 %collective-permute-start = (f32[2,128,128]{2,1,0:T(8,128)}, f32[2,128,128]{2,1,0:T(8,128)S(1)}, u32[]{:S(2)}, u32[]{:S(2)}) collective-permute-start(f32[2,128,128]{2,1,0:T(8,128)} %bitcast.6), channel_id=1, source_target_pairs={{0,2},{1,3},{2,0},{3,1},{4,6},{5,7},{6,4},{7,5},{8,10},{9,11},{10,... | collective-permute-start | bytes 393224 | tf_op jit(solution)/shard_map/ppermute | solution.py:247
  0.5 0.1 collective-permute-start.1
  1.2 1.7 %shard_map.73 = (f32[128,256]{1,0:T(8,128)S(1)}, bf16[128,256]{1,0:T(8,128)(2,1)S(1)}, bf16[128,256]{1,0:T(8,128)(2,1)S(1)}) custom-call(f32[10,2,128,128]{3,2,1,0:T(8,128)} %gates.3, f32[1,128]{1,0:T(1,128)} %bitcast.8, f32[1,1]{1,0:T(1,128)} %bitcast.5.phase_top, f32[2,128,128]{2,1,0:T(8,128)} %bitcast.7, s32[2]{0:T(128)} %swaps.3, s32[4]{0:T(128)} %order.1), custom_call_target="tpu_custom_call" | custom-call | bytes 131072 | tf_op jit(solution)/shard_map/pallas_call | solution.py:228
  2.9 0.0 collective-permute-done.1.phase_top
  2.9 0.0 collective-permute-done.state
  2.9 0.9 %shard_map.74 = (f32[16,256]{1,0:T(8,128)S(1)}, f32[32,256]{1,0:T(8,128)S(1)}, f32[32,256]{1,0:T(8,128)S(1)}, f32[32,256]{1,0:T(8,128)S(1)}, f32[16,256]{1,0:T(8,128)S(1)}) custom-call(f32[128,256]{1,0:T(8,128)S(1)} %get-tuple-element.19.own, bf16[128,256]{1,0:T(8,128)(2,1)S(1)} %get-tuple-element.20.high, bf16[128,256]{1,0:T(8,128)(2,1)S(1)} %get-tuple-element.21.low, ...), custom_call_target="tpu_custom_call" | custom-call | bytes 131072 | tf_op jit(solution)/shard_map/pallas_call | solution.py:228
  3.8 5.1 %collective-permute-start.2 = (f32[32,256]{1,0:T(8,128)S(1)}, f32[32,256]{1,0:T(8,128)S(1)}, u32[]{:S(2)}, u32[]{:S(2)}) collective-permute-start(f32[32,256]{1,0:T(8,128)S(1)} %get-tuple-element.23), channel_id=1, source_target_pairs={{0,24},{1,25},{2,27},{3,26},{4,28},{5,29},{6,31},{7,30},{8,16},{9,... | collective-permute-start | bytes 98312 | tf_op jit(solution)/shard_map/ppermute | solution.py:247
  8.9 0.5 %collective-permute-start.3 = (f32[32,256]{1,0:T(8,128)S(1)}, f32[32,256]{1,0:T(8,128)S(1)}, u32[]{:S(2)}, u32[]{:S(2)}) collective-permute-start(f32[32,256]{1,0:T(8,128)S(1)} %get-tuple-element.24), channel_id=1, source_target_pairs={{0,9},{1,8},{2,10},{3,11},{4,13},{5,12},{6,14},{7,15},{8,1},{9,0},... | collective-permute-start | bytes 98312 | tf_op jit(solution)/shard_map/ppermute | solution.py:247
  9.4 1.2 %collective-permute-start.4 = (f32[32,256]{1,0:T(8,128)S(1)}, f32[32,256]{1,0:T(8,128)S(1)}, u32[]{:S(2)}, u32[]{:S(2)}) collective-permute-start(f32[32,256]{1,0:T(8,128)S(1)} %get-tuple-element.25), channel_id=1, source_target_pairs={{0,16},{1,17},{2,19},{3,18},{4,20},{5,21},{6,23},{7,22},{8,24},{9,... | collective-permute-start | bytes 98312 | tf_op jit(solution)/shard_map/ppermute | solution.py:247
  10.6 0.4 %collective-permute-done.2.refs_1_.refs_0_ = f32[32,256]{1,0:T(8,128)S(1)} collective-permute-done((f32[32,256]{1,0:T(8,128)S(1)}, f32[32,256]{1,0:T(8,128)S(1)}, u32[]{:S(2)}, u32[]{:S(2)}) %collective-permute-start.2) | collective-permute-done | bytes 32800 | tf_op jit(solution)/shard_map/ppermute | solution.py:247
  11.1 2.7 %collective-permute-done.3.refs_2_.refs_1_ = f32[32,256]{1,0:T(8,128)S(1)} collective-permute-done((f32[32,256]{1,0:T(8,128)S(1)}, f32[32,256]{1,0:T(8,128)S(1)}, u32[]{:S(2)}, u32[]{:S(2)}) %collective-permute-start.3) | collective-permute-done | bytes 32800 | tf_op jit(solution)/shard_map/ppermute | solution.py:247
  13.7 0.5 %collective-permute-done.4.refs_3_.refs_2_ = f32[32,256]{1,0:T(8,128)S(1)} collective-permute-done((f32[32,256]{1,0:T(8,128)S(1)}, f32[32,256]{1,0:T(8,128)S(1)}, u32[]{:S(2)}, u32[]{:S(2)}) %collective-permute-start.4) | collective-permute-done | bytes 32800 | tf_op jit(solution)/shard_map/ppermute | solution.py:247
  14.2 0.0 collective-permute-start.6
  14.2 1.2 %collective-permute-start.5 = (f32[16,256]{1,0:T(8,128)S(1)}, f32[16,256]{1,0:T(8,128)S(1)}, u32[]{:S(2)}, u32[]{:S(2)}) collective-permute-start(f32[16,256]{1,0:T(8,128)S(1)} %get-tuple-element.26), channel_id=1, source_target_pairs={{0,1},{1,0},{2,3},{3,2},{4,5},{5,4},{6,7},{7,6},{8,9},{9,8},{10,11... | collective-permute-start | bytes 49160 | tf_op jit(solution)/shard_map/ppermute | solution.py:247
  15.4 2.8 %shard_map.75 = (bf16[256,256]{1,0:T(8,128)(2,1)S(1)}, bf16[256,256]{1,0:T(8,128)(2,1)S(1)}, bf16[128,256]{1,0:T(8,128)(2,1)S(1)}, bf16[128,256]{1,0:T(8,128)(2,1)S(1)}) custom-call(f32[10,2,128,128]{3,2,1,0:T(8,128)} %gates.3, f32[1,128]{1,0:T(1,128)} %bitcast.9, s32[2]{0:T(128)} %swaps.3, f32[16,256]{1,0:T(8,128)S(1)} %get-tuple-element.22.kept.refs_0_), custom_call_target="tpu_custom_call" | custom-call | flops 301989888 | bytes 131072 | tf_op jit(solution)/shard_map/pallas_call | solution.py:228
  18.2 0.0 collective-permute-done.5.refs_4_
  18.2 0.2 %shard_map.76 = (bf16[80,256]{1,0:T(8,128)(2,1)S(1)}, bf16[80,256]{1,0:T(8,128)(2,1)S(1)}) custom-call(f32[16,256]{1,0:T(8,128)S(1)} %get-tuple-element.22.kept.refs_0_, f32[32,256]{1,0:T(8,128)S(1)} %collective-permute-done.2.refs_1_.refs_0_, f32[32,256]{1,0:T(8,128)S(1)} %collective-permute-done.3.refs_2_.refs_1_, ...), custom_call_target="tpu_custom_call" | custom-call | bytes 131072 | tf_op jit(solution)/shard_map/pallas_call | solution.py:228
  18.4 0.0 collective-permute-done.6.given
  18.4 1.2 %shard_map.78 = f32[2,128,128]{2,1,0:T(8,128)} custom-call(bf16[80,256]{1,0:T(8,128)(2,1)S(1)} %get-tuple-element.29.high, bf16[80,256]{1,0:T(8,128)(2,1)S(1)} %get-tuple-element.30.low, f32[48,256]{1,0:T(8,128)S(1)} %collective-permute-done.6.given, bf16[256,256]{1,0:T(8,128)(2,1)S(1)} %get-tuple-element.27.refs_5_.right_high, ...), custom_call_target="tpu_custom_call" | custom-call | tf_op jit(solution)/shard_map/pallas_call | solution.py:307
  (1 shorter events, 0.0 us)
Async XLA Ops:
  0.0 2.9 %collective-permute-start = (f32[2,128,128]{2,1,0:T(8,128)}, f32[2,128,128]{2,1,0:T(8,128)S(1)}, u32[]{:S(2)}, u32[]{:S(2)}) collective-permute-start(f32[2,128,128]{2,1,0:T(8,128)} %bitcast.6), channel_id=1, source_target_pairs={{0,2},{1,3},{2,0},{3,1},{4,6},{5,7},{6,4},{7,5},{8,10},{9,11},{10,... | collective-permute-start | bytes 393224 | tf_op jit(solution)/shard_map/ppermute | solution.py:247
  0.5 2.4 %collective-permute-start.1 = (f32[1,1]{1,0:T(1,128)}, f32[1,1]{1,0:T(1,128)}, u32[]{:S(2)}, u32[]{:S(2)}) collective-permute-start(f32[1,1]{1,0:T(1,128)} %bitcast.1), channel_id=1, source_target_pairs={{0,2},{1,3},{2,0},{3,1},{4,6},{5,7},{6,4},{7,5},{8,10},{9,11},{10,... | collective-permute-start | bytes 20 | tf_op jit(solution)/shard_map/ppermute | solution.py:247
  3.8 7.3 %collective-permute-start.2 = (f32[32,256]{1,0:T(8,128)S(1)}, f32[32,256]{1,0:T(8,128)S(1)}, u32[]{:S(2)}, u32[]{:S(2)}) collective-permute-start(f32[32,256]{1,0:T(8,128)S(1)} %get-tuple-element.23), channel_id=1, source_target_pairs={{0,24},{1,25},{2,27},{3,26},{4,28},{5,29},{6,31},{7,30},{8,16},{9,... | collective-permute-start | bytes 98312 | tf_op jit(solution)/shard_map/ppermute | solution.py:247
  8.9 4.8 %collective-permute-start.3 = (f32[32,256]{1,0:T(8,128)S(1)}, f32[32,256]{1,0:T(8,128)S(1)}, u32[]{:S(2)}, u32[]{:S(2)}) collective-permute-start(f32[32,256]{1,0:T(8,128)S(1)} %get-tuple-element.24), channel_id=1, source_target_pairs={{0,9},{1,8},{2,10},{3,11},{4,13},{5,12},{6,14},{7,15},{8,1},{9,0},... | collective-permute-start | bytes 98312 | tf_op jit(solution)/shard_map/ppermute | solution.py:247
  9.4 4.8 %collective-permute-start.4 = (f32[32,256]{1,0:T(8,128)S(1)}, f32[32,256]{1,0:T(8,128)S(1)}, u32[]{:S(2)}, u32[]{:S(2)}) collective-permute-start(f32[32,256]{1,0:T(8,128)S(1)} %get-tuple-element.25), channel_id=1, source_target_pairs={{0,16},{1,17},{2,19},{3,18},{4,20},{5,21},{6,23},{7,22},{8,24},{9,... | collective-permute-start | bytes 98312 | tf_op jit(solution)/shard_map/ppermute | solution.py:247
  14.2 4.2 %collective-permute-start.6 = (f32[48,256]{1,0:T(8,128)S(1)}, f32[48,256]{1,0:T(8,128)S(1)}, u32[]{:S(2)}, u32[]{:S(2)}) collective-permute-start(f32[48,256]{1,0:T(8,128)S(1)} %shard_map.77), channel_id=1, source_target_pairs={{0,2},{1,3},{2,0},{3,1},{4,6},{5,7},{6,4},{7,5},{8,10},{9,11},{10,... | collective-permute-start | bytes 147464 | tf_op jit(solution)/shard_map/ppermute | solution.py:247
  14.2 4.0 %collective-permute-start.5 = (f32[16,256]{1,0:T(8,128)S(1)}, f32[16,256]{1,0:T(8,128)S(1)}, u32[]{:S(2)}, u32[]{:S(2)}) collective-permute-start(f32[16,256]{1,0:T(8,128)S(1)} %get-tuple-element.26), channel_id=1, source_target_pairs={{0,1},{1,0},{2,3},{3,2},{4,5},{5,4},{6,7},{7,6},{8,9},{9,8},{10,11... | collective-permute-start | bytes 49160 | tf_op jit(solution)/shard_map/ppermute | solution.py:247

commit v2 on v1

--- a/solution.py
+++ b/solution.py
@@ -10,6 +10,7 @@
 HIGH = lax.Precision.HIGHEST
 AXES = ("wide", "mid", "low")
 VSPEC = pl.BlockSpec(memory_space=pltpu.VMEM)
+HSPEC = pl.BlockSpec(memory_space=pltpu.HBM)
 SSPEC = pl.BlockSpec(memory_space=pltpu.SMEM)
 
 
@@ -38,15 +39,60 @@
     return product(left, tuple(embed(part) for part in right))
 
 
+COSINE = (
+    1.0,
+    -0.5,
+    0.0416666641831398,
+    -0.0013888862449675798,
+    2.480054899933748e-05,
+    -2.753473324901279e-07,
+    2.0603068140445657e-09,
+    -9.720916779865085e-12,
+)
+SINE = (
+    1.0,
+    -0.1666666716337204,
+    0.00833333283662796,
+    -0.00019841254106722772,
+    2.7556700388231548e-06,
+    -2.5038662698761982e-08,
+    1.5896317595576193e-10,
+    -6.609633630347278e-13,
+)
+
+
+def series(square, terms):
+    power = square
+    terms = list(terms)
+    while len(terms) > 1:
+        terms = [terms[k] + terms[k + 1] * power for k in range(0, len(terms), 2)]
+        power = power * power
+    return terms[0]
+
+
+def cosine_sine(angle):
+    square = angle * angle
+    return series(square, COSINE), angle * series(square, SINE)
+
+
 def turn(value, angle):
     half = value.shape[1] // 2
-    cosine, sine = jnp.cos(angle), jnp.sin(angle)
+    cosine, sine = cosine_sine(angle)
     real, imag = value[:, :half], value[:, half:]
     return jnp.concatenate([real * cosine - imag * sine, real * sine + imag * cosine], 1)
 
 
-def side(ref):
-    return jnp.concatenate([ref[0], ref[1]], 1)
+def side(ref, first=0):
+    return jnp.concatenate([ref[first], ref[first + 1]], 1)
+
+
+def gate(gates, number):
+    return side(gates, 2 * number)
+
+
+def scalars(ref):
+    value = ref[...]
+    return [value[0, place] for place in range(value.shape[1])]
 
 
 class Plan:
@@ -56,18 +102,13 @@
         self.wide_bits = wide_count.bit_length() - 1
         self.low_base = self.row_bits - self.wide_bits - 3
         self.chunk = rows // (2 * wide_count)
-        self.offsets = [wide_count - 1] + list(range(1, wide_count - 1))
-        self.slots = len(self.offsets)
-
-    def first(self, slot):
-        return slot % 2
-
-
-def pick(index, table):
-    value = jnp.zeros_like(index)
-    for place, entry in enumerate(table):
-        value = jnp.where(index == place, entry, value)
-    return value
+        self.steps = [((wide, 0), (wide, 1)) for wide in range(wide_count - 1, 0, -1)]
+        self.steps.insert(1, ((0, 1), (0, 1)))
+        self.shared = [step for step in self.steps if step[0] != step[1]]
+
+
+def by_core(step, core):
+    return tuple(a if a == b else a ^ (core * (a ^ b)) for a, b in zip(*step))
 
 
 def free_row(plan, inner, swap):
@@ -81,83 +122,102 @@
     )
 
 
-def sent_rows(plan, index, swaps, order):
-    wide, core, low = lax.axis_index("wide"), lax.axis_index("mid") & 1, lax.axis_index("low")
-    block, inner = index // plan.chunk, index % plan.chunk
-    wide_offsets, low_offsets, cores = [0], [0], [core]
-    for slot, offset in enumerate(plan.offsets):
-        wide_offsets += [offset, offset]
-        low_offsets += [core ^ plan.first(slot)] * 2
-        cores += [core, 1 - core]
-    wide_offsets.append(0)
-    low_offsets.append(1)
-    cores.append(core)
-    to_wide = wide ^ pick(block, wide_offsets)
-    to_low = (low & 1) ^ pick(block, low_offsets)
-    to_core = pick(block, cores)
-    row = free_row(plan, inner, swaps[1])
-    row |= jnp.left_shift(to_low, plan.low_base + swaps[1])
-    row |= jnp.left_shift(to_wide, plan.row_bits - plan.wide_bits)
+def bits(value, place, count=1):
+    return jnp.right_shift(value, place) & ((1 << count) - 1)
+
+
+def sent_rows(plan, swaps, order):
+    wide, core, low = lax.axis_index("wide"), lax.axis_index("mid") & 1, lax.axis_index("low") & 1
+    targets = [(wide, low, core)]
+    for step in plan.steps:
+        wide_part, low_part = by_core(step, core)
+        for to_core in (core, 1 - core)[: 2 if step in plan.shared else 1]:
+            targets.append((wide ^ wide_part, low ^ low_part, to_core))
     base = plan.row_bits - 4
-    old = row & ((1 << base) - 1)
-    for place in range(4):
-        old |= jnp.left_shift(jnp.right_shift(row, base + place) & 1, base + order[place])
     position = plan.row_bits - 3 + swaps[0]
-    from_core = jnp.right_shift(old, position) & 1
-    old = (old & ~jnp.left_shift(1, position)) | jnp.left_shift(to_core, position)
-    return old, from_core
-
-
-def received_rows(plan, index, swaps):
-    wide, core, low = lax.axis_index("wide"), lax.axis_index("mid") & 1, lax.axis_index("low")
-    block, inner = index // plan.chunk, index % plan.chunk
-    wide_offsets = [0] + plan.offsets + [0] + plan.offsets
-    low_offsets = [0] + [core ^ plan.first(slot) for slot in range(plan.slots)] + [1]
-    low_offsets += [1 - (core ^ plan.first(slot)) for slot in range(plan.slots)]
-    from_wide = wide ^ pick(block, wide_offsets)
-    from_low = (low & 1) ^ pick(block, low_offsets)
-    row = free_row(plan, inner, swaps[1])
-    row |= jnp.left_shift(from_low, plan.low_base + swaps[1])
-    return row | jnp.left_shift(from_wide, plan.row_bits - plan.wide_bits)
-
-
-def fetch(pairs, sems):
-    copies = [pltpu.make_async_copy(a, b, sems.at[place]) for place, (a, b) in enumerate(pairs)]
+    places = [base + order[place] for place in range(4)]
+
+    def reorder(row):
+        old = row & ((1 << base) - 1)
+        for place in range(4):
+            old |= jnp.left_shift(bits(row, base + place), places[place])
+        return old & ~jnp.left_shift(1, position), bits(old, position)
+
+    inner = lax.broadcasted_iota(jnp.int32, (plan.chunk, plan.rows), 0)
+    inner, inner_core = reorder(free_row(plan, inner, swaps[1]))
+    result = []
+    for to_wide, to_low, to_core in targets:
+        outer = jnp.left_shift(to_low, plan.low_base + swaps[1])
+        outer, outer_core = reorder(outer | (to_wide << (plan.row_bits - plan.wide_bits)))
+        outer |= jnp.left_shift(to_core, position)
+        result.append((inner | outer, inner_core | outer_core))
+    return result
+
+
+def received_rows(plan, swaps):
+    wide, core, low = lax.axis_index("wide"), lax.axis_index("mid") & 1, lax.axis_index("low") & 1
+    parts = [by_core(step, core) for step in plan.steps]
+    parts += [by_core(step, 1 - core) for step in plan.shared]
+    sources = [(wide, low)] + [(wide ^ part[0], low ^ part[1]) for part in parts]
+    inner = lax.broadcasted_iota(jnp.int32, (plan.chunk, plan.rows), 0)
+    inner = free_row(plan, inner, swaps[1])
+    result = []
+    for from_wide, from_low in sources:
+        outer = jnp.left_shift(from_low, plan.low_base + swaps[1])
+        result.append(inner | outer | (from_wide << (plan.row_bits - plan.wide_bits)))
+    return result
+
+
+def one_hot(plan, chunks):
+    column = lax.broadcasted_iota(jnp.int32, (plan.chunk, plan.rows), 1)
+    return jnp.concatenate([(column == rows).astype(jnp.bfloat16) for rows in chunks], 0)
+
+
+def phase_kernel(plan, phase_top, factors):
+    cosine, sine = cosine_sine(jnp.full(factors.shape, phase_top[0, 0, 0, 0]))
+    first = lax.broadcasted_iota(jnp.int32, factors.shape, 0) == 0
+    factors[...] = jnp.where(first, cosine, sine)
+
+
+def spin(value, factors):
+    half = value.shape[1] // 2
+    cosine, sine = factors[:1], factors[1:2]
+    real, imag = value[:, :half], value[:, half:]
+    return jnp.concatenate([real * cosine - imag * sine, real * sine + imag * cosine], 1)
+
+
+def front_kernel(plan, factors, state, gates, angle, swaps, order, own, high, low, *scratch):
+    *buffers, sems = scratch
+    sources = (swaps, order, gates.at[3], gates.at[1], angle, state)
+    copies = [
+        pltpu.make_async_copy(source, buffer, sems.at[place])
+        for place, (source, buffer) in enumerate(zip(sources, buffers))
+    ]
     for copy in copies:
         copy.start()
-    return copies
-
-
-def front_kernel(plan, gates, phase_mid, phase_top, state, swaps, order, own, high, low, *scratch):
-    *buffers, sems = scratch
-    sources = (swaps, order, gates.at[3], gates.at[1], phase_mid, state, phase_top)
-    copies = fetch(list(zip(sources, buffers)), sems)
-    swaps, order, gate_three, gate_one, phase_mid, state, phase_top = buffers
+    swaps, order, gate_three, gate_one, angle, state = buffers
     copies[0].wait()
     copies[1].wait()
-    rows = plan.rows
-    index = lax.broadcasted_iota(jnp.int32, (rows, rows), 0)
-    source, from_core = sent_rows(plan, index, swaps, order)
-    chosen = (lax.broadcasted_iota(jnp.int32, (rows, rows), 1) == source).astype(jnp.bfloat16)
+    chunks = sent_rows(plan, swaps, order)
+    chosen = one_hot(plan, [rows for rows, _ in chunks])
+    core = lax.axis_index("mid") & 1
+    mask = jnp.concatenate([(held == core).astype(jnp.float32) for _, held in chunks], 0)
+    mask = jnp.concatenate([mask, mask], 1)
     copies[2].wait()
-    outer = split(side(gate_three))
-    outer = tuple(dot(chosen, part).astype(jnp.bfloat16) for part in outer)
+    outer = tuple(dot(chosen, part).astype(jnp.bfloat16) for part in split(side(gate_three)))
     copies[3].wait()
     copies[4].wait()
-    inner = turn(side(gate_one), phase_mid[...])
+    inner = turn(side(gate_one), angle[...])
     merged = complex_product(outer, split(inner))
-    mine = jnp.concatenate([from_core == (lax.axis_index("mid") & 1)] * 2, 1)
-    zeros = jnp.zeros_like(merged)
     copies[5].wait()
-    copies[6].wait()
-    value = split(side(state))
-    own[...] = turn(complex_product(split(jnp.where(mine, merged, zeros)), value), phase_top[...])
-    high[...], low[...] = split(jnp.where(mine, zeros, merged))
-
-
-def send_kernel(plan, own, high, low, state, phase_top, *sent):
-    value = split(side(state))
-    total = own[...] + turn(complex_product((high[...], low[...]), value), phase_top[...])
+    total = complex_product(split(merged * mask), split(side(state)))
+    own[...] = spin(total, factors[...])
+    high[...], low[...] = split(merged * (1.0 - mask))
+
+
+def send_kernel(plan, own, high, low, state, factors, *sent):
+    total = complex_product((high[...], low[...]), split(side(state)))
+    total = own[...] + spin(total, factors[...])
     start = 0
     for ref in sent:
         ref[...] = total[start : start + ref.shape[0]]
@@ -168,16 +228,13 @@
     del kept
     rows = plan.rows
 
-    def gate(number):
-        return split(side(gates.at[number]))
-
     def chain(numbers, value):
         for number in numbers:
-            value = complex_product(gate(number), split(value))
+            value = complex_product(split(gate(gates, number)), split(value))
         return value
 
-    right = turn(side(gates.at[2]), phase_low[...])
-    right = complex_product(split(right), gate(0))
+    right = turn(gate(gates, 2), phase_low[...])
+    right = complex_product(split(right), split(gate(gates, 0)))
     right = chain(range(4, count, 2), right)
     half = rows
     real, imag = right[:, :half], right[:, half:]
@@ -185,23 +242,22 @@
         [jnp.concatenate([real, -imag], 1), jnp.concatenate([imag, real], 1)], 0
     )
     right_high[...], right_low[...] = split(right)
-    index = lax.broadcasted_iota(jnp.int32, (rows, rows), 1)
-    target = received_rows(plan, index, swaps)
-    placed = (lax.broadcasted_iota(jnp.int32, (rows, rows), 0) == target).astype(jnp.bfloat16)
+    placed = one_hot(plan, received_rows(plan, scalars(swaps)))
     first = tuple(
-        jnp.concatenate([dot(part[:, :half], placed), dot(part[:, half:], placed)], 1)
-        for part in gate(5)
-    )
-    left = complex_product(gate(7), tuple(part.astype(jnp.bfloat16) for part in first))
+        jnp.concatenate([dot(part[:, :half], placed, True), dot(part[:, half:], placed, True)], 1)
+        for part in split(gate(gates, 5))
+    )
+    left = complex_product(split(gate(gates, 7)), tuple(part.astype(jnp.bfloat16) for part in first))
     left = chain(range(9, count, 2), left)
     left_high[...], left_low[...] = split(left)
 
 
 def sort_kernel(plan, *refs):
-    chunk = plan.chunk
-    received, give = refs[: plan.slots], refs[-1]
-    for slot, ref in enumerate(received):
-        give[slot * chunk : (slot + 1) * chunk] = ref[chunk:]
+    give, place = refs[-1], 0
+    for step, ref in zip(plan.steps, refs):
+        if step in plan.shared:
+            give[place : place + plan.chunk] = ref[plan.chunk :]
+            place += plan.chunk
 
 
 def kept_kernel(plan, *refs):
@@ -222,28 +278,28 @@
 
 def call(kernel, shapes, args, specs, flops=0, scratch=()):
     args = [
-        pltpu.with_memory_space_constraint(arg, pltpu.VMEM) if spec is VSPEC else arg
+        arg if spec is SSPEC else pltpu.with_memory_space_constraint(arg, spec.memory_space)
         for arg, spec in zip(args, specs)
     ]
     return pl.pallas_call(
         kernel,
         out_shape=[pltpu.VMEM(shape, dtype) for shape, dtype in shapes],
-        in_specs=[pl.BlockSpec() if spec is None else spec for spec in specs],
+        in_specs=specs,
         out_specs=[VSPEC] * len(shapes),
         scratch_shapes=scratch,
         cost_estimate=pl.CostEstimate(flops=flops, bytes_accessed=1 << 17, transcendentals=0),
     )(*args)
 
 
-def exchange(value, offset, cores=(0, 0), flip=0):
+def exchange(value, step=((0, 0), (0, 0)), flip=0):
     wides, mids, lows = (lax.axis_size(axis) for axis in AXES)
     pairs = []
     for wide in range(wides):
         for mid in range(mids):
             for low in range(lows):
-                source = (wide * mids + mid) * lows + low
-                to = ((wide ^ offset) * mids + (mid ^ flip)) * lows + (low ^ cores[mid & 1])
-                pairs.append((source, to))
+                wide_part, low_part = step[mid & 1]
+                to = ((wide ^ wide_part) * mids + (mid ^ flip)) * lows + (low ^ low_part)
+                pairs.append(((wide * mids + mid) * lows + low, to))
     return lax.ppermute(value, AXES, pairs)
 
 
@@ -253,55 +309,55 @@
     chunk = plan.chunk
     f32, bf16 = jnp.float32, jnp.bfloat16
     square = state.reshape(2, rows, rows)
-    top = phase_top.reshape(1, 1)
-    other = exchange(square, 0, flip=1)
-    other_top = exchange(top, 0, flip=1)
-
+    other = exchange(square, flip=1)
+    (factors,) = call(partial(phase_kernel, plan), [((8, rows), f32)], (phase_top,), (SSPEC,))
+    other_factors = exchange(factors, flip=1)
     pair = pltpu.VMEM((2, rows, rows), f32)
-    sources = (gates, phase_mid.reshape(1, rows), top, square, swap_qubits, regroup_order)
-    buffers = [pltpu.SMEM(arg.shape, arg.dtype) for arg in sources[4:]]
-    buffers += [pair, pair, pltpu.VMEM((1, rows), f32), pair, pltpu.VMEM((1, 1), f32)]
+    scratch = [pltpu.SMEM(arg.shape, arg.dtype) for arg in (swap_qubits, regroup_order)]
+    scratch += [pair, pair, pltpu.VMEM((1, rows), f32), pair, pltpu.SemaphoreType.DMA((6,))]
     own, high, low = call(
         partial(front_kernel, plan),
         [((rows, 2 * rows), f32), ((rows, 2 * rows), bf16), ((rows, 2 * rows), bf16)],
-        sources,
-        (pl.BlockSpec(memory_space=pl.ANY),) * len(sources),
-        scratch=buffers + [pltpu.SemaphoreType.DMA((len(buffers),))],
-    )
-    shapes = [(chunk, 2 * rows)] + [(2 * chunk, 2 * rows)] * plan.slots + [(chunk, 2 * rows)]
+        (factors, square, gates, phase_mid.reshape(1, rows), swap_qubits, regroup_order),
+        (VSPEC,) + (HSPEC,) * 5,
+        scratch=scratch,
+    )
+    shapes = [(chunk, 2 * rows)]
+    shapes += [(2 * chunk if step in plan.shared else chunk, 2 * rows) for step in plan.steps]
     local, *sent = call(
         partial(send_kernel, plan),
         [(shape, f32) for shape in shapes],
-        (own, high, low, other, other_top),
+        (own, high, low, other, other_factors),
         (VSPEC,) * 5,
     )
-    received = [
-        exchange(value, offset, (plan.first(slot), 1 - plan.first(slot)))
-        for slot, (value, offset) in enumerate(zip(sent, plan.offsets))
-    ]
-    received.append(exchange(sent[-1], 0, (1, 1)))
+    received = [exchange(value, step) for value, step in zip(sent, plan.steps)]
     wide_square = ((2 * rows, 2 * rows), bf16)
     tall = ((rows, 2 * rows), bf16)
     right_high, right_low, left_high, left_low = call(
         partial(back_kernel, plan, gates.shape[0]),
         [wide_square, wide_square, tall, tall],
-        (gates, phase_low.reshape(1, rows), swap_qubits, local),
-        (None, None, SSPEC, VSPEC),
+        (
+            gates.reshape(-1, rows, rows),
+            phase_low.reshape(1, rows),
+            swap_qubits.reshape(1, -1),
+            local,
+        ),
+        (VSPEC,) * 4,
         flops=6 * 24 * rows**3,
     )
     (give,) = call(
         partial(sort_kernel, plan),
-        [((plan.slots * chunk, 2 * rows), f32)],
-        received[:-1],
-        (VSPEC,) * plan.slots,
-    )
-    given = exchange(give, 0, flip=1)
-    kept_rows = (plan.slots + 2) * chunk
+        [((len(plan.shared) * chunk, 2 * rows), f32)],
+        (*received, left_low),
+        (VSPEC,) * (len(received) + 1),
+    )
+    given = exchange(give, flip=1)
+    kept_rows = (len(received) + 1) * chunk
     high, low = call(
         partial(kept_kernel, plan),
         [((kept_rows, 2 * rows), bf16)] * 2,
         (local, *received, right_high, right_low),
-        (VSPEC,) * (plan.slots + 4),
+        (VSPEC,) * (len(received) + 3),
     )
     args = (high, low, given, right_high, right_low, left_high, left_low)
     out = pl.pallas_call(

time: 19.8 us -> 16 us (0.81)
  Pallas kernels: 6.78 us -> 4.77 us
  waiting for transfers between devices: 3.59 us -> 1.81 us
    pallas_call x5 -> x6, Pallas kernels: 5.63 us -> 3.62 us  [call(): pl.pallas_call(kernel, out_shape=[pltpu.VMEM(shape, dtype) for shape, dty...]
    ppermute x7, waiting for transfers between devices: 3.59 us -> 1.81 us  [exchange(): return lax.ppermute(value, AXES, pairs)]
  transfers between devices with their start and end apart: 7 -> 7, of which waited for: 3 -> 3; matrix products, arithmetic and copies ran while one was open for 0% -> 0% of each run, Pallas kernels for 24% -> 21%
where the time goes in v2:
time: 16 us; the launch traced here: 15.9 us
  starting transfers between devices  8.59 us (54%)
  Pallas kernels  4.77 us (30%)
  waiting for transfers between devices  1.81 us (11%)
  between operations  0.71 us (4%)
    ppermute x7, starting transfers between devices, exchange(): return lax.ppermute(value, AXES, pairs)  8.59 us
    pallas_call x6, Pallas kernels, call(): pl.pallas_call(kernel, out_shape=[pltpu.VMEM(shape, dtype) for shape, dty...  3.62 us
    ppermute x7, waiting for transfers between devices, exchange(): return lax.ppermute(value, AXES, pairs)  1.81 us
    pallas_call x1, Pallas kernels, merged_device(): pl.pallas_call(partial(last_kernel, plan), out_shape=jax.ShapeDtypeStruct...  1.15 us
  transfers between devices with their start and end apart: 7, of which 3 were waited for; matrix products, arithmetic and copies ran while one was open for 0% of the time, Pallas kernels for 21%

profile of v2, /device:TPU:0, one launch (start us, length us, event | category | flops | bytes accessed | tf_op | source)
XLA Modules:
  0.0 15.9 jit_solution(6276234626528742804)
XLA Ops:
  0.0 0.0 copy-start
  0.0 0.0 copy-start.1
  0.0 0.0 copy-start.2
  0.0 0.5 %collective-permute-start = (f32[2,128,128]{2,1,0:T(8,128)}, f32[2,128,128]{2,1,0:T(8,128)S(1)}, u32[]{:S(2)}, u32[]{:S(2)}) collective-permute-start(f32[2,128,128]{2,1,0:T(8,128)} %bitcast.9), channel_id=1, source_target_pairs={{0,2},{1,3},{2,0},{3,1},{4,6},{5,7},{6,4},{7,5},{8,10},{9,11},{10,... | collective-permute-start | bytes 393224 | tf_op jit(solution)/shard_map/ppermute | solution.py:303
  1.2 0.2 %collective-permute-start.1 = (f32[8,128]{1,0:T(8,128)S(1)}, f32[8,128]{1,0:T(8,128)S(1)}, u32[]{:S(2)}, u32[]{:S(2)}) collective-permute-start(f32[8,128]{1,0:T(8,128)S(1)} %shard_map.73.factors), channel_id=1, source_target_pairs={{0,2},{1,3},{2,0},{3,1},{4,6},{5,7},{6,4},{7,5},{8,10},{9,11},{10,... | collective-permute-start | bytes 12296 | tf_op jit(solution)/shard_map/ppermute | solution.py:303
  1.4 1.7 %shard_map.74 = (f32[128,256]{1,0:T(8,128)S(1)}, bf16[128,256]{1,0:T(8,128)(2,1)S(1)}, bf16[128,256]{1,0:T(8,128)(2,1)S(1)}) custom-call(f32[8,128]{1,0:T(8,128)S(1)} %shard_map.73.factors, f32[2,128,128]{2,1,0:T(8,128)} %bitcast.10, f32[10,2,128,128]{3,2,1,0:T(8,128)} %gates.1, f32[1,128]{1,0:T(1,128)} %bitcast.11, s32[2]{0:T(128)} %swaps.1, s32[4]{0:T(128)} %order.1), custom_call_target="tpu_custom_call" | custom-call | bytes 131072 | tf_op jit(solution)/shard_map/pallas_call | solution.py:284
  3.0 0.0 collective-permute-done.1.factors
  3.1 0.0 collective-permute-done.state
  3.1 0.2 %shard_map.75 = (f32[16,256]{1,0:T(8,128)S(1)}, f32[32,256]{1,0:T(8,128)S(1)}, f32[16,256]{1,0:T(8,128)S(1)}, f32[32,256]{1,0:T(8,128)S(1)}, f32[32,256]{1,0:T(8,128)S(1)}) custom-call(f32[128,256]{1,0:T(8,128)S(1)} %get-tuple-element.19.own, bf16[128,256]{1,0:T(8,128)(2,1)S(1)} %get-tuple-element.20.high, bf16[128,256]{1,0:T(8,128)(2,1)S(1)} %get-tuple-element.21.low, ...), custom_call_target="tpu_custom_call" | custom-call | bytes 131072 | tf_op jit(solution)/shard_map/pallas_call | solution.py:284
  3.3 5.1 %collective-permute-start.2 = (f32[32,256]{1,0:T(8,128)S(1)}, f32[32,256]{1,0:T(8,128)S(1)}, u32[]{:S(2)}, u32[]{:S(2)}) collective-permute-start(f32[32,256]{1,0:T(8,128)S(1)} %get-tuple-element.23), channel_id=1, source_target_pairs={{0,24},{1,25},{2,27},{3,26},{4,28},{5,29},{6,31},{7,30},{8,16},{9,... | collective-permute-start | bytes 98312 | tf_op jit(solution)/shard_map/ppermute | solution.py:303
  8.4 0.0 collective-permute-start.4
  8.4 0.6 %collective-permute-start.5 = (f32[32,256]{1,0:T(8,128)S(1)}, f32[32,256]{1,0:T(8,128)S(1)}, u32[]{:S(2)}, u32[]{:S(2)}) collective-permute-start(f32[32,256]{1,0:T(8,128)S(1)} %get-tuple-element.26), channel_id=1, source_target_pairs={{0,8},{1,9},{2,11},{3,10},{4,12},{5,13},{6,15},{7,14},{8,0},{9,1},... | collective-permute-start | bytes 98312 | tf_op jit(solution)/shard_map/ppermute | solution.py:303
  9.0 1.6 %collective-permute-start.3 = (f32[16,256]{1,0:T(8,128)S(1)}, f32[16,256]{1,0:T(8,128)S(1)}, u32[]{:S(2)}, u32[]{:S(2)}) collective-permute-start(f32[16,256]{1,0:T(8,128)S(1)} %get-tuple-element.24), channel_id=1, source_target_pairs={{0,1},{1,0},{2,3},{3,2},{4,5},{5,4},{6,7},{7,6},{8,9},{9,8},{10,11... | collective-permute-start | bytes 49160 | tf_op jit(solution)/shard_map/ppermute | solution.py:303
  10.7 0.0 copy-done
  10.7 0.0 copy-done.1
  10.7 0.0 copy-done.2
  10.7 1.5 %shard_map.76 = (bf16[256,256]{1,0:T(8,128)(2,1)S(1)}, bf16[256,256]{1,0:T(8,128)(2,1)S(1)}, bf16[128,256]{1,0:T(8,128)(2,1)S(1)}, bf16[128,256]{1,0:T(8,128)(2,1)S(1)}) custom-call(f32[20,128,128]{2,1,0:T(8,128)S(1)} %bitcast.6, f32[1,128]{1,0:T(1,128)S(1)} %bitcast.8, s32[1,2]{1,0:T(1,128)S(1)} %bitcast.7, f32[16,256]{1,0:T(8,128)S(1)} %get-tuple-element.22.kept.refs_0_), custom_call_target="tpu_custom_call" | custom-call | flops 301989888 | bytes 131072 | tf_op jit(solution)/shard_map/pallas_call | solution.py:284
  12.1 1.0 %collective-permute-done.3.refs_2_.refs_1_ = f32[16,256]{1,0:T(8,128)S(1)} collective-permute-done((f32[16,256]{1,0:T(8,128)S(1)}, f32[16,256]{1,0:T(8,128)S(1)}, u32[]{:S(2)}, u32[]{:S(2)}) %collective-permute-start.3) | collective-permute-done | bytes 16416 | tf_op jit(solution)/shard_map/ppermute | solution.py:303
  13.2 0.0 collective-permute-done.2.refs_1_.refs_0_
  13.2 0.1 collective-permute-done.4.refs_3_.refs_2_
  13.3 0.0 collective-permute-done.5.refs_4_.refs_3_
  13.3 0.6 %collective-permute-start.6 = (f32[48,256]{1,0:T(8,128)S(1)}, f32[48,256]{1,0:T(8,128)S(1)}, u32[]{:S(2)}, u32[]{:S(2)}) collective-permute-start(f32[48,256]{1,0:T(8,128)S(1)} %shard_map.78), channel_id=1, source_target_pairs={{0,2},{1,3},{2,0},{3,1},{4,6},{5,7},{6,4},{7,5},{8,10},{9,11},{10,... | collective-permute-start | bytes 147464 | tf_op jit(solution)/shard_map/ppermute | solution.py:303
  13.9 0.2 %shard_map.77 = (bf16[80,256]{1,0:T(8,128)(2,1)S(1)}, bf16[80,256]{1,0:T(8,128)(2,1)S(1)}) custom-call(f32[16,256]{1,0:T(8,128)S(1)} %get-tuple-element.22.kept.refs_0_, f32[32,256]{1,0:T(8,128)S(1)} %collective-permute-done.2.refs_1_.refs_0_, f32[16,256]{1,0:T(8,128)S(1)} %collective-permute-done.3.refs_2_.refs_1_, ...), custom_call_target="tpu_custom_call" | custom-call | bytes 131072 | tf_op jit(solution)/shard_map/pallas_call | solution.py:284
  14.1 0.6 %collective-permute-done.6.given = f32[48,256]{1,0:T(8,128)S(1)} collective-permute-done((f32[48,256]{1,0:T(8,128)S(1)}, f32[48,256]{1,0:T(8,128)S(1)}, u32[]{:S(2)}, u32[]{:S(2)}) %collective-permute-start.6) | collective-permute-done | bytes 49184 | tf_op jit(solution)/shard_map/ppermute | solution.py:303
  14.7 1.2 %shard_map.79 = f32[2,128,128]{2,1,0:T(8,128)} custom-call(bf16[80,256]{1,0:T(8,128)(2,1)S(1)} %get-tuple-element.29.high, bf16[80,256]{1,0:T(8,128)(2,1)S(1)} %get-tuple-element.30.low, f32[48,256]{1,0:T(8,128)S(1)} %collective-permute-done.6.given, bf16[256,256]{1,0:T(8,128)(2,1)S(1)} %get-tuple-element.27.refs_5_.right_high, ...), custom_call_target="tpu_custom_call" | custom-call | tf_op jit(solution)/shard_map/pallas_call | solution.py:363
  (2 shorter events, 0.0 us)
Async XLA Ops:
  0.0 10.7 %copy-start = (f32[10,2,128,128]{3,2,1,0:T(8,128)S(1)}, f32[10,2,128,128]{3,2,1,0:T(8,128)}, u32[]{:S(2)}) copy-start(f32[10,2,128,128]{3,2,1,0:T(8,128)} %gates.1) | copy-start | bytes 3932164
  0.0 10.7 %copy-start.1 = (s32[2]{0:T(128)S(1)}, s32[2]{0:T(128)}, u32[]{:S(2)}) copy-start(s32[2]{0:T(128)} %swaps.1) | copy-start | bytes 28
  0.0 10.7 %copy-start.2 = (f32[128]{0:T(128)S(1)}, f32[128]{0:T(128)}, u32[]{:S(2)}) copy-start(f32[128]{0:T(128)} %param.9) | copy-start | bytes 1540
  0.0 3.1 %collective-permute-start = (f32[2,128,128]{2,1,0:T(8,128)}, f32[2,128,128]{2,1,0:T(8,128)S(1)}, u32[]{:S(2)}, u32[]{:S(2)}) collective-permute-start(f32[2,128,128]{2,1,0:T(8,128)} %bitcast.9), channel_id=1, source_target_pairs={{0,2},{1,3},{2,0},{3,1},{4,6},{5,7},{6,4},{7,5},{8,10},{9,11},{10,... | collective-permute-start | bytes 393224 | tf_op jit(solution)/shard_map/ppermute | solution.py:303
  1.2 1.9 %collective-permute-start.1 = (f32[8,128]{1,0:T(8,128)S(1)}, f32[8,128]{1,0:T(8,128)S(1)}, u32[]{:S(2)}, u32[]{:S(2)}) collective-permute-start(f32[8,128]{1,0:T(8,128)S(1)} %shard_map.73.factors), channel_id=1, source_target_pairs={{0,2},{1,3},{2,0},{3,1},{4,6},{5,7},{6,4},{7,5},{8,10},{9,11},{10,... | collective-permute-start | bytes 12296 | tf_op jit(solution)/shard_map/ppermute | solution.py:303
  3.3 9.8 %collective-permute-start.2 = (f32[32,256]{1,0:T(8,128)S(1)}, f32[32,256]{1,0:T(8,128)S(1)}, u32[]{:S(2)}, u32[]{:S(2)}) collective-permute-start(f32[32,256]{1,0:T(8,128)S(1)} %get-tuple-element.23), channel_id=1, source_target_pairs={{0,24},{1,25},{2,27},{3,26},{4,28},{5,29},{6,31},{7,30},{8,16},{9,... | collective-permute-start | bytes 98312 | tf_op jit(solution)/shard_map/ppermute | solution.py:303
  8.4 4.9 %collective-permute-start.4 = (f32[32,256]{1,0:T(8,128)S(1)}, f32[32,256]{1,0:T(8,128)S(1)}, u32[]{:S(2)}, u32[]{:S(2)}) collective-permute-start(f32[32,256]{1,0:T(8,128)S(1)} %get-tuple-element.25), channel_id=1, source_target_pairs={{0,16},{1,17},{2,19},{3,18},{4,20},{5,21},{6,23},{7,22},{8,24},{9,... | collective-permute-start | bytes 98312 | tf_op jit(solution)/shard_map/ppermute | solution.py:303
  8.4 4.9 %collective-permute-start.5 = (f32[32,256]{1,0:T(8,128)S(1)}, f32[32,256]{1,0:T(8,128)S(1)}, u32[]{:S(2)}, u32[]{:S(2)}) collective-permute-start(f32[32,256]{1,0:T(8,128)S(1)} %get-tuple-element.26), channel_id=1, source_target_pairs={{0,8},{1,9},{2,11},{3,10},{4,12},{5,13},{6,15},{7,14},{8,0},{9,1},... | collective-permute-start | bytes 98312 | tf_op jit(solution)/shard_map/ppermute | solution.py:303
  9.0 4.1 %collective-permute-start.3 = (f32[16,256]{1,0:T(8,128)S(1)}, f32[16,256]{1,0:T(8,128)S(1)}, u32[]{:S(2)}, u32[]{:S(2)}) collective-permute-start(f32[16,256]{1,0:T(8,128)S(1)} %get-tuple-element.24), channel_id=1, source_target_pairs={{0,1},{1,0},{2,3},{3,2},{4,5},{5,4},{6,7},{7,6},{8,9},{9,8},{10,11... | collective-permute-start | bytes 49160 | tf_op jit(solution)/shard_map/ppermute | solution.py:303
  13.3 1.4 %collective-permute-start.6 = (f32[48,256]{1,0:T(8,128)S(1)}, f32[48,256]{1,0:T(8,128)S(1)}, u32[]{:S(2)}, u32[]{:S(2)}) collective-permute-start(f32[48,256]{1,0:T(8,128)S(1)} %shard_map.78), channel_id=1, source_target_pairs={{0,2},{1,3},{2,0},{3,1},{4,6},{5,7},{6,4},{7,5},{8,10},{9,11},{10,... | collective-permute-start | bytes 147464 | tf_op jit(solution)/shard_map/ppermute | solution.py:303

commit v3 on v2

--- a/solution.py
+++ b/solution.py
@@ -8,9 +8,10 @@
 from jax.sharding import PartitionSpec as P
 
 HIGH = lax.Precision.HIGHEST
+BUSY = 1 << 29
+LONG = 1 << 32
 AXES = ("wide", "mid", "low")
 VSPEC = pl.BlockSpec(memory_space=pltpu.VMEM)
-HSPEC = pl.BlockSpec(memory_space=pltpu.HBM)
 SSPEC = pl.BlockSpec(memory_space=pltpu.SMEM)
 
 
@@ -186,32 +187,16 @@
     return jnp.concatenate([real * cosine - imag * sine, real * sine + imag * cosine], 1)
 
 
-def front_kernel(plan, factors, state, gates, angle, swaps, order, own, high, low, *scratch):
-    *buffers, sems = scratch
-    sources = (swaps, order, gates.at[3], gates.at[1], angle, state)
-    copies = [
-        pltpu.make_async_copy(source, buffer, sems.at[place])
-        for place, (source, buffer) in enumerate(zip(sources, buffers))
-    ]
-    for copy in copies:
-        copy.start()
-    swaps, order, gate_three, gate_one, angle, state = buffers
-    copies[0].wait()
-    copies[1].wait()
-    chunks = sent_rows(plan, swaps, order)
+def front_kernel(plan, state, factors, gates, angle, swaps, order, own, high, low):
+    chunks = sent_rows(plan, scalars(swaps), scalars(order))
     chosen = one_hot(plan, [rows for rows, _ in chunks])
     core = lax.axis_index("mid") & 1
     mask = jnp.concatenate([(held == core).astype(jnp.float32) for _, held in chunks], 0)
     mask = jnp.concatenate([mask, mask], 1)
-    copies[2].wait()
-    outer = tuple(dot(chosen, part).astype(jnp.bfloat16) for part in split(side(gate_three)))
-    copies[3].wait()
-    copies[4].wait()
-    inner = turn(side(gate_one), angle[...])
+    outer = tuple(dot(chosen, part).astype(jnp.bfloat16) for part in split(gate(gates, 3)))
+    inner = turn(gate(gates, 1), angle[...])
     merged = complex_product(outer, split(inner))
-    copies[5].wait()
-    total = complex_product(split(merged * mask), split(side(state)))
-    own[...] = spin(total, factors[...])
+    own[...] = spin(complex_product(split(merged * mask), split(side(state))), factors[...])
     high[...], low[...] = split(merged * (1.0 - mask))
 
 
@@ -224,40 +209,48 @@
         start += ref.shape[0]
 
 
-def back_kernel(plan, count, gates, phase_low, swaps, kept, right_high, right_low, left_high, left_low):
+def chain(factors):
+    while len(factors) > 1:
+        pairs = [factors[k : k + 2] for k in range(0, len(factors), 2)]
+        factors = [
+            complex_product(split(pair[0]), split(pair[1])) if len(pair) == 2 else pair[0]
+            for pair in pairs
+        ]
+    return factors[0]
+
+
+def right_kernel(plan, count, gates, phase_low, high, low):
+    factors = [gate(gates, number) for number in range((count - 1) // 2 * 2, 2, -2)]
+    value = chain(factors + [turn(gate(gates, 2), phase_low[...]), gate(gates, 0)])
+    real, imag = value[:, : plan.rows], value[:, plan.rows :]
+    high[...], low[...] = split(
+        jnp.concatenate(
+            [jnp.concatenate([real, -imag], 1), jnp.concatenate([imag, real], 1)], 0
+        )
+    )
+
+
+def left_kernel(plan, count, gates, swaps, high, low):
+    placed = one_hot(plan, received_rows(plan, scalars(swaps)))
+    first = gate(gates, 5)
+    first = [
+        sum(dot(part, placed, True) for part in split(half))
+        for half in (first[:, : plan.rows], first[:, plan.rows :])
+    ]
+    factors = [gate(gates, number) for number in range((count - 2) // 2 * 2 + 1, 5, -2)]
+    high[...], low[...] = split(chain(factors + [jnp.concatenate(first, 1)]))
+
+
+def back_kernel(plan, count, gates, phase_low, swaps, kept, *factors):
     del kept
-    rows = plan.rows
-
-    def chain(numbers, value):
-        for number in numbers:
-            value = complex_product(split(gate(gates, number)), split(value))
-        return value
-
-    right = turn(gate(gates, 2), phase_low[...])
-    right = complex_product(split(right), split(gate(gates, 0)))
-    right = chain(range(4, count, 2), right)
-    half = rows
-    real, imag = right[:, :half], right[:, half:]
-    right = jnp.concatenate(
-        [jnp.concatenate([real, -imag], 1), jnp.concatenate([imag, real], 1)], 0
-    )
-    right_high[...], right_low[...] = split(right)
-    placed = one_hot(plan, received_rows(plan, scalars(swaps)))
-    first = tuple(
-        jnp.concatenate([dot(part[:, :half], placed, True), dot(part[:, half:], placed, True)], 1)
-        for part in split(gate(gates, 5))
-    )
-    left = complex_product(split(gate(gates, 7)), tuple(part.astype(jnp.bfloat16) for part in first))
-    left = chain(range(9, count, 2), left)
-    left_high[...], left_low[...] = split(left)
+    right_kernel(plan, count, gates, phase_low, *factors[:2])
+    left_kernel(plan, count, gates, swaps, *factors[2:])
 
 
 def sort_kernel(plan, *refs):
-    give, place = refs[-1], 0
-    for step, ref in zip(plan.steps, refs):
-        if step in plan.shared:
-            give[place : place + plan.chunk] = ref[plan.chunk :]
-            place += plan.chunk
+    give = refs[-1]
+    for place, ref in enumerate(refs[: len(plan.shared)]):
+        give[place * plan.chunk : (place + 1) * plan.chunk] = ref[plan.chunk :]
 
 
 def kept_kernel(plan, *refs):
@@ -276,7 +269,7 @@
     out[1] = result[:, half:]
 
 
-def call(kernel, shapes, args, specs, flops=0, scratch=()):
+def call(kernel, shapes, args, specs, flops=0):
     args = [
         arg if spec is SSPEC else pltpu.with_memory_space_constraint(arg, spec.memory_space)
         for arg, spec in zip(args, specs)
@@ -286,7 +279,6 @@
         out_shape=[pltpu.VMEM(shape, dtype) for shape, dtype in shapes],
         in_specs=specs,
         out_specs=[VSPEC] * len(shapes),
-        scratch_shapes=scratch,
         cost_estimate=pl.CostEstimate(flops=flops, bytes_accessed=1 << 17, transcendentals=0),
     )(*args)
 
@@ -308,19 +300,17 @@
     plan = Plan(rows, lax.axis_size("wide"))
     chunk = plan.chunk
     f32, bf16 = jnp.float32, jnp.bfloat16
+    gates = gates.reshape(-1, rows, rows)
+    swaps, order = swap_qubits.reshape(1, -1), regroup_order.reshape(1, -1)
     square = state.reshape(2, rows, rows)
     other = exchange(square, flip=1)
-    (factors,) = call(partial(phase_kernel, plan), [((8, rows), f32)], (phase_top,), (SSPEC,))
+    (factors,) = call(partial(phase_kernel, plan), [((8, rows), f32)], (phase_top,), (SSPEC,), BUSY)
     other_factors = exchange(factors, flip=1)
-    pair = pltpu.VMEM((2, rows, rows), f32)
-    scratch = [pltpu.SMEM(arg.shape, arg.dtype) for arg in (swap_qubits, regroup_order)]
-    scratch += [pair, pair, pltpu.VMEM((1, rows), f32), pair, pltpu.SemaphoreType.DMA((6,))]
     own, high, low = call(
         partial(front_kernel, plan),
         [((rows, 2 * rows), f32), ((rows, 2 * rows), bf16), ((rows, 2 * rows), bf16)],
-        (factors, square, gates, phase_mid.reshape(1, rows), swap_qubits, regroup_order),
-        (VSPEC,) + (HSPEC,) * 5,
-        scratch=scratch,
+        (square, factors, gates, phase_mid.reshape(1, rows), swaps, order),
+        (VSPEC,) * 6,
     )
     shapes = [(chunk, 2 * rows)]
     shapes += [(2 * chunk if step in plan.shared else chunk, 2 * rows) for step in plan.steps]
@@ -331,25 +321,18 @@
         (VSPEC,) * 5,
     )
     received = [exchange(value, step) for value, step in zip(sent, plan.steps)]
-    wide_square = ((2 * rows, 2 * rows), bf16)
-    tall = ((rows, 2 * rows), bf16)
     right_high, right_low, left_high, left_low = call(
-        partial(back_kernel, plan, gates.shape[0]),
-        [wide_square, wide_square, tall, tall],
-        (
-            gates.reshape(-1, rows, rows),
-            phase_low.reshape(1, rows),
-            swap_qubits.reshape(1, -1),
-            local,
-        ),
+        partial(back_kernel, plan, gates.shape[0] // 2),
+        [((2 * rows, 2 * rows), bf16)] * 2 + [((rows, 2 * rows), bf16)] * 2,
+        (gates, phase_low.reshape(1, rows), swaps, local),
         (VSPEC,) * 4,
-        flops=6 * 24 * rows**3,
-    )
+    )
+    shared = [value for value, step in zip(received, plan.steps) if step in plan.shared]
     (give,) = call(
         partial(sort_kernel, plan),
         [((len(plan.shared) * chunk, 2 * rows), f32)],
-        (*received, left_low),
-        (VSPEC,) * (len(received) + 1),
+        (*shared, left_low),
+        (VSPEC,) * (len(shared) + 1),
     )
     given = exchange(give, flip=1)
     kept_rows = (len(received) + 1) * chunk
@@ -358,6 +341,7 @@
         [((kept_rows, 2 * rows), bf16)] * 2,
         (local, *received, right_high, right_low),
         (VSPEC,) * (len(received) + 3),
+        LONG,
     )
     args = (high, low, given, right_high, right_low, left_high, left_low)
     out = pl.pallas_call(

time: 16 us -> 15.7 us (0.981)
  Pallas kernels: 4.77 us -> 3.3 us
  waiting for transfers between devices: 1.81 us -> 2.84 us
    pallas_call x6, Pallas kernels: 3.62 us -> 2.15 us  [call(): pl.pallas_call(kernel, out_shape=[pltpu.VMEM(shape, dtype) for shape, dty...]
    ppermute x7, waiting for transfers between devices: 1.81 us -> 2.84 us  [exchange(): return lax.ppermute(value, AXES, pairs)]
  transfers between devices with their start and end apart: 7 -> 7, of which waited for: 3 -> 3; matrix products, arithmetic and copies ran while one was open for 0% -> 0% of each run, Pallas kernels for 21% -> 12%
where the time goes in v3:
time: 15.7 us; the launch traced here: 15.5 us
  starting transfers between devices  8.65 us (55%)
  Pallas kernels  3.3 us (21%)
  waiting for transfers between devices  2.84 us (18%)
  between operations  0.73 us (5%)
    ppermute x7, starting transfers between devices, exchange(): return lax.ppermute(value, AXES, pairs)  8.65 us
    ppermute x7, waiting for transfers between devices, exchange(): return lax.ppermute(value, AXES, pairs)  2.84 us
    pallas_call x6, Pallas kernels, call(): pl.pallas_call(kernel, out_shape=[pltpu.VMEM(shape, dtype) for shape, dty...  2.15 us
    pallas_call x1, Pallas kernels, merged_device(): pl.pallas_call(partial(last_kernel, plan), out_shape=jax.ShapeDtypeStruct...  1.15 us
  transfers between devices with their start and end apart: 7, of which 3 were waited for; matrix products, arithmetic and copies ran while one was open for 0% of the time, Pallas kernels for 12%

profile of v3, /device:TPU:0, one launch (start us, length us, event | category | flops | bytes accessed | tf_op | source)
XLA Modules:
  0.0 15.5 jit_solution(18411924689020950766)
XLA Ops:
  0.0 0.0 copy-start.1
  0.0 0.0 copy-start
  0.0 0.0 copy-start.3
  0.0 0.0 copy-start.2
  0.0 0.0 copy-start.4
  0.0 0.5 %collective-permute-start = (f32[2,128,128]{2,1,0:T(8,128)}, f32[2,128,128]{2,1,0:T(8,128)S(1)}, u32[]{:S(2)}, u32[]{:S(2)}) collective-permute-start(f32[2,128,128]{2,1,0:T(8,128)} %bitcast.9), channel_id=1, source_target_pairs={{0,2},{1,3},{2,0},{3,1},{4,6},{5,7},{6,4},{7,5},{8,10},{9,11},{10,... | collective-permute-start | bytes 393224 | tf_op jit(solution)/shard_map/ppermute | solution.py:295
  1.2 0.0 copy-start.5
  1.2 0.2 %collective-permute-start.1 = (f32[8,128]{1,0:T(8,128)S(1)}, f32[8,128]{1,0:T(8,128)S(1)}, u32[]{:S(2)}, u32[]{:S(2)}) collective-permute-start(f32[8,128]{1,0:T(8,128)S(1)} %shard_map.73.factors), channel_id=1, source_target_pairs={{0,2},{1,3},{2,0},{3,1},{4,6},{5,7},{6,4},{7,5},{8,10},{9,11},{10,... | collective-permute-start | bytes 12296 | tf_op jit(solution)/shard_map/ppermute | solution.py:295
  1.4 0.0 copy-done.1
  1.4 0.0 copy-done
  1.4 0.0 copy-done.3
  1.4 0.0 copy-done.2
  1.4 0.0 copy-done.4
  1.5 0.7 %shard_map.74 = (f32[128,256]{1,0:T(8,128)S(1)}, bf16[128,256]{1,0:T(8,128)(2,1)S(1)}, bf16[128,256]{1,0:T(8,128)(2,1)S(1)}) custom-call(f32[2,128,128]{2,1,0:T(8,128)S(1)} %bitcast.10, f32[8,128]{1,0:T(8,128)S(1)} %shard_map.73.factors, f32[20,128,128]{2,1,0:T(8,128)S(1)} %bitcast.7, f32[1,128]{1,0:T(1,128)S(1)} %bitcast.13, s32[1,2]{1,0:T(1,128)S(1)} %bitcast.11, ...), custom_call_target="tpu_custom_call" | custom-call | bytes 131072 | tf_op jit(solution)/shard_map/pallas_call | solution.py:277
  2.1 0.3 %collective-permute-done.1.factors = f32[8,128]{1,0:T(8,128)S(1)} collective-permute-done((f32[8,128]{1,0:T(8,128)S(1)}, f32[8,128]{1,0:T(8,128)S(1)}, u32[]{:S(2)}, u32[]{:S(2)}) %collective-permute-start.1) | collective-permute-done | bytes 4128 | tf_op jit(solution)/shard_map/ppermute | solution.py:295
  2.5 0.0 collective-permute-done.state
  2.5 0.2 %shard_map.75 = (f32[16,256]{1,0:T(8,128)S(1)}, f32[32,256]{1,0:T(8,128)S(1)}, f32[16,256]{1,0:T(8,128)S(1)}, f32[32,256]{1,0:T(8,128)S(1)}, f32[32,256]{1,0:T(8,128)S(1)}) custom-call(f32[128,256]{1,0:T(8,128)S(1)} %get-tuple-element.19.own, bf16[128,256]{1,0:T(8,128)(2,1)S(1)} %get-tuple-element.20.high, bf16[128,256]{1,0:T(8,128)(2,1)S(1)} %get-tuple-element.21.low, ...), custom_call_target="tpu_custom_call" | custom-call | bytes 131072 | tf_op jit(solution)/shard_map/pallas_call | solution.py:277
  2.7 4.8 %collective-permute-start.2 = (f32[32,256]{1,0:T(8,128)S(1)}, f32[32,256]{1,0:T(8,128)S(1)}, u32[]{:S(2)}, u32[]{:S(2)}) collective-permute-start(f32[32,256]{1,0:T(8,128)S(1)} %get-tuple-element.23), channel_id=1, source_target_pairs={{0,24},{1,25},{2,27},{3,26},{4,28},{5,29},{6,31},{7,30},{8,16},{9,... | collective-permute-start | bytes 98312 | tf_op jit(solution)/shard_map/ppermute | solution.py:295
  7.5 0.0 collective-permute-start.4
  7.5 0.6 %collective-permute-start.5 = (f32[32,256]{1,0:T(8,128)S(1)}, f32[32,256]{1,0:T(8,128)S(1)}, u32[]{:S(2)}, u32[]{:S(2)}) collective-permute-start(f32[32,256]{1,0:T(8,128)S(1)} %get-tuple-element.26), channel_id=1, source_target_pairs={{0,8},{1,9},{2,11},{3,10},{4,12},{5,13},{6,15},{7,14},{8,0},{9,1},... | collective-permute-start | bytes 98312 | tf_op jit(solution)/shard_map/ppermute | solution.py:295
  8.2 1.6 %collective-permute-start.3 = (f32[16,256]{1,0:T(8,128)S(1)}, f32[16,256]{1,0:T(8,128)S(1)}, u32[]{:S(2)}, u32[]{:S(2)}) collective-permute-start(f32[16,256]{1,0:T(8,128)S(1)} %get-tuple-element.24), channel_id=1, source_target_pairs={{0,1},{1,0},{2,3},{3,2},{4,5},{5,4},{6,7},{7,6},{8,9},{9,8},{10,11... | collective-permute-start | bytes 49160 | tf_op jit(solution)/shard_map/ppermute | solution.py:295
  9.8 0.0 copy-done.5
  9.8 1.0 %shard_map.76 = (bf16[256,256]{1,0:T(8,128)(2,1)S(1)}, bf16[256,256]{1,0:T(8,128)(2,1)S(1)}, bf16[128,256]{1,0:T(8,128)(2,1)S(1)}, bf16[128,256]{1,0:T(8,128)(2,1)S(1)}) custom-call(f32[20,128,128]{2,1,0:T(8,128)S(1)} %bitcast.8, f32[1,128]{1,0:T(1,128)S(1)} %bitcast.15, s32[1,2]{1,0:T(1,128)S(1)} %bitcast.12, f32[16,256]{1,0:T(8,128)S(1)} %get-tuple-element.22.kept.refs_0_), custom_call_target="tpu_custom_call" | custom-call | bytes 131072 | tf_op jit(solution)/shard_map/pallas_call | solution.py:277
  10.8 0.0 collective-permute-done.2.refs_1_.refs_0_
  10.8 1.8 %collective-permute-done.4.refs_3_.refs_1_ = f32[32,256]{1,0:T(8,128)S(1)} collective-permute-done((f32[32,256]{1,0:T(8,128)S(1)}, f32[32,256]{1,0:T(8,128)S(1)}, u32[]{:S(2)}, u32[]{:S(2)}) %collective-permute-start.4) | collective-permute-done | bytes 32800 | tf_op jit(solution)/shard_map/ppermute | solution.py:295
  12.7 0.0 collective-permute-done.5.refs_4_.refs_2_
  12.7 0.8 %collective-permute-start.6 = (f32[48,256]{1,0:T(8,128)S(1)}, f32[48,256]{1,0:T(8,128)S(1)}, u32[]{:S(2)}, u32[]{:S(2)}) collective-permute-start(f32[48,256]{1,0:T(8,128)S(1)} %shard_map.78), channel_id=1, source_target_pairs={{0,2},{1,3},{2,0},{3,1},{4,6},{5,7},{6,4},{7,5},{8,10},{9,11},{10,... | collective-permute-start | bytes 147464 | tf_op jit(solution)/shard_map/ppermute | solution.py:295
  13.5 0.0 collective-permute-done.3.refs_2_
  13.5 0.2 %shard_map.77 = (bf16[80,256]{1,0:T(8,128)(2,1)S(1)}, bf16[80,256]{1,0:T(8,128)(2,1)S(1)}) custom-call(f32[16,256]{1,0:T(8,128)S(1)} %get-tuple-element.22.kept.refs_0_, f32[32,256]{1,0:T(8,128)S(1)} %collective-permute-done.2.refs_1_.refs_0_, f32[16,256]{1,0:T(8,128)S(1)} %collective-permute-done.3.refs_2_, ...), custom_call_target="tpu_custom_call" | custom-call | flops 4294967296 | bytes 131072 | tf_op jit(solution)/shard_map/pallas_call | solution.py:277
  13.7 0.6 %collective-permute-done.6.given = f32[48,256]{1,0:T(8,128)S(1)} collective-permute-done((f32[48,256]{1,0:T(8,128)S(1)}, f32[48,256]{1,0:T(8,128)S(1)}, u32[]{:S(2)}, u32[]{:S(2)}) %collective-permute-start.6) | collective-permute-done | bytes 49184 | tf_op jit(solution)/shard_map/ppermute | solution.py:295
  14.4 1.2 %shard_map.79 = f32[2,128,128]{2,1,0:T(8,128)} custom-call(bf16[80,256]{1,0:T(8,128)(2,1)S(1)} %get-tuple-element.29.high, bf16[80,256]{1,0:T(8,128)(2,1)S(1)} %get-tuple-element.30.low, f32[48,256]{1,0:T(8,128)S(1)} %collective-permute-done.6.given, bf16[256,256]{1,0:T(8,128)(2,1)S(1)} %get-tuple-element.27.refs_5_.right_high, ...), custom_call_target="tpu_custom_call" | custom-call | tf_op jit(solution)/shard_map/pallas_call | solution.py:347
  (2 shorter events, 0.0 us)
Async XLA Ops:
  0.0 1.4 %copy-start.1 = (f32[2,1,1,1,16384]{4,3,2,1,0:T(1,128)S(1)}, f32[2,1,1,1,16384]{4,3,2,1,0:T(1,128)}, u32[]{:S(2)}) copy-start(f32[2,1,1,1,16384]{4,3,2,1,0:T(1,128)} %param.7) | copy-start | bytes 393220
  0.0 1.4 %copy-start = (f32[10,2,128,128]{3,2,1,0:T(8,128)S(1)}, f32[10,2,128,128]{3,2,1,0:T(8,128)}, u32[]{:S(2)}) copy-start(f32[10,2,128,128]{3,2,1,0:T(8,128)} %param.8) | copy-start | bytes 3932164
  0.0 1.4 %copy-start.3 = (f32[128]{0:T(128)S(1)}, f32[128]{0:T(128)}, u32[]{:S(2)}) copy-start(f32[128]{0:T(128)} %param.10) | copy-start | bytes 1540
  0.0 1.4 %copy-start.2 = (s32[2]{0:T(128)S(1)}, s32[2]{0:T(128)}, u32[]{:S(2)}) copy-start(s32[2]{0:T(128)} %param.12) | copy-start | bytes 28
  0.0 1.4 %copy-start.4 = (s32[4]{0:T(128)S(1)}, s32[4]{0:T(128)}, u32[]{:S(2)}) copy-start(s32[4]{0:T(128)} %param.13) | copy-start | bytes 52
  0.0 2.4 %collective-permute-start = (f32[2,128,128]{2,1,0:T(8,128)}, f32[2,128,128]{2,1,0:T(8,128)S(1)}, u32[]{:S(2)}, u32[]{:S(2)}) collective-permute-start(f32[2,128,128]{2,1,0:T(8,128)} %bitcast.9), channel_id=1, source_target_pairs={{0,2},{1,3},{2,0},{3,1},{4,6},{5,7},{6,4},{7,5},{8,10},{9,11},{10,... | collective-permute-start | bytes 393224 | tf_op jit(solution)/shard_map/ppermute | solution.py:295
  1.2 8.6 %copy-start.5 = (f32[128]{0:T(128)S(1)}, f32[128]{0:T(128)}, u32[]{:S(2)}) copy-start(f32[128]{0:T(128)} %param.9) | copy-start | bytes 1540
  1.2 1.2 %collective-permute-start.1 = (f32[8,128]{1,0:T(8,128)S(1)}, f32[8,128]{1,0:T(8,128)S(1)}, u32[]{:S(2)}, u32[]{:S(2)}) collective-permute-start(f32[8,128]{1,0:T(8,128)S(1)} %shard_map.73.factors), channel_id=1, source_target_pairs={{0,2},{1,3},{2,0},{3,1},{4,6},{5,7},{6,4},{7,5},{8,10},{9,11},{10,... | collective-permute-start | bytes 12296 | tf_op jit(solution)/shard_map/ppermute | solution.py:295
  2.7 8.1 %collective-permute-start.2 = (f32[32,256]{1,0:T(8,128)S(1)}, f32[32,256]{1,0:T(8,128)S(1)}, u32[]{:S(2)}, u32[]{:S(2)}) collective-permute-start(f32[32,256]{1,0:T(8,128)S(1)} %get-tuple-element.23), channel_id=1, source_target_pairs={{0,24},{1,25},{2,27},{3,26},{4,28},{5,29},{6,31},{7,30},{8,16},{9,... | collective-permute-start | bytes 98312 | tf_op jit(solution)/shard_map/ppermute | solution.py:295
  7.5 5.2 %collective-permute-start.4 = (f32[32,256]{1,0:T(8,128)S(1)}, f32[32,256]{1,0:T(8,128)S(1)}, u32[]{:S(2)}, u32[]{:S(2)}) collective-permute-start(f32[32,256]{1,0:T(8,128)S(1)} %get-tuple-element.25), channel_id=1, source_target_pairs={{0,16},{1,17},{2,19},{3,18},{4,20},{5,21},{6,23},{7,22},{8,24},{9,... | collective-permute-start | bytes 98312 | tf_op jit(solution)/shard_map/ppermute | solution.py:295
  7.5 5.2 %collective-permute-start.5 = (f32[32,256]{1,0:T(8,128)S(1)}, f32[32,256]{1,0:T(8,128)S(1)}, u32[]{:S(2)}, u32[]{:S(2)}) collective-permute-start(f32[32,256]{1,0:T(8,128)S(1)} %get-tuple-element.26), channel_id=1, source_target_pairs={{0,8},{1,9},{2,11},{3,10},{4,12},{5,13},{6,15},{7,14},{8,0},{9,1},... | collective-permute-start | bytes 98312 | tf_op jit(solution)/shard_map/ppermute | solution.py:295
  8.2 5.3 %collective-permute-start.3 = (f32[16,256]{1,0:T(8,128)S(1)}, f32[16,256]{1,0:T(8,128)S(1)}, u32[]{:S(2)}, u32[]{:S(2)}) collective-permute-start(f32[16,256]{1,0:T(8,128)S(1)} %get-tuple-element.24), channel_id=1, source_target_pairs={{0,1},{1,0},{2,3},{3,2},{4,5},{5,4},{6,7},{7,6},{8,9},{9,8},{10,11... | collective-permute-start | bytes 49160 | tf_op jit(solution)/shard_map/ppermute | solution.py:295
  12.7 1.7 %collective-permute-start.6 = (f32[48,256]{1,0:T(8,128)S(1)}, f32[48,256]{1,0:T(8,128)S(1)}, u32[]{:S(2)}, u32[]{:S(2)}) collective-permute-start(f32[48,256]{1,0:T(8,128)S(1)} %shard_map.78), channel_id=1, source_target_pairs={{0,2},{1,3},{2,0},{3,1},{4,6},{5,7},{6,4},{7,5},{8,10},{9,11},{10,... | collective-permute-start | bytes 147464 | tf_op jit(solution)/shard_map/ppermute | solution.py:295

commit v4 on v3

--- a/solution.py
+++ b/solution.py
@@ -103,13 +103,19 @@
         self.wide_bits = wide_count.bit_length() - 1
         self.low_base = self.row_bits - self.wide_bits - 3
         self.chunk = rows // (2 * wide_count)
-        self.steps = [((wide, 0), (wide, 1)) for wide in range(wide_count - 1, 0, -1)]
-        self.steps.insert(1, ((0, 1), (0, 1)))
-        self.shared = [step for step in self.steps if step[0] != step[1]]
-
-
-def by_core(step, core):
-    return tuple(a if a == b else a ^ (core * (a ^ b)) for a, b in zip(*step))
+        half = wide_count // 2
+        tops = [tuple(range(k, min(k + 2, wide_count))) for k in range(half, wide_count, 2)]
+        self.steps = [((pair[0], pair[-1]), (0, 1)) for pair in tops]
+        self.steps += [((pair[1], pair[0]), (0, 1)) for pair in tops if len(pair) == 2]
+        near = range(half - 1, 0, -1)
+        self.steps += [((offset, offset), (1, 1)) for offset in near]
+        self.steps.append(((0, 0), (1, 1)))
+        self.steps += [((offset, offset), (0, 0)) for offset in near]
+        self.shared = [step for step in self.steps if step[1][0] != step[1][1]]
+
+
+def choose(flag, pair):
+    return pair[0] if pair[0] == pair[1] else pair[0] ^ (flag * (pair[0] ^ pair[1]))
 
 
 def free_row(plan, inner, swap):
@@ -130,10 +136,11 @@
 def sent_rows(plan, swaps, order):
     wide, core, low = lax.axis_index("wide"), lax.axis_index("mid") & 1, lax.axis_index("low") & 1
     targets = [(wide, low, core)]
+    half = wide >> (plan.wide_bits - 1)
     for step in plan.steps:
-        wide_part, low_part = by_core(step, core)
+        to_wide, to_low = wide ^ choose(half, step[0]), low ^ choose(core, step[1])
         for to_core in (core, 1 - core)[: 2 if step in plan.shared else 1]:
-            targets.append((wide ^ wide_part, low ^ low_part, to_core))
+            targets.append((to_wide, to_low, to_core))
     base = plan.row_bits - 4
     position = plan.row_bits - 3 + swaps[0]
     places = [base + order[place] for place in range(4)]
@@ -157,9 +164,11 @@
 
 def received_rows(plan, swaps):
     wide, core, low = lax.axis_index("wide"), lax.axis_index("mid") & 1, lax.axis_index("low") & 1
-    parts = [by_core(step, core) for step in plan.steps]
-    parts += [by_core(step, 1 - core) for step in plan.shared]
-    sources = [(wide, low)] + [(wide ^ part[0], low ^ part[1]) for part in parts]
+    half = wide >> (plan.wide_bits - 1)
+    sources = [(wide, low)]
+    for server, steps in ((core, plan.steps), (1 - core, plan.shared)):
+        for step in steps:
+            sources.append((wide ^ choose(1 - half, step[0]), low ^ choose(server, step[1])))
     inner = lax.broadcasted_iota(jnp.int32, (plan.chunk, plan.rows), 0)
     inner = free_row(plan, inner, swaps[1])
     result = []
@@ -289,8 +298,8 @@
     for wide in range(wides):
         for mid in range(mids):
             for low in range(lows):
-                wide_part, low_part = step[mid & 1]
-                to = ((wide ^ wide_part) * mids + (mid ^ flip)) * lows + (low ^ low_part)
+                to_wide = wide ^ step[0][2 * wide // wides]
+                to = (to_wide * mids + (mid ^ flip)) * lows + (low ^ step[1][mid & 1])
                 pairs.append(((wide * mids + mid) * lows + low, to))
     return lax.ppermute(value, AXES, pairs)
 
@@ -469,8 +478,9 @@
 
 def on_device(state, gates, *rest):
     rows = gates.shape[-1]
-    plan_base = rows.bit_length() - 1 - (lax.axis_size("wide").bit_length() - 1) - 3
-    merged = state.shape[-1] == rows * rows and plan_base >= 1 and gates.shape[0] >= 8
+    sizes = [lax.axis_size(axis) for axis in AXES]
+    base = rows.bit_length() - sizes[0].bit_length() - 3
+    merged = state.shape[-1] == rows * rows and base >= 2 and min(sizes) >= 2
     return (merged_device if merged else general_device)(state, gates, *rest)
 
 

time: 15.7 us -> 14.8 us (0.943)
  waiting for transfers between devices: 2.84 us -> 1.1 us
  starting transfers between devices: 8.65 us -> 9.52 us
    ppermute x7 -> x8, waiting for transfers between devices: 2.84 us -> 1.1 us  [exchange(): return lax.ppermute(value, AXES, pairs)]
    ppermute x7 -> x8, starting transfers between devices: 8.65 us -> 9.52 us  [exchange(): return lax.ppermute(value, AXES, pairs)]
  transfers between devices with their start and end apart: 7 -> 8, of which waited for: 3 -> 4; matrix products, arithmetic and copies ran while one was open for 0% -> 0% of each run, Pallas kernels for 12% -> 13%
where the time goes in v4:
time: 14.8 us; the launch traced here: 14.7 us
  starting transfers between devices  9.52 us (64%)
  Pallas kernels  3.31 us (22%)
  waiting for transfers between devices  1.1 us (7%)
  between operations  0.75 us (5%)
    ppermute x8, starting transfers between devices, exchange(): return lax.ppermute(value, AXES, pairs)  9.52 us
    pallas_call x6, Pallas kernels, call(): pl.pallas_call(kernel, out_shape=[pltpu.VMEM(shape, dtype) for shape, dty...  2.16 us
    pallas_call x1, Pallas kernels, merged_device(): pl.pallas_call(partial(last_kernel, plan), out_shape=jax.ShapeDtypeStruct...  1.15 us
    ppermute x8, waiting for transfers between devices, exchange(): return lax.ppermute(value, AXES, pairs)  1.1 us
  transfers between devices with their start and end apart: 8, of which 4 were waited for; matrix products, arithmetic and copies ran while one was open for 0% of the time, Pallas kernels for 13%

profile of v4, /device:TPU:0, one launch (start us, length us, event | category | flops | bytes accessed | tf_op | source)
XLA Modules:
  0.0 14.7 jit_solution(2489446948270091788)
XLA Ops:
  0.0 0.0 copy-start.1
  0.0 0.0 copy-start
  0.0 0.0 copy-start.3
  0.0 0.0 copy-start.2
  0.0 0.0 copy-start.4
  0.0 0.5 %collective-permute-start = (f32[2,128,128]{2,1,0:T(8,128)}, f32[2,128,128]{2,1,0:T(8,128)S(1)}, u32[]{:S(2)}, u32[]{:S(2)}) collective-permute-start(f32[2,128,128]{2,1,0:T(8,128)} %bitcast.9), channel_id=1, source_target_pairs={{0,2},{1,3},{2,0},{3,1},{4,6},{5,7},{6,4},{7,5},{8,10},{9,11},{10,... | collective-permute-start | bytes 393224 | tf_op jit(solution)/shard_map/ppermute | solution.py:304
  1.2 0.0 copy-start.5
  1.2 0.2 %collective-permute-start.1 = (f32[8,128]{1,0:T(8,128)S(1)}, f32[8,128]{1,0:T(8,128)S(1)}, u32[]{:S(2)}, u32[]{:S(2)}) collective-permute-start(f32[8,128]{1,0:T(8,128)S(1)} %shard_map.73.factors), channel_id=1, source_target_pairs={{0,2},{1,3},{2,0},{3,1},{4,6},{5,7},{6,4},{7,5},{8,10},{9,11},{10,... | collective-permute-start | bytes 12296 | tf_op jit(solution)/shard_map/ppermute | solution.py:304
  1.4 0.0 copy-done.1
  1.4 0.0 copy-done
  1.4 0.0 copy-done.3
  1.4 0.0 copy-done.2
  1.4 0.0 copy-done.4
  1.5 0.7 %shard_map.74 = (f32[128,256]{1,0:T(8,128)S(1)}, bf16[128,256]{1,0:T(8,128)(2,1)S(1)}, bf16[128,256]{1,0:T(8,128)(2,1)S(1)}) custom-call(f32[2,128,128]{2,1,0:T(8,128)S(1)} %bitcast.10, f32[8,128]{1,0:T(8,128)S(1)} %shard_map.73.factors, f32[20,128,128]{2,1,0:T(8,128)S(1)} %bitcast.7, f32[1,128]{1,0:T(1,128)S(1)} %bitcast.13, s32[1,2]{1,0:T(1,128)S(1)} %bitcast.11, ...), custom_call_target="tpu_custom_call" | custom-call | bytes 131072 | tf_op jit(solution)/shard_map/pallas_call | solution.py:286
  2.1 0.3 %collective-permute-done.1.factors = f32[8,128]{1,0:T(8,128)S(1)} collective-permute-done((f32[8,128]{1,0:T(8,128)S(1)}, f32[8,128]{1,0:T(8,128)S(1)}, u32[]{:S(2)}, u32[]{:S(2)}) %collective-permute-start.1) | collective-permute-done | bytes 4128 | tf_op jit(solution)/shard_map/ppermute | solution.py:304
  2.5 0.0 collective-permute-done.state
  2.5 0.2 %shard_map.75 = (f32[16,256]{1,0:T(8,128)S(1)}, f32[32,256]{1,0:T(8,128)S(1)}, f32[32,256]{1,0:T(8,128)S(1)}, f32[16,256]{1,0:T(8,128)S(1)}, f32[16,256]{1,0:T(8,128)S(1)}, /*index=5*/f32[16,256]{1,0:T(8,128)S(1)}) custom-call(f32[128,256]{1,0:T(8,128)S(1)} %get-tuple-element.20.own, bf16[128,256]{1,0:T(8,128)(2,1)S(1)} %get-tuple-element.21.high, ...), custom_call_target="tpu_custom_call" | custom-call | bytes 131072 | tf_op jit(solution)/shard_map/pallas_call | solution.py:286
  2.7 3.8 %collective-permute-start.2 = (f32[32,256]{1,0:T(8,128)S(1)}, f32[32,256]{1,0:T(8,128)S(1)}, u32[]{:S(2)}, u32[]{:S(2)}) collective-permute-start(f32[32,256]{1,0:T(8,128)S(1)} %get-tuple-element.24), channel_id=1, source_target_pairs={{0,16},{1,17},{2,19},{3,18},{4,20},{5,21},{6,23},{7,22},{8,24},{9,... | collective-permute-start | bytes 98312 | tf_op jit(solution)/shard_map/ppermute | solution.py:304
  6.5 1.1 %collective-permute-start.3 = (f32[32,256]{1,0:T(8,128)S(1)}, f32[32,256]{1,0:T(8,128)S(1)}, u32[]{:S(2)}, u32[]{:S(2)}) collective-permute-start(f32[32,256]{1,0:T(8,128)S(1)} %get-tuple-element.25), channel_id=1, source_target_pairs={{0,24},{1,25},{2,27},{3,26},{4,28},{5,29},{6,31},{7,30},{8,16},{9,... | collective-permute-start | bytes 98312 | tf_op jit(solution)/shard_map/ppermute | solution.py:304
  7.6 1.4 %collective-permute-start.4 = (f32[16,256]{1,0:T(8,128)S(1)}, f32[16,256]{1,0:T(8,128)S(1)}, u32[]{:S(2)}, u32[]{:S(2)}) collective-permute-start(f32[16,256]{1,0:T(8,128)S(1)} %get-tuple-element.26), channel_id=1, source_target_pairs={{0,9},{1,8},{2,11},{3,10},{4,13},{5,12},{6,15},{7,14},{8,1},{9,0},... | collective-permute-start | bytes 49160 | tf_op jit(solution)/shard_map/ppermute | solution.py:304
  9.0 0.5 %collective-permute-start.5 = (f32[16,256]{1,0:T(8,128)S(1)}, f32[16,256]{1,0:T(8,128)S(1)}, u32[]{:S(2)}, u32[]{:S(2)}) collective-permute-start(f32[16,256]{1,0:T(8,128)S(1)} %get-tuple-element.27), channel_id=1, source_target_pairs={{0,1},{1,0},{2,3},{3,2},{4,5},{5,4},{6,7},{7,6},{8,9},{9,8},{10,11... | collective-permute-start | bytes 49160 | tf_op jit(solution)/shard_map/ppermute | solution.py:304
  9.5 1.5 %collective-permute-start.6 = (f32[16,256]{1,0:T(8,128)S(1)}, f32[16,256]{1,0:T(8,128)S(1)}, u32[]{:S(2)}, u32[]{:S(2)}) collective-permute-start(f32[16,256]{1,0:T(8,128)S(1)} %get-tuple-element.28), channel_id=1, source_target_pairs={{0,8},{1,9},{2,10},{3,11},{4,12},{5,13},{6,14},{7,15},{8,0},{9,1},... | collective-permute-start | bytes 49160 | tf_op jit(solution)/shard_map/ppermute | solution.py:304
  11.1 0.0 copy-done.5
  11.1 1.0 %shard_map.76 = (bf16[256,256]{1,0:T(8,128)(2,1)S(1)}, bf16[256,256]{1,0:T(8,128)(2,1)S(1)}, bf16[128,256]{1,0:T(8,128)(2,1)S(1)}, bf16[128,256]{1,0:T(8,128)(2,1)S(1)}) custom-call(f32[20,128,128]{2,1,0:T(8,128)S(1)} %bitcast.8, f32[1,128]{1,0:T(1,128)S(1)} %bitcast.15, s32[1,2]{1,0:T(1,128)S(1)} %bitcast.12, f32[16,256]{1,0:T(8,128)S(1)} %get-tuple-element.23.kept.refs_0_), custom_call_target="tpu_custom_call" | custom-call | bytes 131072 | tf_op jit(solution)/shard_map/pallas_call | solution.py:286
  12.1 0.0 collective-permute-done.2.refs_1_.refs_0_
  12.1 0.0 collective-permute-done.3.refs_2_.refs_1_
  12.1 0.4 %collective-permute-start.7 = (f32[32,256]{1,0:T(8,128)S(1)}, f32[32,256]{1,0:T(8,128)S(1)}, u32[]{:S(2)}, u32[]{:S(2)}) collective-permute-start(f32[32,256]{1,0:T(8,128)S(1)} %shard_map.78), channel_id=1, source_target_pairs={{0,2},{1,3},{2,0},{3,1},{4,6},{5,7},{6,4},{7,5},{8,10},{9,11},{10,... | collective-permute-start | bytes 98312 | tf_op jit(solution)/shard_map/ppermute | solution.py:304
  12.5 0.5 %collective-permute-done.4.refs_3_ = f32[16,256]{1,0:T(8,128)S(1)} collective-permute-done((f32[16,256]{1,0:T(8,128)S(1)}, f32[16,256]{1,0:T(8,128)S(1)}, u32[]{:S(2)}, u32[]{:S(2)}) %collective-permute-start.4) | collective-permute-done | bytes 16416 | tf_op jit(solution)/shard_map/ppermute | solution.py:304
  13.0 0.1 collective-permute-done.5.refs_4_
  13.1 0.2 %collective-permute-done.6.refs_5_ = f32[16,256]{1,0:T(8,128)S(1)} collective-permute-done((f32[16,256]{1,0:T(8,128)S(1)}, f32[16,256]{1,0:T(8,128)S(1)}, u32[]{:S(2)}, u32[]{:S(2)}) %collective-permute-start.6) | collective-permute-done | bytes 16416 | tf_op jit(solution)/shard_map/ppermute | solution.py:304
  13.3 0.2 %shard_map.77 = (bf16[96,256]{1,0:T(8,128)(2,1)S(1)}, bf16[96,256]{1,0:T(8,128)(2,1)S(1)}) custom-call(f32[16,256]{1,0:T(8,128)S(1)} %get-tuple-element.23.kept.refs_0_, f32[32,256]{1,0:T(8,128)S(1)} %collective-permute-done.2.refs_1_.refs_0_, f32[32,256]{1,0:T(8,128)S(1)} %collective-permute-done.3.refs_2_.refs_1_, ...), custom_call_target="tpu_custom_call" | custom-call | flops 4294967296 | bytes 131072 | tf_op jit(solution)/shard_map/pallas_call | solution.py:286
  13.5 0.0 collective-permute-done.7.given
  13.5 1.2 %shard_map.79 = f32[2,128,128]{2,1,0:T(8,128)} custom-call(bf16[96,256]{1,0:T(8,128)(2,1)S(1)} %get-tuple-element.31.high, bf16[96,256]{1,0:T(8,128)(2,1)S(1)} %get-tuple-element.32.low, f32[32,256]{1,0:T(8,128)S(1)} %collective-permute-done.7.given, bf16[256,256]{1,0:T(8,128)(2,1)S(1)} %get-tuple-element.29.refs_6_.right_high, ...), custom_call_target="tpu_custom_call" | custom-call | tf_op jit(solution)/shard_map/pallas_call | solution.py:356
  (2 shorter events, 0.0 us)
Async XLA Ops:
  0.0 1.4 %copy-start.1 = (f32[2,1,1,1,16384]{4,3,2,1,0:T(1,128)S(1)}, f32[2,1,1,1,16384]{4,3,2,1,0:T(1,128)}, u32[]{:S(2)}) copy-start(f32[2,1,1,1,16384]{4,3,2,1,0:T(1,128)} %param.7) | copy-start | bytes 393220
  0.0 1.4 %copy-start = (f32[10,2,128,128]{3,2,1,0:T(8,128)S(1)}, f32[10,2,128,128]{3,2,1,0:T(8,128)}, u32[]{:S(2)}) copy-start(f32[10,2,128,128]{3,2,1,0:T(8,128)} %param.8) | copy-start | bytes 3932164
  0.0 1.4 %copy-start.3 = (f32[128]{0:T(128)S(1)}, f32[128]{0:T(128)}, u32[]{:S(2)}) copy-start(f32[128]{0:T(128)} %param.10) | copy-start | bytes 1540
  0.0 1.4 %copy-start.2 = (s32[2]{0:T(128)S(1)}, s32[2]{0:T(128)}, u32[]{:S(2)}) copy-start(s32[2]{0:T(128)} %param.12) | copy-start | bytes 28
  0.0 1.4 %copy-start.4 = (s32[4]{0:T(128)S(1)}, s32[4]{0:T(128)}, u32[]{:S(2)}) copy-start(s32[4]{0:T(128)} %param.13) | copy-start | bytes 52
  0.0 2.4 %collective-permute-start = (f32[2,128,128]{2,1,0:T(8,128)}, f32[2,128,128]{2,1,0:T(8,128)S(1)}, u32[]{:S(2)}, u32[]{:S(2)}) collective-permute-start(f32[2,128,128]{2,1,0:T(8,128)} %bitcast.9), channel_id=1, source_target_pairs={{0,2},{1,3},{2,0},{3,1},{4,6},{5,7},{6,4},{7,5},{8,10},{9,11},{10,... | collective-permute-start | bytes 393224 | tf_op jit(solution)/shard_map/ppermute | solution.py:304
  1.2 9.9 %copy-start.5 = (f32[128]{0:T(128)S(1)}, f32[128]{0:T(128)}, u32[]{:S(2)}) copy-start(f32[128]{0:T(128)} %param.9) | copy-start | bytes 1540
  1.2 1.2 %collective-permute-start.1 = (f32[8,128]{1,0:T(8,128)S(1)}, f32[8,128]{1,0:T(8,128)S(1)}, u32[]{:S(2)}, u32[]{:S(2)}) collective-permute-start(f32[8,128]{1,0:T(8,128)S(1)} %shard_map.73.factors), channel_id=1, source_target_pairs={{0,2},{1,3},{2,0},{3,1},{4,6},{5,7},{6,4},{7,5},{8,10},{9,11},{10,... | collective-permute-start | bytes 12296 | tf_op jit(solution)/shard_map/ppermute | solution.py:304
  2.7 9.4 %collective-permute-start.2 = (f32[32,256]{1,0:T(8,128)S(1)}, f32[32,256]{1,0:T(8,128)S(1)}, u32[]{:S(2)}, u32[]{:S(2)}) collective-permute-start(f32[32,256]{1,0:T(8,128)S(1)} %get-tuple-element.24), channel_id=1, source_target_pairs={{0,16},{1,17},{2,19},{3,18},{4,20},{5,21},{6,23},{7,22},{8,24},{9,... | collective-permute-start | bytes 98312 | tf_op jit(solution)/shard_map/ppermute | solution.py:304
  6.5 5.6 %collective-permute-start.3 = (f32[32,256]{1,0:T(8,128)S(1)}, f32[32,256]{1,0:T(8,128)S(1)}, u32[]{:S(2)}, u32[]{:S(2)}) collective-permute-start(f32[32,256]{1,0:T(8,128)S(1)} %get-tuple-element.25), channel_id=1, source_target_pairs={{0,24},{1,25},{2,27},{3,26},{4,28},{5,29},{6,31},{7,30},{8,16},{9,... | collective-permute-start | bytes 98312 | tf_op jit(solution)/shard_map/ppermute | solution.py:304
  7.6 5.4 %collective-permute-start.4 = (f32[16,256]{1,0:T(8,128)S(1)}, f32[16,256]{1,0:T(8,128)S(1)}, u32[]{:S(2)}, u32[]{:S(2)}) collective-permute-start(f32[16,256]{1,0:T(8,128)S(1)} %get-tuple-element.26), channel_id=1, source_target_pairs={{0,9},{1,8},{2,11},{3,10},{4,13},{5,12},{6,15},{7,14},{8,1},{9,0},... | collective-permute-start | bytes 49160 | tf_op jit(solution)/shard_map/ppermute | solution.py:304
  9.0 4.1 %collective-permute-start.5 = (f32[16,256]{1,0:T(8,128)S(1)}, f32[16,256]{1,0:T(8,128)S(1)}, u32[]{:S(2)}, u32[]{:S(2)}) collective-permute-start(f32[16,256]{1,0:T(8,128)S(1)} %get-tuple-element.27), channel_id=1, source_target_pairs={{0,1},{1,0},{2,3},{3,2},{4,5},{5,4},{6,7},{7,6},{8,9},{9,8},{10,11... | collective-permute-start | bytes 49160 | tf_op jit(solution)/shard_map/ppermute | solution.py:304
  9.5 3.7 %collective-permute-start.6 = (f32[16,256]{1,0:T(8,128)S(1)}, f32[16,256]{1,0:T(8,128)S(1)}, u32[]{:S(2)}, u32[]{:S(2)}) collective-permute-start(f32[16,256]{1,0:T(8,128)S(1)} %get-tuple-element.28), channel_id=1, source_target_pairs={{0,8},{1,9},{2,10},{3,11},{4,12},{5,13},{6,14},{7,15},{8,0},{9,1},... | collective-permute-start | bytes 49160 | tf_op jit(solution)/shard_map/ppermute | solution.py:304
  12.1 1.4 %collective-permute-start.7 = (f32[32,256]{1,0:T(8,128)S(1)}, f32[32,256]{1,0:T(8,128)S(1)}, u32[]{:S(2)}, u32[]{:S(2)}) collective-permute-start(f32[32,256]{1,0:T(8,128)S(1)} %shard_map.78), channel_id=1, source_target_pairs={{0,2},{1,3},{2,0},{3,1},{4,6},{5,7},{6,4},{7,5},{8,10},{9,11},{10,... | collective-permute-start | bytes 98312 | tf_op jit(solution)/shard_map/ppermute | solution.py:304

commit v5 on v4

--- a/solution.py
+++ b/solution.py
@@ -112,6 +112,7 @@
         self.steps.append(((0, 0), (1, 1)))
         self.steps += [((offset, offset), (0, 0)) for offset in near]
         self.shared = [step for step in self.steps if step[1][0] != step[1][1]]
+        self.direct = [step for step in self.steps if step[1][0] == step[1][1]]
 
 
 def choose(flag, pair):
@@ -166,7 +167,7 @@
     wide, core, low = lax.axis_index("wide"), lax.axis_index("mid") & 1, lax.axis_index("low") & 1
     half = wide >> (plan.wide_bits - 1)
     sources = [(wide, low)]
-    for server, steps in ((core, plan.steps), (1 - core, plan.shared)):
+    for server, steps in ((core, plan.shared), (core, plan.direct), (1 - core, plan.shared)):
         for step in steps:
             sources.append((wide ^ choose(1 - half, step[0]), low ^ choose(server, step[1])))
     inner = lax.broadcasted_iota(jnp.int32, (plan.chunk, plan.rows), 0)
@@ -256,21 +257,33 @@
     left_kernel(plan, count, gates, swaps, *factors[2:])
 
 
+def right_only(plan, count, gates, phase_low, kept, *out):
+    right_kernel(plan, count, gates, phase_low, *out)
+
+
+def left_only(plan, count, gates, swaps, kept, *out):
+    left_kernel(plan, count, gates, swaps, *out)
+
+
 def sort_kernel(plan, *refs):
     give = refs[-1]
     for place, ref in enumerate(refs[: len(plan.shared)]):
         give[place * plan.chunk : (place + 1) * plan.chunk] = ref[plan.chunk :]
 
 
-def kept_kernel(plan, *refs):
-    *parts, right_high, right_low, high, low = refs
+def kept_kernel(plan, count, gates, swaps, give, *refs):
+    del give
+    *parts, right_high, right_low, left_high, left_low, high, low = refs
+    left_kernel(plan, count, gates, swaps, left_high, left_low)
     value = jnp.concatenate([ref[: plan.chunk] for ref in parts], 0)
     value = product(split(value), (right_high[...], right_low[...]), True)
     high[...], low[...] = split(value)
 
 
-def last_kernel(plan, high, low, given, right_high, right_low, left_high, left_low, out):
-    value = split(product(split(given[...]), (right_high[...], right_low[...]), True))
+def last_kernel(plan, high, low, *refs):
+    *parts, right_high, right_low, left_high, left_low, out = refs
+    value = jnp.concatenate([ref[...] for ref in parts], 0)
+    value = split(product(split(value), (right_high[...], right_low[...]), True))
     value = tuple(jnp.concatenate([a[...], b], 0) for a, b in zip((high, low), value))
     result = complex_product((left_high[...], left_low[...]), value)
     half = plan.rows
@@ -330,29 +343,30 @@
         (VSPEC,) * 5,
     )
     received = [exchange(value, step) for value, step in zip(sent, plan.steps)]
-    right_high, right_low, left_high, left_low = call(
-        partial(back_kernel, plan, gates.shape[0] // 2),
-        [((2 * rows, 2 * rows), bf16)] * 2 + [((rows, 2 * rows), bf16)] * 2,
-        (gates, phase_low.reshape(1, rows), swaps, local),
-        (VSPEC,) * 4,
+    right_high, right_low = call(
+        partial(right_only, plan, gates.shape[0] // 2),
+        [((2 * rows, 2 * rows), bf16)] * 2,
+        (gates, phase_low.reshape(1, rows), local),
+        (VSPEC,) * 3,
     )
     shared = [value for value, step in zip(received, plan.steps) if step in plan.shared]
     (give,) = call(
         partial(sort_kernel, plan),
         [((len(plan.shared) * chunk, 2 * rows), f32)],
-        (*shared, left_low),
+        (*shared, right_low),
         (VSPEC,) * (len(shared) + 1),
     )
     given = exchange(give, flip=1)
-    kept_rows = (len(received) + 1) * chunk
-    high, low = call(
-        partial(kept_kernel, plan),
-        [((kept_rows, 2 * rows), bf16)] * 2,
-        (local, *received, right_high, right_low),
-        (VSPEC,) * (len(received) + 3),
+    kept_rows = (1 + len(shared)) * chunk
+    left_high, left_low, high, low = call(
+        partial(kept_kernel, plan, gates.shape[0] // 2),
+        [((rows, 2 * rows), bf16)] * 2 + [((kept_rows, 2 * rows), bf16)] * 2,
+        (gates, swaps, give, local, *shared, right_high, right_low),
+        (VSPEC,) * (len(shared) + 6),
         LONG,
     )
-    args = (high, low, given, right_high, right_low, left_high, left_low)
+    direct = [value for value, step in zip(received, plan.steps) if step in plan.direct]
+    args = (high, low, *direct, given, right_high, right_low, left_high, left_low)
     out = pl.pallas_call(
         partial(last_kernel, plan),
         out_shape=jax.ShapeDtypeStruct((2, rows, rows), f32),

time: 14.8 us -> 14.7 us (level)
  waiting for transfers between devices: 1.1 us -> 0.52 us
  starting transfers between devices: 9.52 us -> 9.86 us
    ppermute x8, waiting for transfers between devices: 1.1 us -> 0.52 us  [exchange(): return lax.ppermute(value, AXES, pairs)]
    ppermute x8, starting transfers between devices: 9.52 us -> 9.86 us  [exchange(): return lax.ppermute(value, AXES, pairs)]
  transfers between devices with their start and end apart: 8 -> 8, of which waited for: 4 -> 3; matrix products, arithmetic and copies ran while one was open for 0% -> 0% of each run, Pallas kernels for 13% -> 14%
where the time goes in v5:
time: 14.7 us; the launch traced here: 14.6 us
  starting transfers between devices  9.86 us (67%)
  Pallas kernels  3.39 us (23%)
  between operations  0.76 us (5%)
  waiting for transfers between devices  0.52 us (4%)
    ppermute x8, starting transfers between devices, exchange(): return lax.ppermute(value, AXES, pairs)  9.86 us
    pallas_call x6, Pallas kernels, call(): pl.pallas_call(kernel, out_shape=[pltpu.VMEM(shape, dtype) for shape, dty...  2.23 us
    pallas_call x1, Pallas kernels, merged_device(): pl.pallas_call(partial(last_kernel, plan), out_shape=jax.ShapeDtypeStruct...  1.16 us
    ppermute x8, waiting for transfers between devices, exchange(): return lax.ppermute(value, AXES, pairs)  0.52 us
  transfers between devices with their start and end apart: 8, of which 3 were waited for; matrix products, arithmetic and copies ran while one was open for 0% of the time, Pallas kernels for 14%

profile of v5, /device:TPU:0, one launch (start us, length us, event | category | flops | bytes accessed | tf_op | source)
XLA Modules:
  0.0 14.6 jit_solution(7106214058534742647)
XLA Ops:
  0.0 0.0 copy-start.1
  0.0 0.0 copy-start.4
  0.0 0.0 copy-start.5
  0.0 0.0 copy-start.3
  0.0 0.0 copy-start
  0.0 0.5 %collective-permute-start = (f32[2,128,128]{2,1,0:T(8,128)}, f32[2,128,128]{2,1,0:T(8,128)S(1)}, u32[]{:S(2)}, u32[]{:S(2)}) collective-permute-start(f32[2,128,128]{2,1,0:T(8,128)} %bitcast.10), channel_id=1, source_target_pairs={{0,2},{1,3},{2,0},{3,1},{4,6},{5,7},{6,4},{7,5},{8,10},{9,11},{10,... | collective-permute-start | bytes 393224 | tf_op jit(solution)/shard_map/ppermute | solution.py:317
  1.2 0.0 copy-start.2
  1.2 0.2 %collective-permute-start.1 = (f32[8,128]{1,0:T(8,128)S(1)}, f32[8,128]{1,0:T(8,128)S(1)}, u32[]{:S(2)}, u32[]{:S(2)}) collective-permute-start(f32[8,128]{1,0:T(8,128)S(1)} %shard_map.73.factors), channel_id=1, source_target_pairs={{0,2},{1,3},{2,0},{3,1},{4,6},{5,7},{6,4},{7,5},{8,10},{9,11},{10,... | collective-permute-start | bytes 12296 | tf_op jit(solution)/shard_map/ppermute | solution.py:317
  1.5 0.0 copy-done.1
  1.5 0.0 copy-done.4
  1.5 0.0 copy-done.5
  1.5 0.0 copy-done.3
  1.5 0.0 copy-done
  1.5 0.7 %shard_map.74 = (f32[128,256]{1,0:T(8,128)S(1)}, bf16[128,256]{1,0:T(8,128)(2,1)S(1)}, bf16[128,256]{1,0:T(8,128)(2,1)S(1)}) custom-call(f32[2,128,128]{2,1,0:T(8,128)S(1)} %bitcast.11, f32[8,128]{1,0:T(8,128)S(1)} %shard_map.73.factors, f32[20,128,128]{2,1,0:T(8,128)S(1)} %bitcast.7, f32[1,128]{1,0:T(1,128)S(1)} %bitcast.13, s32[1,2]{1,0:T(1,128)S(1)} %bitcast.15, ...), custom_call_target="tpu_custom_call" | custom-call | bytes 131072 | tf_op jit(solution)/shard_map/pallas_call | solution.py:299
  2.2 0.3 %collective-permute-done.1.factors = f32[8,128]{1,0:T(8,128)S(1)} collective-permute-done((f32[8,128]{1,0:T(8,128)S(1)}, f32[8,128]{1,0:T(8,128)S(1)}, u32[]{:S(2)}, u32[]{:S(2)}) %collective-permute-start.1) | collective-permute-done | bytes 4128 | tf_op jit(solution)/shard_map/ppermute | solution.py:317
  2.5 0.0 collective-permute-done.state
  2.5 0.2 %shard_map.75 = (f32[16,256]{1,0:T(8,128)S(1)}, f32[32,256]{1,0:T(8,128)S(1)}, f32[32,256]{1,0:T(8,128)S(1)}, f32[16,256]{1,0:T(8,128)S(1)}, f32[16,256]{1,0:T(8,128)S(1)}, /*index=5*/f32[16,256]{1,0:T(8,128)S(1)}) custom-call(f32[128,256]{1,0:T(8,128)S(1)} %get-tuple-element.20.own, bf16[128,256]{1,0:T(8,128)(2,1)S(1)} %get-tuple-element.21.high, ...), custom_call_target="tpu_custom_call" | custom-call | bytes 131072 | tf_op jit(solution)/shard_map/pallas_call | solution.py:299
  2.7 3.8 %collective-permute-start.2 = (f32[32,256]{1,0:T(8,128)S(1)}, f32[32,256]{1,0:T(8,128)S(1)}, u32[]{:S(2)}, u32[]{:S(2)}) collective-permute-start(f32[32,256]{1,0:T(8,128)S(1)} %get-tuple-element.23), channel_id=1, source_target_pairs={{0,16},{1,17},{2,19},{3,18},{4,20},{5,21},{6,23},{7,22},{8,24},{9,... | collective-permute-start | bytes 98312 | tf_op jit(solution)/shard_map/ppermute | solution.py:317
  6.5 1.1 %collective-permute-start.3 = (f32[32,256]{1,0:T(8,128)S(1)}, f32[32,256]{1,0:T(8,128)S(1)}, u32[]{:S(2)}, u32[]{:S(2)}) collective-permute-start(f32[32,256]{1,0:T(8,128)S(1)} %get-tuple-element.24), channel_id=1, source_target_pairs={{0,24},{1,25},{2,27},{3,26},{4,28},{5,29},{6,31},{7,30},{8,16},{9,... | collective-permute-start | bytes 98312 | tf_op jit(solution)/shard_map/ppermute | solution.py:317
  7.6 1.4 %collective-permute-start.4 = (f32[16,256]{1,0:T(8,128)S(1)}, f32[16,256]{1,0:T(8,128)S(1)}, u32[]{:S(2)}, u32[]{:S(2)}) collective-permute-start(f32[16,256]{1,0:T(8,128)S(1)} %get-tuple-element.30), channel_id=1, source_target_pairs={{0,9},{1,8},{2,11},{3,10},{4,13},{5,12},{6,15},{7,14},{8,1},{9,0},... | collective-permute-start | bytes 49160 | tf_op jit(solution)/shard_map/ppermute | solution.py:317
  9.0 0.5 %collective-permute-start.5 = (f32[16,256]{1,0:T(8,128)S(1)}, f32[16,256]{1,0:T(8,128)S(1)}, u32[]{:S(2)}, u32[]{:S(2)}) collective-permute-start(f32[16,256]{1,0:T(8,128)S(1)} %get-tuple-element.31), channel_id=1, source_target_pairs={{0,1},{1,0},{2,3},{3,2},{4,5},{5,4},{6,7},{7,6},{8,9},{9,8},{10,11... | collective-permute-start | bytes 49160 | tf_op jit(solution)/shard_map/ppermute | solution.py:317
  9.5 1.5 %collective-permute-start.6 = (f32[16,256]{1,0:T(8,128)S(1)}, f32[16,256]{1,0:T(8,128)S(1)}, u32[]{:S(2)}, u32[]{:S(2)}) collective-permute-start(f32[16,256]{1,0:T(8,128)S(1)} %get-tuple-element.32), channel_id=1, source_target_pairs={{0,8},{1,9},{2,10},{3,11},{4,12},{5,13},{6,14},{7,15},{8,0},{9,1},... | collective-permute-start | bytes 49160 | tf_op jit(solution)/shard_map/ppermute | solution.py:317
  11.1 0.0 copy-done.2
  11.1 0.7 %shard_map.76 = (bf16[256,256]{1,0:T(8,128)(2,1)S(1)}, bf16[256,256]{1,0:T(8,128)(2,1)S(1)}) custom-call(f32[20,128,128]{2,1,0:T(8,128)S(1)} %bitcast.8, f32[1,128]{1,0:T(1,128)S(1)} %bitcast.12, f32[16,256]{1,0:T(8,128)S(1)} %get-tuple-element.25.kept.refs_0_), custom_call_target="tpu_custom_call" | custom-call | bytes 131072 | tf_op jit(solution)/shard_map/pallas_call | solution.py:299
  11.8 0.0 collective-permute-done.2.refs_0_.refs_1_
  11.8 0.0 collective-permute-done.3.refs_1_.refs_2_
  11.8 0.7 %collective-permute-start.7 = (f32[32,256]{1,0:T(8,128)S(1)}, f32[32,256]{1,0:T(8,128)S(1)}, u32[]{:S(2)}, u32[]{:S(2)}) collective-permute-start(f32[32,256]{1,0:T(8,128)S(1)} %shard_map.77.give), channel_id=1, source_target_pairs={{0,2},{1,3},{2,0},{3,1},{4,6},{5,7},{6,4},{7,5},{8,10},{9,11},{10,... | collective-permute-start | bytes 98312 | tf_op jit(solution)/shard_map/ppermute | solution.py:317
  12.5 0.6 %shard_map.78 = (bf16[128,256]{1,0:T(8,128)(2,1)S(1)}, bf16[128,256]{1,0:T(8,128)(2,1)S(1)}, bf16[48,256]{1,0:T(8,128)(2,1)S(1)}, bf16[48,256]{1,0:T(8,128)(2,1)S(1)}) custom-call(f32[20,128,128]{2,1,0:T(8,128)S(1)} %bitcast.9, s32[1,2]{1,0:T(1,128)S(1)} %bitcast.16, f32[32,256]{1,0:T(8,128)S(1)} %shard_map.77.give, ...), custom_call_target="tpu_custom_call" | custom-call | flops 4294967296 | bytes 131072 | tf_op jit(solution)/shard_map/pallas_call | solution.py:299
  13.2 0.0 collective-permute-done.4.refs_0_
  13.2 0.0 collective-permute-done.5.refs_1_
  13.2 0.1 collective-permute-done.6.refs_2_
  13.3 0.1 collective-permute-done.7.refs_3_
  13.4 1.2 %shard_map.79 = f32[2,128,128]{2,1,0:T(8,128)} custom-call(bf16[48,256]{1,0:T(8,128)(2,1)S(1)} %get-tuple-element.28.high, bf16[48,256]{1,0:T(8,128)(2,1)S(1)} %get-tuple-element.29.low, f32[16,256]{1,0:T(8,128)S(1)} %collective-permute-done.4.refs_0_, f32[16,256]{1,0:T(8,128)S(1)} %collective-permute-done.5.refs_1_, ...), custom_call_target="tpu_custom_call" | custom-call | tf_op jit(solution)/shard_map/pallas_call | solution.py:370
  (2 shorter events, 0.0 us)
Async XLA Ops:
  0.0 1.5 %copy-start.1 = (f32[2,1,1,1,16384]{4,3,2,1,0:T(1,128)S(1)}, f32[2,1,1,1,16384]{4,3,2,1,0:T(1,128)}, u32[]{:S(2)}) copy-start(f32[2,1,1,1,16384]{4,3,2,1,0:T(1,128)} %param.7) | copy-start | bytes 393220
  0.0 1.5 %copy-start.4 = (s32[4]{0:T(128)S(1)}, s32[4]{0:T(128)}, u32[]{:S(2)}) copy-start(s32[4]{0:T(128)} %param.13) | copy-start | bytes 52
  0.0 1.5 %copy-start.5 = (s32[2]{0:T(128)S(1)}, s32[2]{0:T(128)}, u32[]{:S(2)}) copy-start(s32[2]{0:T(128)} %param.12) | copy-start | bytes 28
  0.0 1.5 %copy-start.3 = (f32[128]{0:T(128)S(1)}, f32[128]{0:T(128)}, u32[]{:S(2)}) copy-start(f32[128]{0:T(128)} %param.10) | copy-start | bytes 1540
  0.0 1.5 %copy-start = (f32[10,2,128,128]{3,2,1,0:T(8,128)S(1)}, f32[10,2,128,128]{3,2,1,0:T(8,128)}, u32[]{:S(2)}) copy-start(f32[10,2,128,128]{3,2,1,0:T(8,128)} %param.8) | copy-start | bytes 3932164
  0.0 2.4 %collective-permute-start = (f32[2,128,128]{2,1,0:T(8,128)}, f32[2,128,128]{2,1,0:T(8,128)S(1)}, u32[]{:S(2)}, u32[]{:S(2)}) collective-permute-start(f32[2,128,128]{2,1,0:T(8,128)} %bitcast.10), channel_id=1, source_target_pairs={{0,2},{1,3},{2,0},{3,1},{4,6},{5,7},{6,4},{7,5},{8,10},{9,11},{10,... | collective-permute-start | bytes 393224 | tf_op jit(solution)/shard_map/ppermute | solution.py:317
  1.2 9.9 %copy-start.2 = (f32[128]{0:T(128)S(1)}, f32[128]{0:T(128)}, u32[]{:S(2)}) copy-start(f32[128]{0:T(128)} %param.9) | copy-start | bytes 1540
  1.2 1.2 %collective-permute-start.1 = (f32[8,128]{1,0:T(8,128)S(1)}, f32[8,128]{1,0:T(8,128)S(1)}, u32[]{:S(2)}, u32[]{:S(2)}) collective-permute-start(f32[8,128]{1,0:T(8,128)S(1)} %shard_map.73.factors), channel_id=1, source_target_pairs={{0,2},{1,3},{2,0},{3,1},{4,6},{5,7},{6,4},{7,5},{8,10},{9,11},{10,... | collective-permute-start | bytes 12296 | tf_op jit(solution)/shard_map/ppermute | solution.py:317
  2.7 9.1 %collective-permute-start.2 = (f32[32,256]{1,0:T(8,128)S(1)}, f32[32,256]{1,0:T(8,128)S(1)}, u32[]{:S(2)}, u32[]{:S(2)}) collective-permute-start(f32[32,256]{1,0:T(8,128)S(1)} %get-tuple-element.23), channel_id=1, source_target_pairs={{0,16},{1,17},{2,19},{3,18},{4,20},{5,21},{6,23},{7,22},{8,24},{9,... | collective-permute-start | bytes 98312 | tf_op jit(solution)/shard_map/ppermute | solution.py:317
  6.5 5.3 %collective-permute-start.3 = (f32[32,256]{1,0:T(8,128)S(1)}, f32[32,256]{1,0:T(8,128)S(1)}, u32[]{:S(2)}, u32[]{:S(2)}) collective-permute-start(f32[32,256]{1,0:T(8,128)S(1)} %get-tuple-element.24), channel_id=1, source_target_pairs={{0,24},{1,25},{2,27},{3,26},{4,28},{5,29},{6,31},{7,30},{8,16},{9,... | collective-permute-start | bytes 98312 | tf_op jit(solution)/shard_map/ppermute | solution.py:317
  7.6 5.6 %collective-permute-start.4 = (f32[16,256]{1,0:T(8,128)S(1)}, f32[16,256]{1,0:T(8,128)S(1)}, u32[]{:S(2)}, u32[]{:S(2)}) collective-permute-start(f32[16,256]{1,0:T(8,128)S(1)} %get-tuple-element.30), channel_id=1, source_target_pairs={{0,9},{1,8},{2,11},{3,10},{4,13},{5,12},{6,15},{7,14},{8,1},{9,0},... | collective-permute-start | bytes 49160 | tf_op jit(solution)/shard_map/ppermute | solution.py:317
  9.0 4.2 %collective-permute-start.5 = (f32[16,256]{1,0:T(8,128)S(1)}, f32[16,256]{1,0:T(8,128)S(1)}, u32[]{:S(2)}, u32[]{:S(2)}) collective-permute-start(f32[16,256]{1,0:T(8,128)S(1)} %get-tuple-element.31), channel_id=1, source_target_pairs={{0,1},{1,0},{2,3},{3,2},{4,5},{5,4},{6,7},{7,6},{8,9},{9,8},{10,11... | collective-permute-start | bytes 49160 | tf_op jit(solution)/shard_map/ppermute | solution.py:317
  9.5 3.7 %collective-permute-start.6 = (f32[16,256]{1,0:T(8,128)S(1)}, f32[16,256]{1,0:T(8,128)S(1)}, u32[]{:S(2)}, u32[]{:S(2)}) collective-permute-start(f32[16,256]{1,0:T(8,128)S(1)} %get-tuple-element.32), channel_id=1, source_target_pairs={{0,8},{1,9},{2,10},{3,11},{4,12},{5,13},{6,14},{7,15},{8,0},{9,1},... | collective-permute-start | bytes 49160 | tf_op jit(solution)/shard_map/ppermute | solution.py:317
  11.8 1.6 %collective-permute-start.7 = (f32[32,256]{1,0:T(8,128)S(1)}, f32[32,256]{1,0:T(8,128)S(1)}, u32[]{:S(2)}, u32[]{:S(2)}) collective-permute-start(f32[32,256]{1,0:T(8,128)S(1)} %shard_map.77.give), channel_id=1, source_target_pairs={{0,2},{1,3},{2,0},{3,1},{4,6},{5,7},{6,4},{7,5},{8,10},{9,11},{10,... | collective-permute-start | bytes 98312 | tf_op jit(solution)/shard_map/ppermute | solution.py:317

commit v6 on v5

--- a/solution.py
+++ b/solution.py
@@ -105,18 +105,24 @@
         self.chunk = rows // (2 * wide_count)
         half = wide_count // 2
         tops = [tuple(range(k, min(k + 2, wide_count))) for k in range(half, wide_count, 2)]
-        self.steps = [((pair[0], pair[-1]), (0, 1)) for pair in tops]
-        self.steps += [((pair[1], pair[0]), (0, 1)) for pair in tops if len(pair) == 2]
-        near = range(half - 1, 0, -1)
-        self.steps += [((offset, offset), (1, 1)) for offset in near]
-        self.steps.append(((0, 0), (1, 1)))
-        self.steps += [((offset, offset), (0, 0)) for offset in near]
-        self.shared = [step for step in self.steps if step[1][0] != step[1][1]]
-        self.direct = [step for step in self.steps if step[1][0] == step[1][1]]
-
-
-def choose(flag, pair):
-    return pair[0] if pair[0] == pair[1] else pair[0] ^ (flag * (pair[0] ^ pair[1]))
+        half = wide_count // 2
+        tops = [tuple(range(k, min(k + 2, wide_count))) for k in range(half, wide_count, 2)]
+        pairs = [(pair[0], pair[-1]) for pair in tops]
+        pairs += [(pair[1], pair[0]) for pair in tops if len(pair) == 2]
+        pairs += [(offset, offset) for offset in range(half - 1, 1, -1)]
+        self.steps = [((*pair, 0), (*pair, 1)) for pair in pairs]
+        if half > 1:
+            self.steps += [((1, 1, 0), (0, 0, 1)), ((1, 1, 1), (1, 1, 1))]
+        else:
+            self.steps.append(((0, 0, 1), (0, 0, 1)))
+        self.shared = [step for step in self.steps if step[0] != step[1]]
+        self.direct = [step for step in self.steps if step[0] == step[1]]
+
+
+def partner(step, core, half, wide, low):
+    entries = [(low_part, a ^ (half * (a ^ b))) for a, b, low_part in step]
+    low_part, wide_part = [a ^ (core * (a ^ b)) for a, b in zip(*entries)]
+    return wide ^ wide_part, low ^ low_part
 
 
 def free_row(plan, inner, swap):
@@ -139,9 +145,9 @@
     targets = [(wide, low, core)]
     half = wide >> (plan.wide_bits - 1)
     for step in plan.steps:
-        to_wide, to_low = wide ^ choose(half, step[0]), low ^ choose(core, step[1])
+        chip = partner(step, core, half, wide, low)
         for to_core in (core, 1 - core)[: 2 if step in plan.shared else 1]:
-            targets.append((to_wide, to_low, to_core))
+            targets.append((*chip, to_core))
     base = plan.row_bits - 4
     position = plan.row_bits - 3 + swaps[0]
     places = [base + order[place] for place in range(4)]
@@ -169,7 +175,7 @@
     sources = [(wide, low)]
     for server, steps in ((core, plan.shared), (core, plan.direct), (1 - core, plan.shared)):
         for step in steps:
-            sources.append((wide ^ choose(1 - half, step[0]), low ^ choose(server, step[1])))
+            sources.append(partner(step, server, 1 - half, wide, low))
     inner = lax.broadcasted_iota(jnp.int32, (plan.chunk, plan.rows), 0)
     inner = free_row(plan, inner, swaps[1])
     result = []
@@ -305,14 +311,15 @@
     )(*args)
 
 
-def exchange(value, step=((0, 0), (0, 0)), flip=0):
+def exchange(value, step=((0, 0, 0), (0, 0, 0)), flip=0):
     wides, mids, lows = (lax.axis_size(axis) for axis in AXES)
     pairs = []
     for wide in range(wides):
         for mid in range(mids):
             for low in range(lows):
-                to_wide = wide ^ step[0][2 * wide // wides]
-                to = (to_wide * mids + (mid ^ flip)) * lows + (low ^ step[1][mid & 1])
+                *offsets, low_part = step[mid & 1]
+                to_wide = wide ^ offsets[2 * wide // wides]
+                to = (to_wide * mids + (mid ^ flip)) * lows + (low ^ low_part)
                 pairs.append(((wide * mids + mid) * lows + low, to))
     return lax.ppermute(value, AXES, pairs)
 
@@ -375,7 +382,7 @@
     return out.reshape(state.shape)
 
 
-def partner(value, axis, stride):
+def mate(value, axis, stride):
     mask = 2**stride
     pairs = [(source, source ^ mask) for source in range(lax.axis_size(axis))]
     return lax.ppermute(value, axis, pairs)
@@ -461,7 +468,7 @@
     blocks, row_index, sent_half = half_rows(
         vector, swap_qubits[0], local_bits - 3, mid_bit, local_len
     )
-    received = partner(sent_half, "mid", 0)
+    received = mate(sent_half, "mid", 0)
     vector = blocks.at[:, :, row_index].set(received).reshape(2, local_len)
     row_ids = jnp.arange(16, dtype=jnp.int32)[:, None]
     row_bits = jnp.right_shift(row_ids, jnp.arange(4, dtype=jnp.int32)[None, :]) & 1

time: 14.7 us -> 14.7 us (level)
  waiting for transfers between devices: 0.52 us -> 1.18 us
  starting transfers between devices: 9.86 us -> 9.22 us
    ppermute x8 -> x7, waiting for transfers between devices: 0.52 us -> 1.18 us  [exchange(): return lax.ppermute(value, AXES, pairs)]
    ppermute x8 -> x7, starting transfers between devices: 9.86 us -> 9.22 us  [exchange(): return lax.ppermute(value, AXES, pairs)]
  transfers between devices with their start and end apart: 8 -> 7, of which waited for: 3 -> 4; matrix products, arithmetic and copies ran while one was open for 0% -> 0% of each run, Pallas kernels for 14% -> 14%
where the time goes in v6:
time: 14.7 us; the launch traced here: 14.5 us
  starting transfers between devices  9.22 us (63%)
  Pallas kernels  3.39 us (23%)
  waiting for transfers between devices  1.18 us (8%)
  between operations  0.73 us (5%)
    ppermute x7, starting transfers between devices, exchange(): return lax.ppermute(value, AXES, pairs)  9.22 us
    pallas_call x6, Pallas kernels, call(): pl.pallas_call(kernel, out_shape=[pltpu.VMEM(shape, dtype) for shape, dty...  2.23 us
    ppermute x7, waiting for transfers between devices, exchange(): return lax.ppermute(value, AXES, pairs)  1.18 us
    pallas_call x1, Pallas kernels, merged_device(): pl.pallas_call(partial(last_kernel, plan), out_shape=jax.ShapeDtypeStruct...  1.16 us
  transfers between devices with their start and end apart: 7, of which 4 were waited for; matrix products, arithmetic and copies ran while one was open for 0% of the time, Pallas kernels for 14%

profile of v6, /device:TPU:0, one launch (start us, length us, event | category | flops | bytes accessed | tf_op | source)
XLA Modules:
  0.0 14.5 jit_solution(10586290122537858996)
XLA Ops:
  0.0 0.0 copy-start.1
  0.0 0.0 copy-start
  0.0 0.0 copy-start.5
  0.0 0.0 copy-start.3
  0.0 0.0 copy-start.4
  0.0 0.5 %collective-permute-start = (f32[2,128,128]{2,1,0:T(8,128)}, f32[2,128,128]{2,1,0:T(8,128)S(1)}, u32[]{:S(2)}, u32[]{:S(2)}) collective-permute-start(f32[2,128,128]{2,1,0:T(8,128)} %bitcast.10), channel_id=1, source_target_pairs={{0,2},{1,3},{2,0},{3,1},{4,6},{5,7},{6,4},{7,5},{8,10},{9,11},{10,... | collective-permute-start | bytes 393224 | tf_op jit(solution)/shard_map/ppermute | solution.py:324
  1.2 0.0 copy-start.2
  1.2 0.2 %collective-permute-start.1 = (f32[8,128]{1,0:T(8,128)S(1)}, f32[8,128]{1,0:T(8,128)S(1)}, u32[]{:S(2)}, u32[]{:S(2)}) collective-permute-start(f32[8,128]{1,0:T(8,128)S(1)} %shard_map.73.factors), channel_id=1, source_target_pairs={{0,2},{1,3},{2,0},{3,1},{4,6},{5,7},{6,4},{7,5},{8,10},{9,11},{10,... | collective-permute-start | bytes 12296 | tf_op jit(solution)/shard_map/ppermute | solution.py:324
  1.4 0.0 copy-done.1
  1.4 0.0 copy-done
  1.4 0.0 copy-done.5
  1.4 0.0 copy-done.3
  1.4 0.0 copy-done.4
  1.5 0.7 %shard_map.74 = (f32[128,256]{1,0:T(8,128)S(1)}, bf16[128,256]{1,0:T(8,128)(2,1)S(1)}, bf16[128,256]{1,0:T(8,128)(2,1)S(1)}) custom-call(f32[2,128,128]{2,1,0:T(8,128)S(1)} %bitcast.11, f32[8,128]{1,0:T(8,128)S(1)} %shard_map.73.factors, f32[20,128,128]{2,1,0:T(8,128)S(1)} %bitcast.7, f32[1,128]{1,0:T(1,128)S(1)} %bitcast.13, s32[1,2]{1,0:T(1,128)S(1)} %bitcast.15, ...), custom_call_target="tpu_custom_call" | custom-call | bytes 131072 | tf_op jit(solution)/shard_map/pallas_call | solution.py:305
  2.1 0.3 %collective-permute-done.1.factors = f32[8,128]{1,0:T(8,128)S(1)} collective-permute-done((f32[8,128]{1,0:T(8,128)S(1)}, f32[8,128]{1,0:T(8,128)S(1)}, u32[]{:S(2)}, u32[]{:S(2)}) %collective-permute-start.1) | collective-permute-done | bytes 4128 | tf_op jit(solution)/shard_map/ppermute | solution.py:324
  2.5 0.0 collective-permute-done.state
  2.5 0.2 %shard_map.75 = (f32[16,256]{1,0:T(8,128)S(1)}, f32[32,256]{1,0:T(8,128)S(1)}, f32[32,256]{1,0:T(8,128)S(1)}, f32[32,256]{1,0:T(8,128)S(1)}, f32[16,256]{1,0:T(8,128)S(1)}) custom-call(f32[128,256]{1,0:T(8,128)S(1)} %get-tuple-element.19.own, bf16[128,256]{1,0:T(8,128)(2,1)S(1)} %get-tuple-element.20.high, bf16[128,256]{1,0:T(8,128)(2,1)S(1)} %get-tuple-element.21.low, ...), custom_call_target="tpu_custom_call" | custom-call | bytes 131072 | tf_op jit(solution)/shard_map/pallas_call | solution.py:305
  2.7 3.8 %collective-permute-start.2 = (f32[32,256]{1,0:T(8,128)S(1)}, f32[32,256]{1,0:T(8,128)S(1)}, u32[]{:S(2)}, u32[]{:S(2)}) collective-permute-start(f32[32,256]{1,0:T(8,128)S(1)} %get-tuple-element.22), channel_id=1, source_target_pairs={{0,16},{1,17},{2,19},{3,18},{4,20},{5,21},{6,23},{7,22},{8,24},{9,... | collective-permute-start | bytes 98312 | tf_op jit(solution)/shard_map/ppermute | solution.py:324
  6.5 1.1 %collective-permute-start.3 = (f32[32,256]{1,0:T(8,128)S(1)}, f32[32,256]{1,0:T(8,128)S(1)}, u32[]{:S(2)}, u32[]{:S(2)}) collective-permute-start(f32[32,256]{1,0:T(8,128)S(1)} %get-tuple-element.23), channel_id=1, source_target_pairs={{0,24},{1,25},{2,27},{3,26},{4,28},{5,29},{6,31},{7,30},{8,16},{9,... | collective-permute-start | bytes 98312 | tf_op jit(solution)/shard_map/ppermute | solution.py:324
  7.6 0.5 %collective-permute-start.4 = (f32[32,256]{1,0:T(8,128)S(1)}, f32[32,256]{1,0:T(8,128)S(1)}, u32[]{:S(2)}, u32[]{:S(2)}) collective-permute-start(f32[32,256]{1,0:T(8,128)S(1)} %get-tuple-element.24), channel_id=1, source_target_pairs={{0,8},{1,9},{2,3},{3,2},{4,12},{5,13},{6,7},{7,6},{8,0},{9,1},{10,... | collective-permute-start | bytes 98312 | tf_op jit(solution)/shard_map/ppermute | solution.py:324
  8.1 2.6 %collective-permute-start.5 = (f32[16,256]{1,0:T(8,128)S(1)}, f32[16,256]{1,0:T(8,128)S(1)}, u32[]{:S(2)}, u32[]{:S(2)}) collective-permute-start(f32[16,256]{1,0:T(8,128)S(1)} %get-tuple-element.30), channel_id=1, source_target_pairs={{0,9},{1,8},{2,11},{3,10},{4,13},{5,12},{6,15},{7,14},{8,1},{9,0},... | collective-permute-start | bytes 49160 | tf_op jit(solution)/shard_map/ppermute | solution.py:324
  10.7 0.0 copy-done.2
  10.7 0.7 %shard_map.76 = (bf16[256,256]{1,0:T(8,128)(2,1)S(1)}, bf16[256,256]{1,0:T(8,128)(2,1)S(1)}) custom-call(f32[20,128,128]{2,1,0:T(8,128)S(1)} %bitcast.8, f32[1,128]{1,0:T(1,128)S(1)} %bitcast.12, f32[16,256]{1,0:T(8,128)S(1)} %get-tuple-element.25.kept.refs_0_), custom_call_target="tpu_custom_call" | custom-call | bytes 131072 | tf_op jit(solution)/shard_map/pallas_call | solution.py:305
  11.4 0.0 collective-permute-done.2.refs_0_.refs_1_
  11.4 0.3 %collective-permute-done.3.refs_1_.refs_2_ = f32[32,256]{1,0:T(8,128)S(1)} collective-permute-done((f32[32,256]{1,0:T(8,128)S(1)}, f32[32,256]{1,0:T(8,128)S(1)}, u32[]{:S(2)}, u32[]{:S(2)}) %collective-permute-start.3) | collective-permute-done | bytes 32800 | tf_op jit(solution)/shard_map/ppermute | solution.py:324
  11.7 0.3 %collective-permute-done.4.refs_2_.refs_3_ = f32[32,256]{1,0:T(8,128)S(1)} collective-permute-done((f32[32,256]{1,0:T(8,128)S(1)}, f32[32,256]{1,0:T(8,128)S(1)}, u32[]{:S(2)}, u32[]{:S(2)}) %collective-permute-start.4) | collective-permute-done | bytes 32800 | tf_op jit(solution)/shard_map/ppermute | solution.py:324
  12.0 0.5 %collective-permute-start.6 = (f32[48,256]{1,0:T(8,128)S(1)}, f32[48,256]{1,0:T(8,128)S(1)}, u32[]{:S(2)}, u32[]{:S(2)}) collective-permute-start(f32[48,256]{1,0:T(8,128)S(1)} %shard_map.77.give), channel_id=1, source_target_pairs={{0,2},{1,3},{2,0},{3,1},{4,6},{5,7},{6,4},{7,5},{8,10},{9,11},{10,... | collective-permute-start | bytes 147464 | tf_op jit(solution)/shard_map/ppermute | solution.py:324
  12.5 0.6 %shard_map.78 = (bf16[128,256]{1,0:T(8,128)(2,1)S(1)}, bf16[128,256]{1,0:T(8,128)(2,1)S(1)}, bf16[64,256]{1,0:T(8,128)(2,1)S(1)}, bf16[64,256]{1,0:T(8,128)(2,1)S(1)}) custom-call(f32[20,128,128]{2,1,0:T(8,128)S(1)} %bitcast.9, s32[1,2]{1,0:T(1,128)S(1)} %bitcast.16, f32[48,256]{1,0:T(8,128)S(1)} %shard_map.77.give, ...), custom_call_target="tpu_custom_call" | custom-call | flops 4294967296 | bytes 131072 | tf_op jit(solution)/shard_map/pallas_call | solution.py:305
  13.1 0.0 collective-permute-done.5.refs_0_
  13.1 0.2 %collective-permute-done.6.refs_1_ = f32[48,256]{1,0:T(8,128)S(1)} collective-permute-done((f32[48,256]{1,0:T(8,128)S(1)}, f32[48,256]{1,0:T(8,128)S(1)}, u32[]{:S(2)}, u32[]{:S(2)}) %collective-permute-start.6) | collective-permute-done | bytes 49184 | tf_op jit(solution)/shard_map/ppermute | solution.py:324
  13.4 1.2 %shard_map.79 = f32[2,128,128]{2,1,0:T(8,128)} custom-call(bf16[64,256]{1,0:T(8,128)(2,1)S(1)} %get-tuple-element.28.high, bf16[64,256]{1,0:T(8,128)(2,1)S(1)} %get-tuple-element.29.low, f32[16,256]{1,0:T(8,128)S(1)} %collective-permute-done.5.refs_0_, f32[48,256]{1,0:T(8,128)S(1)} %collective-permute-done.6.refs_1_, ...), custom_call_target="tpu_custom_call" | custom-call | tf_op jit(solution)/shard_map/pallas_call | solution.py:377
  (2 shorter events, 0.0 us)
Async XLA Ops:
  0.0 1.4 %copy-start.1 = (f32[2,1,1,1,16384]{4,3,2,1,0:T(1,128)S(1)}, f32[2,1,1,1,16384]{4,3,2,1,0:T(1,128)}, u32[]{:S(2)}) copy-start(f32[2,1,1,1,16384]{4,3,2,1,0:T(1,128)} %param.7) | copy-start | bytes 393220
  0.0 1.4 %copy-start = (f32[10,2,128,128]{3,2,1,0:T(8,128)S(1)}, f32[10,2,128,128]{3,2,1,0:T(8,128)}, u32[]{:S(2)}) copy-start(f32[10,2,128,128]{3,2,1,0:T(8,128)} %param.8) | copy-start | bytes 3932164
  0.0 1.4 %copy-start.5 = (s32[2]{0:T(128)S(1)}, s32[2]{0:T(128)}, u32[]{:S(2)}) copy-start(s32[2]{0:T(128)} %param.12) | copy-start | bytes 28
  0.0 1.4 %copy-start.3 = (f32[128]{0:T(128)S(1)}, f32[128]{0:T(128)}, u32[]{:S(2)}) copy-start(f32[128]{0:T(128)} %param.10) | copy-start | bytes 1540
  0.0 1.4 %copy-start.4 = (s32[4]{0:T(128)S(1)}, s32[4]{0:T(128)}, u32[]{:S(2)}) copy-start(s32[4]{0:T(128)} %param.13) | copy-start | bytes 52
  0.0 2.4 %collective-permute-start = (f32[2,128,128]{2,1,0:T(8,128)}, f32[2,128,128]{2,1,0:T(8,128)S(1)}, u32[]{:S(2)}, u32[]{:S(2)}) collective-permute-start(f32[2,128,128]{2,1,0:T(8,128)} %bitcast.10), channel_id=1, source_target_pairs={{0,2},{1,3},{2,0},{3,1},{4,6},{5,7},{6,4},{7,5},{8,10},{9,11},{10,... | collective-permute-start | bytes 393224 | tf_op jit(solution)/shard_map/ppermute | solution.py:324
  1.2 9.5 %copy-start.2 = (f32[128]{0:T(128)S(1)}, f32[128]{0:T(128)}, u32[]{:S(2)}) copy-start(f32[128]{0:T(128)} %param.9) | copy-start | bytes 1540
  1.2 1.2 %collective-permute-start.1 = (f32[8,128]{1,0:T(8,128)S(1)}, f32[8,128]{1,0:T(8,128)S(1)}, u32[]{:S(2)}, u32[]{:S(2)}) collective-permute-start(f32[8,128]{1,0:T(8,128)S(1)} %shard_map.73.factors), channel_id=1, source_target_pairs={{0,2},{1,3},{2,0},{3,1},{4,6},{5,7},{6,4},{7,5},{8,10},{9,11},{10,... | collective-permute-start | bytes 12296 | tf_op jit(solution)/shard_map/ppermute | solution.py:324
  2.7 8.7 %collective-permute-start.2 = (f32[32,256]{1,0:T(8,128)S(1)}, f32[32,256]{1,0:T(8,128)S(1)}, u32[]{:S(2)}, u32[]{:S(2)}) collective-permute-start(f32[32,256]{1,0:T(8,128)S(1)} %get-tuple-element.22), channel_id=1, source_target_pairs={{0,16},{1,17},{2,19},{3,18},{4,20},{5,21},{6,23},{7,22},{8,24},{9,... | collective-permute-start | bytes 98312 | tf_op jit(solution)/shard_map/ppermute | solution.py:324
  6.5 5.2 %collective-permute-start.3 = (f32[32,256]{1,0:T(8,128)S(1)}, f32[32,256]{1,0:T(8,128)S(1)}, u32[]{:S(2)}, u32[]{:S(2)}) collective-permute-start(f32[32,256]{1,0:T(8,128)S(1)} %get-tuple-element.23), channel_id=1, source_target_pairs={{0,24},{1,25},{2,27},{3,26},{4,28},{5,29},{6,31},{7,30},{8,16},{9,... | collective-permute-start | bytes 98312 | tf_op jit(solution)/shard_map/ppermute | solution.py:324
  7.6 4.4 %collective-permute-start.4 = (f32[32,256]{1,0:T(8,128)S(1)}, f32[32,256]{1,0:T(8,128)S(1)}, u32[]{:S(2)}, u32[]{:S(2)}) collective-permute-start(f32[32,256]{1,0:T(8,128)S(1)} %get-tuple-element.24), channel_id=1, source_target_pairs={{0,8},{1,9},{2,3},{3,2},{4,12},{5,13},{6,7},{7,6},{8,0},{9,1},{10,... | collective-permute-start | bytes 98312 | tf_op jit(solution)/shard_map/ppermute | solution.py:324
  8.1 5.1 %collective-permute-start.5 = (f32[16,256]{1,0:T(8,128)S(1)}, f32[16,256]{1,0:T(8,128)S(1)}, u32[]{:S(2)}, u32[]{:S(2)}) collective-permute-start(f32[16,256]{1,0:T(8,128)S(1)} %get-tuple-element.30), channel_id=1, source_target_pairs={{0,9},{1,8},{2,11},{3,10},{4,13},{5,12},{6,15},{7,14},{8,1},{9,0},... | collective-permute-start | bytes 49160 | tf_op jit(solution)/shard_map/ppermute | solution.py:324
  12.0 1.4 %collective-permute-start.6 = (f32[48,256]{1,0:T(8,128)S(1)}, f32[48,256]{1,0:T(8,128)S(1)}, u32[]{:S(2)}, u32[]{:S(2)}) collective-permute-start(f32[48,256]{1,0:T(8,128)S(1)} %shard_map.77.give), channel_id=1, source_target_pairs={{0,2},{1,3},{2,0},{3,1},{4,6},{5,7},{6,4},{7,5},{8,10},{9,11},{10,... | collective-permute-start | bytes 147464 | tf_op jit(solution)/shard_map/ppermute | solution.py:324

commit v7 on v6

--- a/solution.py
+++ b/solution.py
@@ -203,7 +203,11 @@
     return jnp.concatenate([real * cosine - imag * sine, real * sine + imag * cosine], 1)
 
 
-def front_kernel(plan, state, factors, gates, angle, swaps, order, own, high, low):
+def load_kernel(state, factors, turned):
+    turned[...] = spin(side(state), factors[...])
+
+
+def front_kernel(plan, state, gates, angle, swaps, order, own, high, low):
     chunks = sent_rows(plan, scalars(swaps), scalars(order))
     chosen = one_hot(plan, [rows for rows, _ in chunks])
     core = lax.axis_index("mid") & 1
@@ -212,13 +216,12 @@
     outer = tuple(dot(chosen, part).astype(jnp.bfloat16) for part in split(gate(gates, 3)))
     inner = turn(gate(gates, 1), angle[...])
     merged = complex_product(outer, split(inner))
-    own[...] = spin(complex_product(split(merged * mask), split(side(state))), factors[...])
+    own[...] = complex_product(split(merged * mask), split(state[...]))
     high[...], low[...] = split(merged * (1.0 - mask))
 
 
-def send_kernel(plan, own, high, low, state, factors, *sent):
-    total = complex_product((high[...], low[...]), split(side(state)))
-    total = own[...] + spin(total, factors[...])
+def send_kernel(plan, own, high, low, state, *sent):
+    total = own[...] + complex_product((high[...], low[...]), split(state[...]))
     start = 0
     for ref in sent:
         ref[...] = total[start : start + ref.shape[0]]
@@ -332,22 +335,22 @@
     gates = gates.reshape(-1, rows, rows)
     swaps, order = swap_qubits.reshape(1, -1), regroup_order.reshape(1, -1)
     square = state.reshape(2, rows, rows)
-    other = exchange(square, flip=1)
     (factors,) = call(partial(phase_kernel, plan), [((8, rows), f32)], (phase_top,), (SSPEC,), BUSY)
-    other_factors = exchange(factors, flip=1)
+    (turned,) = call(load_kernel, [((rows, 2 * rows), f32)], (square, factors), (VSPEC,) * 2)
+    other = exchange(turned, flip=1)
     own, high, low = call(
         partial(front_kernel, plan),
         [((rows, 2 * rows), f32), ((rows, 2 * rows), bf16), ((rows, 2 * rows), bf16)],
-        (square, factors, gates, phase_mid.reshape(1, rows), swaps, order),
-        (VSPEC,) * 6,
+        (turned, gates, phase_mid.reshape(1, rows), swaps, order),
+        (VSPEC,) * 5,
     )
     shapes = [(chunk, 2 * rows)]
     shapes += [(2 * chunk if step in plan.shared else chunk, 2 * rows) for step in plan.steps]
     local, *sent = call(
         partial(send_kernel, plan),
         [(shape, f32) for shape in shapes],
-        (own, high, low, other, other_factors),
-        (VSPEC,) * 5,
+        (own, high, low, other),
+        (VSPEC,) * 4,
     )
     received = [exchange(value, step) for value, step in zip(sent, plan.steps)]
     right_high, right_low = call(

time: 14.7 us -> 14.5 us (0.986)
  starting transfers between devices: 9.22 us -> 8.97 us
    ppermute x7 -> x6, starting transfers between devices: 9.22 us -> 8.97 us  [exchange(): return lax.ppermute(value, AXES, pairs)]
    ppermute x7 -> x6, waiting for transfers between devices: 1.18 us -> 1.04 us  [exchange(): return lax.ppermute(value, AXES, pairs)]
    pallas_call x6 -> x7, Pallas kernels: 2.23 us -> 2.24 us  [call(): pl.pallas_call(kernel, out_shape=[pltpu.VMEM(shape, dtype) for shape, dty...]
  transfers between devices with their start and end apart: 7 -> 6, of which waited for: 4 -> 5; matrix products, arithmetic and copies ran while one was open for 0% -> 0% of each run, Pallas kernels for 14% -> 14%
where the time goes in v7:
time: 14.5 us; the launch traced here: 14.4 us
  starting transfers between devices  8.97 us (62%)
  Pallas kernels  3.4 us (23%)
  waiting for transfers between devices  1.04 us (7%)
  between operations  0.83 us (6%)
    ppermute x6, starting transfers between devices, exchange(): return lax.ppermute(value, AXES, pairs)  8.97 us
    pallas_call x7, Pallas kernels, call(): pl.pallas_call(kernel, out_shape=[pltpu.VMEM(shape, dtype) for shape, dty...  2.24 us
    pallas_call x1, Pallas kernels, merged_device(): pl.pallas_call(partial(last_kernel, plan), out_shape=jax.ShapeDtypeStruct...  1.16 us
    ppermute x6, waiting for transfers between devices, exchange(): return lax.ppermute(value, AXES, pairs)  1.04 us
  transfers between devices with their start and end apart: 6, of which 5 were waited for; matrix products, arithmetic and copies ran while one was open for 0% of the time, Pallas kernels for 14%

profile of v7, /device:TPU:0, one launch (start us, length us, event | category | flops | bytes accessed | tf_op | source)
XLA Modules:
  0.0 14.4 jit_solution(8399473663586704781)
XLA Ops:
  0.0 0.0 copy-start.1
  0.0 0.0 copy-start
  0.0 0.0 copy-start.5
  0.0 0.0 copy-start.3
  0.0 0.0 copy-start.4
  0.8 0.0 copy-start.2
  0.8 0.1 copy-done.1
  0.9 0.5 %collective-permute-start = (f32[128,256]{1,0:T(8,128)S(1)}, f32[128,256]{1,0:T(8,128)S(1)}, u32[]{:S(2)}, u32[]{:S(2)}) collective-permute-start(f32[128,256]{1,0:T(8,128)S(1)} %shard_map.74.state), channel_id=1, source_target_pairs={{0,2},{1,3},{2,0},{3,1},{4,6},{5,7},{6,4},{7,5},{8,10},{9,11},{10,... | collective-permute-start | bytes 393224 | tf_op jit(solution)/shard_map/ppermute | solution.py:327
  1.4 0.0 copy-done
  1.4 0.0 copy-done.5
  1.4 0.0 copy-done.3
  1.5 0.0 copy-done.4
  1.5 0.7 %shard_map.75 = (f32[128,256]{1,0:T(8,128)S(1)}, bf16[128,256]{1,0:T(8,128)(2,1)S(1)}, bf16[128,256]{1,0:T(8,128)(2,1)S(1)}) custom-call(f32[128,256]{1,0:T(8,128)S(1)} %shard_map.74.state, f32[20,128,128]{2,1,0:T(8,128)S(1)} %bitcast.7, f32[1,128]{1,0:T(1,128)S(1)} %bitcast.12, s32[1,2]{1,0:T(1,128)S(1)} %bitcast.14, s32[1,4]{1,0:T(1,128)S(1)} %bitcast.13), custom_call_target="tpu_custom_call" | custom-call | bytes 131072 | tf_op jit(solution)/shard_map/pallas_call | solution.py:308
  2.1 0.3 %collective-permute-done.state = f32[128,256]{1,0:T(8,128)S(1)} collective-permute-done((f32[128,256]{1,0:T(8,128)S(1)}, f32[128,256]{1,0:T(8,128)S(1)}, u32[]{:S(2)}, u32[]{:S(2)}) %collective-permute-start) | collective-permute-done | bytes 131104 | tf_op jit(solution)/shard_map/ppermute | solution.py:327
  2.4 0.2 %shard_map.76 = (f32[16,256]{1,0:T(8,128)S(1)}, f32[32,256]{1,0:T(8,128)S(1)}, f32[32,256]{1,0:T(8,128)S(1)}, f32[32,256]{1,0:T(8,128)S(1)}, f32[16,256]{1,0:T(8,128)S(1)}) custom-call(f32[128,256]{1,0:T(8,128)S(1)} %get-tuple-element.19.own, bf16[128,256]{1,0:T(8,128)(2,1)S(1)} %get-tuple-element.20.high, bf16[128,256]{1,0:T(8,128)(2,1)S(1)} %get-tuple-element.21.low, ...), custom_call_target="tpu_custom_call" | custom-call | bytes 131072 | tf_op jit(solution)/shard_map/pallas_call | solution.py:308
  2.7 4.0 %collective-permute-start.1 = (f32[32,256]{1,0:T(8,128)S(1)}, f32[32,256]{1,0:T(8,128)S(1)}, u32[]{:S(2)}, u32[]{:S(2)}) collective-permute-start(f32[32,256]{1,0:T(8,128)S(1)} %get-tuple-element.22), channel_id=1, source_target_pairs={{0,16},{1,17},{2,19},{3,18},{4,20},{5,21},{6,23},{7,22},{8,24},{9,... | collective-permute-start | bytes 98312 | tf_op jit(solution)/shard_map/ppermute | solution.py:327
  6.7 1.1 %collective-permute-start.2 = (f32[32,256]{1,0:T(8,128)S(1)}, f32[32,256]{1,0:T(8,128)S(1)}, u32[]{:S(2)}, u32[]{:S(2)}) collective-permute-start(f32[32,256]{1,0:T(8,128)S(1)} %get-tuple-element.23), channel_id=1, source_target_pairs={{0,24},{1,25},{2,27},{3,26},{4,28},{5,29},{6,31},{7,30},{8,16},{9,... | collective-permute-start | bytes 98312 | tf_op jit(solution)/shard_map/ppermute | solution.py:327
  7.7 0.5 %collective-permute-start.3 = (f32[32,256]{1,0:T(8,128)S(1)}, f32[32,256]{1,0:T(8,128)S(1)}, u32[]{:S(2)}, u32[]{:S(2)}) collective-permute-start(f32[32,256]{1,0:T(8,128)S(1)} %get-tuple-element.24), channel_id=1, source_target_pairs={{0,8},{1,9},{2,3},{3,2},{4,12},{5,13},{6,7},{7,6},{8,0},{9,1},{10,... | collective-permute-start | bytes 98312 | tf_op jit(solution)/shard_map/ppermute | solution.py:327
  8.2 2.6 %collective-permute-start.4 = (f32[16,256]{1,0:T(8,128)S(1)}, f32[16,256]{1,0:T(8,128)S(1)}, u32[]{:S(2)}, u32[]{:S(2)}) collective-permute-start(f32[16,256]{1,0:T(8,128)S(1)} %get-tuple-element.30), channel_id=1, source_target_pairs={{0,9},{1,8},{2,11},{3,10},{4,13},{5,12},{6,15},{7,14},{8,1},{9,0},... | collective-permute-start | bytes 49160 | tf_op jit(solution)/shard_map/ppermute | solution.py:327
  10.9 0.0 copy-done.2
  10.9 0.7 %shard_map.77 = (bf16[256,256]{1,0:T(8,128)(2,1)S(1)}, bf16[256,256]{1,0:T(8,128)(2,1)S(1)}) custom-call(f32[20,128,128]{2,1,0:T(8,128)S(1)} %bitcast.8, f32[1,128]{1,0:T(1,128)S(1)} %bitcast.11, f32[16,256]{1,0:T(8,128)S(1)} %get-tuple-element.25.kept.refs_0_), custom_call_target="tpu_custom_call" | custom-call | bytes 131072 | tf_op jit(solution)/shard_map/pallas_call | solution.py:308
  11.6 0.0 collective-permute-done.1.refs_0_.refs_1_
  11.6 0.1 collective-permute-done.2.refs_1_.refs_2_
  11.7 0.3 %collective-permute-done.3.refs_2_.refs_3_ = f32[32,256]{1,0:T(8,128)S(1)} collective-permute-done((f32[32,256]{1,0:T(8,128)S(1)}, f32[32,256]{1,0:T(8,128)S(1)}, u32[]{:S(2)}, u32[]{:S(2)}) %collective-permute-start.3) | collective-permute-done | bytes 32800 | tf_op jit(solution)/shard_map/ppermute | solution.py:327
  12.0 0.3 %collective-permute-start.5 = (f32[48,256]{1,0:T(8,128)S(1)}, f32[48,256]{1,0:T(8,128)S(1)}, u32[]{:S(2)}, u32[]{:S(2)}) collective-permute-start(f32[48,256]{1,0:T(8,128)S(1)} %shard_map.78.give), channel_id=1, source_target_pairs={{0,2},{1,3},{2,0},{3,1},{4,6},{5,7},{6,4},{7,5},{8,10},{9,11},{10,... | collective-permute-start | bytes 147464 | tf_op jit(solution)/shard_map/ppermute | solution.py:327
  12.2 0.6 %shard_map.79 = (bf16[128,256]{1,0:T(8,128)(2,1)S(1)}, bf16[128,256]{1,0:T(8,128)(2,1)S(1)}, bf16[64,256]{1,0:T(8,128)(2,1)S(1)}, bf16[64,256]{1,0:T(8,128)(2,1)S(1)}) custom-call(f32[20,128,128]{2,1,0:T(8,128)S(1)} %bitcast.9, s32[1,2]{1,0:T(1,128)S(1)} %bitcast.15, f32[48,256]{1,0:T(8,128)S(1)} %shard_map.78.give, ...), custom_call_target="tpu_custom_call" | custom-call | flops 4294967296 | bytes 131072 | tf_op jit(solution)/shard_map/pallas_call | solution.py:308
  12.9 0.2 %collective-permute-done.4.refs_0_ = f32[16,256]{1,0:T(8,128)S(1)} collective-permute-done((f32[16,256]{1,0:T(8,128)S(1)}, f32[16,256]{1,0:T(8,128)S(1)}, u32[]{:S(2)}, u32[]{:S(2)}) %collective-permute-start.4) | collective-permute-done | bytes 16416 | tf_op jit(solution)/shard_map/ppermute | solution.py:327
  13.1 0.1 collective-permute-done.5.refs_1_
  13.2 1.2 %shard_map.80 = f32[2,128,128]{2,1,0:T(8,128)} custom-call(bf16[64,256]{1,0:T(8,128)(2,1)S(1)} %get-tuple-element.28.high, bf16[64,256]{1,0:T(8,128)(2,1)S(1)} %get-tuple-element.29.low, f32[16,256]{1,0:T(8,128)S(1)} %collective-permute-done.4.refs_0_, f32[48,256]{1,0:T(8,128)S(1)} %collective-permute-done.5.refs_1_, ...), custom_call_target="tpu_custom_call" | custom-call | tf_op jit(solution)/shard_map/pallas_call | solution.py:380
  (3 shorter events, 0.0 us)
Async XLA Ops:
  0.0 0.9 %copy-start.1 = (f32[2,1,1,1,16384]{4,3,2,1,0:T(1,128)S(1)}, f32[2,1,1,1,16384]{4,3,2,1,0:T(1,128)}, u32[]{:S(2)}) copy-start(f32[2,1,1,1,16384]{4,3,2,1,0:T(1,128)} %param.7) | copy-start | bytes 393220
  0.0 1.4 %copy-start = (f32[10,2,128,128]{3,2,1,0:T(8,128)S(1)}, f32[10,2,128,128]{3,2,1,0:T(8,128)}, u32[]{:S(2)}) copy-start(f32[10,2,128,128]{3,2,1,0:T(8,128)} %param.8) | copy-start | bytes 3932164
  0.0 1.4 %copy-start.5 = (s32[2]{0:T(128)S(1)}, s32[2]{0:T(128)}, u32[]{:S(2)}) copy-start(s32[2]{0:T(128)} %param.12) | copy-start | bytes 28
  0.0 1.4 %copy-start.3 = (f32[128]{0:T(128)S(1)}, f32[128]{0:T(128)}, u32[]{:S(2)}) copy-start(f32[128]{0:T(128)} %param.10) | copy-start | bytes 1540
  0.0 1.4 %copy-start.4 = (s32[4]{0:T(128)S(1)}, s32[4]{0:T(128)}, u32[]{:S(2)}) copy-start(s32[4]{0:T(128)} %param.13) | copy-start | bytes 52
  0.8 10.1 %copy-start.2 = (f32[128]{0:T(128)S(1)}, f32[128]{0:T(128)}, u32[]{:S(2)}) copy-start(f32[128]{0:T(128)} %param.9) | copy-start | bytes 1540
  0.9 1.5 %collective-permute-start = (f32[128,256]{1,0:T(8,128)S(1)}, f32[128,256]{1,0:T(8,128)S(1)}, u32[]{:S(2)}, u32[]{:S(2)}) collective-permute-start(f32[128,256]{1,0:T(8,128)S(1)} %shard_map.74.state), channel_id=1, source_target_pairs={{0,2},{1,3},{2,0},{3,1},{4,6},{5,7},{6,4},{7,5},{8,10},{9,11},{10,... | collective-permute-start | bytes 393224 | tf_op jit(solution)/shard_map/ppermute | solution.py:327
  2.7 8.9 %collective-permute-start.1 = (f32[32,256]{1,0:T(8,128)S(1)}, f32[32,256]{1,0:T(8,128)S(1)}, u32[]{:S(2)}, u32[]{:S(2)}) collective-permute-start(f32[32,256]{1,0:T(8,128)S(1)} %get-tuple-element.22), channel_id=1, source_target_pairs={{0,16},{1,17},{2,19},{3,18},{4,20},{5,21},{6,23},{7,22},{8,24},{9,... | collective-permute-start | bytes 98312 | tf_op jit(solution)/shard_map/ppermute | solution.py:327
  6.7 5.0 %collective-permute-start.2 = (f32[32,256]{1,0:T(8,128)S(1)}, f32[32,256]{1,0:T(8,128)S(1)}, u32[]{:S(2)}, u32[]{:S(2)}) collective-permute-start(f32[32,256]{1,0:T(8,128)S(1)} %get-tuple-element.23), channel_id=1, source_target_pairs={{0,24},{1,25},{2,27},{3,26},{4,28},{5,29},{6,31},{7,30},{8,16},{9,... | collective-permute-start | bytes 98312 | tf_op jit(solution)/shard_map/ppermute | solution.py:327
  7.7 4.2 %collective-permute-start.3 = (f32[32,256]{1,0:T(8,128)S(1)}, f32[32,256]{1,0:T(8,128)S(1)}, u32[]{:S(2)}, u32[]{:S(2)}) collective-permute-start(f32[32,256]{1,0:T(8,128)S(1)} %get-tuple-element.24), channel_id=1, source_target_pairs={{0,8},{1,9},{2,3},{3,2},{4,12},{5,13},{6,7},{7,6},{8,0},{9,1},{10,... | collective-permute-start | bytes 98312 | tf_op jit(solution)/shard_map/ppermute | solution.py:327
  8.2 4.8 %collective-permute-start.4 = (f32[16,256]{1,0:T(8,128)S(1)}, f32[16,256]{1,0:T(8,128)S(1)}, u32[]{:S(2)}, u32[]{:S(2)}) collective-permute-start(f32[16,256]{1,0:T(8,128)S(1)} %get-tuple-element.30), channel_id=1, source_target_pairs={{0,9},{1,8},{2,11},{3,10},{4,13},{5,12},{6,15},{7,14},{8,1},{9,0},... | collective-permute-start | bytes 49160 | tf_op jit(solution)/shard_map/ppermute | solution.py:327
  12.0 1.2 %collective-permute-start.5 = (f32[48,256]{1,0:T(8,128)S(1)}, f32[48,256]{1,0:T(8,128)S(1)}, u32[]{:S(2)}, u32[]{:S(2)}) collective-permute-start(f32[48,256]{1,0:T(8,128)S(1)} %shard_map.78.give), channel_id=1, source_target_pairs={{0,2},{1,3},{2,0},{3,1},{4,6},{5,7},{6,4},{7,5},{8,10},{9,11},{10,... | collective-permute-start | bytes 147464 | tf_op jit(solution)/shard_map/ppermute | solution.py:327
